TPU v7x, 32 devices: a whole 2x2x4 slice. The times are simulated.
32 devices in a mesh: dp: 4 (over z), seq: 4 (over x, core), blk: 2 (over y).
Axes of the slice: x: 2, y: 2, z: 4, core: 2. Of those that a mesh axis runs over, the one named last changes fastest.
Arguments:
- tokens: bfloat16 [4096, 1024], P(('dp', 'seq', 'blk')), may hold values from -6 to 6
- first_gain: bfloat16 [1024], P(('dp', 'seq', 'blk')), may hold values from 0.099609375 to 1.8984375
- first_shift: bfloat16 [1024], P(('dp', 'seq', 'blk')), may hold values from -3 to 3
- joint_weight: bfloat16 [1024, 3072], P(('dp', 'blk'), 'seq'), may hold values from -0.1875 to 0.1875
- joint_bias: bfloat16 [16, 128], P('seq', ('dp', 'blk')), may hold values from -3 to 3
- output_weight: bfloat16 [1024, 1024], P('seq', ('dp', 'blk')), may hold values from -0.75 to 0.75
- output_bias: bfloat16 [1024], P(('dp', 'seq', 'blk')), may hold values from -3 to 3
- second_gain: bfloat16 [1024], P(('dp', 'seq', 'blk')), may hold values from 0.099609375 to 1.8984375
- second_shift: bfloat16 [1024], P(('dp', 'seq', 'blk')), may hold values from -3 to 3
- expand_weight: bfloat16 [1024, 4096], P(('dp', 'blk'), 'seq'), may hold values from -0.1875 to 0.1875
- expand_bias: bfloat16 [4, 1024], P('seq', ('dp', 'blk')), may hold values from -3 to 3
- reduce_weight: bfloat16 [4096, 1024], P('seq', ('dp', 'blk')), may hold values from -0.1875 to 0.1875
- reduce_bias: bfloat16 [1024], P(('dp', 'seq', 'blk')), may hold values from -3 to 3
- cotangent: bfloat16 [4096, 1024], P(('dp', 'seq', 'blk')), may hold values from -6 to 6
Outputs:
- layer_output: bfloat16 [4096, 1024], P(('dp', 'seq', 'blk'))
- input_grad: bfloat16 [4096, 1024], P(('dp', 'seq', 'blk'))
- first_gain_grad: float32 [1024], P(('dp', 'seq', 'blk'))
- first_shift_grad: float32 [1024], P(('dp', 'seq', 'blk'))
- joint_weight_grad: float32 [1024, 3072], P(('dp', 'blk'), 'seq')
- joint_bias_grad: float32 [16, 128], P('seq', ('dp', 'blk'))
- output_weight_grad: float32 [1024, 1024], P('seq', ('dp', 'blk'))
- output_bias_grad: float32 [1024], P(('dp', 'seq', 'blk'))
- second_gain_grad: float32 [1024], P(('dp', 'seq', 'blk'))
- second_shift_grad: float32 [1024], P(('dp', 'seq', 'blk'))
- expand_weight_grad: float32 [1024, 4096], P(('dp', 'blk'), 'seq')
- expand_bias_grad: float32 [4, 1024], P('seq', ('dp', 'blk'))
- reduce_weight_grad: float32 [4096, 1024], P('seq', ('dp', 'blk'))
- reduce_bias_grad: float32 [1024], P(('dp', 'seq', 'blk'))
All inputs are finite; a program needn't handle non-finite values.
Results may differ from a plain program's by a relative error of at most 0.02.
Values may be sent and summed in bfloat16 or wider, within the bound.
No kernel may reach another device: no remote copies, remote signals or barrier semaphores. Data moves between devices by JAX's collectives and lax.ppermute only.
A program may use at most 128 MiB of HBM per device.

v0:
```python
import jax
import jax.numpy as jnp
from jax import lax
from jax.sharding import PartitionSpec as P

H = 16
HD = 64


epsilon = 1e-05


def layer_norm(values, gain_row, shift_row):
    average = jnp.mean(values, -1, keepdims=True)
    centred = values - average
    variance = jnp.mean(centred * centred, -1, keepdims=True)
    return centred * lax.rsqrt(variance + epsilon) * gain_row + shift_row


def local_bias(pair_local, head_local):
    paired = pair_local.reshape(head_local, 2, HD)
    return jnp.stack([paired[:, 0], jnp.zeros_like(paired[:, 0]), paired[:, 1]], axis=1).reshape(
        head_local * 3 * HD
    )


def gelu_tanh(values):
    return jax.nn.gelu(values, approximate=True)


def score_tile(query_block, key_tile, places, tile_start, slopes, scale_factor):
    tile_rows = key_tile.shape[0]
    key_places = tile_start + jnp.arange(tile_rows, dtype=jnp.int32)
    scores = (
        jnp.einsum("qhd,khd->hqk", query_block, key_tile, preferred_element_type=jnp.float32)
        * scale_factor
    )
    offsets = (key_places[None, :] - places[:, None]).astype(jnp.float32)
    scores = scores + slopes[:, None, None] * offsets[None]
    allowed = (key_places[None, :] <= places[:, None])[None]
    return (jnp.where(allowed, scores, -1e30), allowed)


def attend_forward(queries, all_keys, all_values, places, slopes):
    row_count, head_local, head_width = queries.shape
    block_rows = min(512, row_count)
    tile_rows = min(512, all_keys.shape[0])
    scale_factor = head_width ** (-0.5)
    query_blocks = queries.reshape(row_count // block_rows, block_rows, head_local, head_width)
    place_blocks = places.reshape(row_count // block_rows, block_rows)

    def one_block(block_pair):
        query_block, block_places = block_pair
        needed = (block_places[-1] + tile_rows) // tile_rows

        def one_tile(counter, state_carry):
            running_max, running_sum, running_total = state_carry
            tile_start = counter * tile_rows
            key_tile = lax.dynamic_slice_in_dim(all_keys, tile_start, tile_rows, 0)
            value_tile = lax.dynamic_slice_in_dim(all_values, tile_start, tile_rows, 0)
            scores, allowed = score_tile(
                query_block, key_tile, block_places, tile_start, slopes, scale_factor
            )
            new_max = jnp.maximum(running_max, jnp.max(scores, -1))
            weights_tile = jnp.where(allowed, jnp.exp(scores - new_max[..., None]), 0.0)
            factor = jnp.exp(running_max - new_max)
            running_sum = running_sum * factor + jnp.sum(weights_tile, -1)
            running_total = running_total * factor[..., None] + jnp.einsum(
                "hqk,khd->hqd",
                weights_tile.astype(jnp.bfloat16),
                value_tile,
                preferred_element_type=jnp.float32,
            )
            return (new_max, running_sum, running_total)

        start_state = (
            jnp.full((head_local, block_rows), -1e30, jnp.float32),
            jnp.zeros((head_local, block_rows), jnp.float32),
            jnp.zeros((head_local, block_rows, head_width), jnp.float32),
        )
        running_max, running_sum, running_total = lax.fori_loop(0, needed, one_tile, start_state)
        return (running_total / running_sum[..., None], running_max + jnp.log(running_sum))

    outputs, log_sums = lax.map(one_block, (query_blocks, place_blocks))
    outputs = jnp.transpose(outputs, (0, 2, 1, 3)).reshape(row_count, head_local, head_width)
    return (outputs, log_sums)


def attend_backward(queries, all_keys, all_values, places, slopes, grad_out, log_sums, deltas):
    row_count, head_local, head_width = queries.shape
    key_count = all_keys.shape[0]
    block_rows = min(512, row_count)
    tile_rows = min(512, key_count)
    scale_factor = head_width ** (-0.5)
    block_count = row_count // block_rows
    query_blocks = queries.reshape(block_count, block_rows, head_local, head_width)
    grad_blocks = grad_out.reshape(block_count, block_rows, head_local, head_width)
    place_blocks = places.reshape(block_count, block_rows)
    delta_blocks = jnp.transpose(deltas.reshape(block_count, block_rows, head_local), (0, 2, 1))

    def one_block(key_grads, block_inputs):
        query_block, grad_block, block_places, block_lse, block_delta = block_inputs
        needed = (block_places[-1] + tile_rows) // tile_rows

        def one_tile(counter, inner_carry):
            query_grad, key_sums = inner_carry
            tile_start = counter * tile_rows
            key_tile = lax.dynamic_slice_in_dim(all_keys, tile_start, tile_rows, 0)
            value_tile = lax.dynamic_slice_in_dim(all_values, tile_start, tile_rows, 0)
            scores, allowed = score_tile(
                query_block, key_tile, block_places, tile_start, slopes, scale_factor
            )
            probs = jnp.where(allowed, jnp.exp(scores - block_lse[..., None]), 0.0)
            value_grad = jnp.einsum(
                "hqk,qhd->khd",
                probs.astype(jnp.bfloat16),
                grad_block,
                preferred_element_type=jnp.float32,
            )
            prob_grad = jnp.einsum(
                "qhd,khd->hqk", grad_block, value_tile, preferred_element_type=jnp.float32
            )
            score_grad = (probs * (prob_grad - block_delta[..., None])).astype(jnp.bfloat16)
            query_grad = (
                query_grad
                + jnp.einsum(
                    "hqk,khd->qhd", score_grad, key_tile, preferred_element_type=jnp.float32
                )
                * scale_factor
            )
            key_grad = (
                jnp.einsum(
                    "hqk,qhd->khd", score_grad, query_block, preferred_element_type=jnp.float32
                )
                * scale_factor
            )
            current = lax.dynamic_slice_in_dim(key_sums, tile_start, tile_rows, 0)
            update = current + jnp.concatenate([key_grad, value_grad], -1)
            key_sums = lax.dynamic_update_slice_in_dim(key_sums, update, tile_start, 0)
            return (query_grad, key_sums)

        start_grad = jnp.zeros((block_rows, head_local, head_width), jnp.float32)
        query_grad, key_grads = lax.fori_loop(0, needed, one_tile, (start_grad, key_grads))
        return (key_grads, query_grad)

    start_keys = jnp.zeros((key_count, head_local, 2 * head_width), jnp.float32)
    key_grads, query_grads = lax.scan(
        one_block, start_keys, (query_blocks, grad_blocks, place_blocks, log_sums, delta_blocks)
    )
    return (query_grads.reshape(row_count, head_local, head_width), key_grads)


def local(
    tokens,
    first_gain,
    first_shift,
    joint_weight,
    joint_bias,
    output_weight,
    output_bias,
    second_gain,
    second_shift,
    expand_weight,
    expand_bias,
    reduce_weight,
    reduce_bias,
    cotangent,
):
    seq_count = lax.axis_size("seq")
    blk_count = lax.axis_size("blk")
    head_local = H // seq_count
    tok_rows = tokens.shape[0]
    inputs = tokens.astype(jnp.float32)
    small_full = (
        lax.all_gather(first_gain, ("dp", "seq", "blk"), axis=0, tiled=True),
        lax.all_gather(first_shift, ("dp", "seq", "blk"), axis=0, tiled=True),
        lax.all_gather(output_bias, ("dp", "seq", "blk"), axis=0, tiled=True),
        lax.all_gather(second_gain, ("dp", "seq", "blk"), axis=0, tiled=True),
        lax.all_gather(second_shift, ("dp", "seq", "blk"), axis=0, tiled=True),
        lax.all_gather(reduce_bias, ("dp", "seq", "blk"), axis=0, tiled=True),
    )
    gain_one, shift_one, out_shift, gain_two, shift_two, reduce_shift = [
        piece.astype(jnp.float32) for piece in small_full
    ]
    joint_local, pair_local, out_local = (
        lax.all_gather(joint_weight, ("dp", "blk"), axis=0, tiled=True),
        lax.all_gather(joint_bias, ("dp", "blk"), axis=1, tiled=True),
        lax.all_gather(output_weight, ("dp", "blk"), axis=1, tiled=True),
    )
    expand_local, expand_shift, reduce_local = (
        lax.all_gather(expand_weight, ("dp", "blk"), axis=0, tiled=True),
        lax.all_gather(expand_bias, ("dp", "blk"), axis=1, tiled=True),
        lax.all_gather(reduce_weight, ("dp", "blk"), axis=1, tiled=True),
    )
    outgoing = layer_norm(inputs, gain_one, shift_one).astype(jnp.bfloat16)
    arrived = lax.all_gather(outgoing, "seq", axis=0, tiled=True)
    row_count = arrived.shape[0]
    mixed_cols = jnp.dot(arrived, joint_local, preferred_element_type=jnp.float32)
    mixed_cols = mixed_cols + local_bias(pair_local.astype(jnp.float32), head_local)
    by_head = mixed_cols.astype(jnp.bfloat16).reshape(row_count, head_local, 3 * HD)
    queries = by_head[:, :, :HD]
    key_value = by_head[:, :, HD:].reshape(seq_count, tok_rows, head_local, 2 * HD)
    ordered = lax.all_gather(key_value, "blk", axis=1, tiled=True)
    ordered = ordered.reshape(seq_count * blk_count * tok_rows, head_local, 2 * HD)
    all_keys = ordered[:, :, :HD]
    all_values = ordered[:, :, HD:]
    places = (
        (jnp.arange(seq_count, dtype=jnp.int32)[:, None] * blk_count + lax.axis_index("blk"))
        * tok_rows
        + jnp.arange(tok_rows, dtype=jnp.int32)[None, :]
    ).reshape(row_count)
    head_ids = lax.axis_index("seq") * head_local + jnp.arange(head_local, dtype=jnp.int32)
    slopes = jnp.exp2(-8.0 * (head_ids + 1).astype(jnp.float32) / H)
    attended, log_sums = attend_forward(queries, all_keys, all_values, places, slopes)
    attended_low = attended.reshape(row_count, head_local * HD).astype(jnp.bfloat16)
    branch_part = jnp.dot(attended_low, out_local, preferred_element_type=jnp.float32)
    branch_sum = lax.psum_scatter(
        branch_part.astype(jnp.bfloat16), "seq", scatter_dimension=0, tiled=True
    ).astype(jnp.float32)
    middle = inputs + (branch_sum + out_shift)
    normed_two = layer_norm(middle, gain_two, shift_two).astype(jnp.bfloat16)
    normed_two_group, cot_group = (
        lax.all_gather(normed_two, "seq", axis=0, tiled=True),
        lax.all_gather(cotangent, "seq", axis=0, tiled=True),
    )
    hidden = jnp.dot(normed_two_group, expand_local, preferred_element_type=jnp.float32)
    hidden = hidden + expand_shift.astype(jnp.float32).reshape(-1)
    activated, gelu_pull = jax.vjp(gelu_tanh, hidden)
    activated_low = activated.astype(jnp.bfloat16)
    result_part = jnp.dot(activated_low, reduce_local, preferred_element_type=jnp.float32)
    result_sum = lax.psum_scatter(
        result_part.astype(jnp.bfloat16), "seq", scatter_dimension=0, tiled=True
    ).astype(jnp.float32)
    layer_output = (middle + (result_sum + reduce_shift)).astype(jnp.bfloat16)
    upstream = cotangent.astype(jnp.float32)
    reduce_grad = jnp.einsum(
        "tf,td->fd", activated_low, cot_group, preferred_element_type=jnp.float32
    )
    reduce_shift_grad = jnp.sum(upstream, 0)
    activated_grad = jnp.einsum(
        "td,fd->tf", cot_group, reduce_local, preferred_element_type=jnp.float32
    )
    hidden_grad = gelu_pull(activated_grad)[0].astype(jnp.bfloat16)
    expand_grad = jnp.einsum(
        "tc,tf->cf", normed_two_group, hidden_grad, preferred_element_type=jnp.float32
    )
    expand_shift_grad = jnp.sum(hidden_grad.astype(jnp.float32), 0).reshape(
        expand_shift.shape[0], -1
    )
    normed_two_part = jnp.einsum(
        "tf,cf->tc", hidden_grad, expand_local, preferred_element_type=jnp.float32
    )
    normed_two_grad = lax.psum_scatter(
        normed_two_part.astype(jnp.bfloat16), "seq", scatter_dimension=0, tiled=True
    ).astype(jnp.float32)
    unused_value, norm_two_pull = jax.vjp(layer_norm, middle, gain_two, shift_two)
    middle_norm_grad, gain_two_grad, shift_two_grad = norm_two_pull(normed_two_grad)
    middle_grad = upstream + middle_norm_grad
    branch_grad = middle_grad.astype(jnp.bfloat16)
    out_shift_grad = jnp.sum(branch_grad.astype(jnp.float32), 0)
    branch_group = lax.all_gather(branch_grad, "seq", axis=0, tiled=True)
    out_grad = jnp.einsum(
        "tc,td->cd", attended_low, branch_group, preferred_element_type=jnp.float32
    )
    attended_grad = jnp.einsum(
        "td,cd->tc", branch_group, out_local, preferred_element_type=jnp.float32
    ).astype(jnp.bfloat16)
    grad_heads = attended_grad.reshape(row_count, head_local, HD)
    deltas = jnp.sum(grad_heads.astype(jnp.float32) * attended, -1)
    query_grads, key_grads = attend_backward(
        queries, all_keys, all_values, places, slopes, grad_heads, log_sums, deltas
    )
    key_terms = key_grads.reshape(seq_count, blk_count * tok_rows, head_local * 2 * HD)
    key_sums = lax.psum_scatter(
        key_terms.astype(jnp.bfloat16), "blk", scatter_dimension=1, tiled=True
    ).astype(jnp.float32)
    combined = jnp.concatenate(
        [
            query_grads.astype(jnp.bfloat16),
            key_sums.reshape(row_count, head_local, 2 * HD).astype(jnp.bfloat16),
        ],
        -1,
    )
    mixed_grad = combined.reshape(row_count, head_local * 3 * HD)
    joint_grad = jnp.einsum("tc,tk->ck", arrived, mixed_grad, preferred_element_type=jnp.float32)
    bias_sums = jnp.sum(mixed_grad.astype(jnp.float32), 0).reshape(head_local, 3, HD)
    pair_grad = jnp.concatenate([bias_sums[:, 0], bias_sums[:, 2]], -1)
    normed_one_part = jnp.einsum(
        "tk,ck->tc", mixed_grad, joint_local, preferred_element_type=jnp.float32
    )
    normed_one_grad = lax.psum_scatter(
        normed_one_part.astype(jnp.bfloat16), "seq", scatter_dimension=0, tiled=True
    ).astype(jnp.float32)
    unused_first, norm_one_pull = jax.vjp(layer_norm, inputs, gain_one, shift_one)
    input_norm_grad, gain_one_grad, shift_one_grad = norm_one_pull(normed_one_grad)
    input_grad = (middle_grad + input_norm_grad).astype(jnp.bfloat16)
    weight_sums = (
        lax.psum_scatter(
            joint_grad.astype(jnp.bfloat16), ("dp", "blk"), scatter_dimension=0, tiled=True
        ).astype(jnp.float32),
        lax.psum_scatter(
            pair_grad.astype(jnp.bfloat16), ("dp", "blk"), scatter_dimension=1, tiled=True
        ).astype(jnp.float32),
        lax.psum_scatter(
            out_grad.astype(jnp.bfloat16), ("dp", "blk"), scatter_dimension=1, tiled=True
        ).astype(jnp.float32),
        lax.psum_scatter(
            expand_grad.astype(jnp.bfloat16), ("dp", "blk"), scatter_dimension=0, tiled=True
        ).astype(jnp.float32),
        lax.psum_scatter(
            expand_shift_grad.astype(jnp.bfloat16), ("dp", "blk"), scatter_dimension=1, tiled=True
        ).astype(jnp.float32),
        lax.psum_scatter(
            reduce_grad.astype(jnp.bfloat16), ("dp", "blk"), scatter_dimension=1, tiled=True
        ).astype(jnp.float32),
    )
    small_sums = (
        lax.psum_scatter(gain_one_grad, ("dp", "seq", "blk"), scatter_dimension=0, tiled=True),
        lax.psum_scatter(shift_one_grad, ("dp", "seq", "blk"), scatter_dimension=0, tiled=True),
        lax.psum_scatter(out_shift_grad, ("dp", "seq", "blk"), scatter_dimension=0, tiled=True),
        lax.psum_scatter(gain_two_grad, ("dp", "seq", "blk"), scatter_dimension=0, tiled=True),
        lax.psum_scatter(shift_two_grad, ("dp", "seq", "blk"), scatter_dimension=0, tiled=True),
        lax.psum_scatter(reduce_shift_grad, ("dp", "seq", "blk"), scatter_dimension=0, tiled=True),
    )
    return (
        layer_output,
        input_grad,
        small_sums[0],
        small_sums[1],
        weight_sums[0],
        weight_sums[1],
        weight_sums[2],
        small_sums[2],
        small_sums[3],
        small_sums[4],
        weight_sums[3],
        weight_sums[4],
        weight_sums[5],
        small_sums[5],
    )


def solution(mesh):
    return jax.shard_map(
        local,
        mesh=mesh,
        in_specs=(
            P(("dp", "seq", "blk"), None),
            P(("dp", "seq", "blk")),
            P(("dp", "seq", "blk")),
            P(("dp", "blk"), "seq"),
            P("seq", ("dp", "blk")),
            P("seq", ("dp", "blk")),
            P(("dp", "seq", "blk")),
            P(("dp", "seq", "blk")),
            P(("dp", "seq", "blk")),
            P(("dp", "blk"), "seq"),
            P("seq", ("dp", "blk")),
            P("seq", ("dp", "blk")),
            P(("dp", "seq", "blk")),
            P(("dp", "seq", "blk"), None),
        ),
        out_specs=(
            P(("dp", "seq", "blk"), None),
            P(("dp", "seq", "blk"), None),
            P(("dp", "seq", "blk")),
            P(("dp", "seq", "blk")),
            P(("dp", "blk"), "seq"),
            P("seq", ("dp", "blk")),
            P("seq", ("dp", "blk")),
            P(("dp", "seq", "blk")),
            P(("dp", "seq", "blk")),
            P(("dp", "seq", "blk")),
            P(("dp", "blk"), "seq"),
            P("seq", ("dp", "blk")),
            P("seq", ("dp", "blk")),
            P(("dp", "seq", "blk")),
        ),
        check_vma=False,
    )
```

profile of v0, /device:TPU:0, one launch (start us, length us, event | category | flops | bytes accessed | tf_op | source)
XLA Modules:
  0.0 972.9 jit_solution(2049299633563035208)
XLA Ops:
  14.6 42.2 %all-reduce.13 = (bf16[1024]{0:T(1024)(128)(2,1)S(1)}, bf16[1024]{0:T(1024)(128)(2,1)S(1)}, bf16[1024]{0:T(1024)(128)(2,1)S(1)}, bf16[1024]{0:T(1024)(128)(2,1)S...) all-reduce(bf16[1024]{0:T(1024)(128)(2,1)S(1)} %dynamic-update-slic, ...), channel_id=1, replica_groups=mesh['dp'=4,'seq'=4,'blk'=2] {'dp','seq','blk'}, use_global_device_ids=true, to_apply=%add.4 | all-reduce | flops 6144 | bytes 24576
  59.5 20.5 %all-gather = bf16[8,16,4]{1,2,0:T(4,128)(2,1)S(1)} all-gather(bf16[1,16,4]{1,2,0:T(4,128)(2,1)} %bitcast.186), channel_id=1, replica_groups=mesh['dp'=4,'seq'=4,'blk'=2] {'dp','blk'}, dimensions={0}, use_global_device_ids=true | all-gather | bytes 1152 | tf_op jit(solution)/shard_map/all_gather | solution.py:187
  80.4 41.4 %all-gather.12.cloned.1.call-done = bf16[1024,768]{1,0:T(8,128)(2,1)} async-done(((bf16[128,768]{1,0:T(8,128)(2,1)}), bf16[1024,768]{1,0:T(8,128)(2,1)}) %all-gather.12.cloned.1.call-update) | async-done | bytes 1572880 | tf_op jit(solution)/shard_map/all_gather | solution.py:186
  127.2 28.0 %all_gather.57 = bf16[256,1024]{1,0:T(8,128)(2,1)S(1)} all-gather(bf16[256,128]{1,0:T(8,128)(2,1)S(1)} %copy-done.14), channel_id=1, replica_groups=mesh['dp'=4,'seq'=4,'blk'=2] {'dp','blk'}, dimensions={1}, use_global_device_ids=true | all-gather | bytes 589824 | tf_op jit(solution)/shard_map/all_gather | solution.py:188
  157.2 10.0 %while.47 = (s32[]{:T(128)}, f32[4,512]{1,0:T(4,128)S(1)}, f32[4,512]{1,0:T(4,128)S(1)}, f32[4,512,64]{1,2,0:T(8,128)S(1)}, s32[]{:T(128)}, /*index=5*/bf16[1024...) while((s32[]{:T(128)}, f32[4,512]{1,0:T(4,128)S(1)}, ...), condition=%wide.region_5.6_spmd.clone, body=%wide.region_2.5_spmd.clone.sunk | while | flops 289412096 | bytes 19805428 | solution.py:81
  169.5 23.1 %reduce-scatter.22.cloned.1.call-done = bf16[128,1024]{1,0:T(8,128)(2,1)} async-done(((bf16[512,1024]{1,0:T(8,128)(2,1)}), bf16[128,1024]{1,0:T(8,128)(2,1)}) %reduce-scatter.22.cloned.1.call-update) | async-done | bytes 262160 | tf_op jit(solution)/shard_map/reduce_scatter | solution.py:217
  198.4 20.6 %all_gather.63 = bf16[1,1024]{1,0:T(2,128)(2,1)S(1)} all-gather(bf16[1,128]{1,0:T(2,128)(2,1)S(1)} %copy-done.21), channel_id=1, replica_groups=mesh['dp'=4,'seq'=4,'blk'=2] {'dp','blk'}, dimensions={1}, use_global_device_ids=true | all-gather | bytes 2304 | tf_op jit(solution)/shard_map/all_gather | solution.py:192
  219.0 25.2 %all-gather.18.cloned.1.call-done = bf16[1024,1024]{1,0:T(8,128)(2,1)} async-done(((bf16[128,1024]{1,0:T(8,128)(2,1)}), bf16[1024,1024]{1,0:T(8,128)(2,1)}) %all-gather.18.cloned.1.call-update) | async-done | bytes 2097168 | tf_op jit(solution)/shard_map/all_gather | solution.py:191
  244.2 17.3 %all-gather.16.cloned.1.call-done = bf16[512,1024]{1,0:T(8,128)(2,1)} async-done(((bf16[128,1024]{1,0:T(8,128)(2,1)}), bf16[512,1024]{1,0:T(8,128)(2,1)}) %all-gather.16.cloned.1.call-update) | async-done | bytes 1048592 | tf_op jit(solution)/shard_map/all_gather | solution.py:223
  261.5 4.5 fusion.87
  266.0 13.9 %all-gather.22.cloned.1.call-done = bf16[512,1024]{1,0:T(8,128)(2,1)} async-done(((bf16[128,1024]{1,0:T(8,128)(2,1)}), bf16[512,1024]{1,0:T(8,128)(2,1)}) %all-gather.22.cloned.1.call-update) | async-done | bytes 1048592 | tf_op jit(solution)/shard_map/all_gather | solution.py:224
  279.9 53.4 %all-gather.20.cloned.1.call-done = bf16[1024,1024]{1,0:T(8,128)(2,1)} async-done(((bf16[1024,128]{1,0:T(8,128)(2,1)}), bf16[1024,1024]{1,0:T(8,128)(2,1)}) %all-gather.20.cloned.1.call-update) | async-done | bytes 2097168 | tf_op jit(solution)/shard_map/all_gather | solution.py:193
  333.3 5.2 fusion.80
  341.8 4.8 convolution_convert_fusion.5
  346.7 18.3 %reduce-scatter.26.cloned.1.call-done = bf16[128,1024]{1,0:T(8,128)(2,1)} async-done(((bf16[512,1024]{1,0:T(8,128)(2,1)}), bf16[128,1024]{1,0:T(8,128)(2,1)}) %reduce-scatter.26.cloned.1.call-update) | async-done | bytes 262160 | tf_op jit(solution)/shard_map/reduce_scatter | solution.py:253
  366.2 26.0 %reduce-scatter.24.cloned.1.call-done = bf16[128,1024]{1,0:T(8,128)(2,1)} async-done(((bf16[512,1024]{1,0:T(8,128)(2,1)}), bf16[128,1024]{1,0:T(8,128)(2,1)}) %reduce-scatter.24.cloned.1.call-update) | async-done | bytes 262160 | tf_op jit(solution)/shard_map/reduce_scatter | solution.py:231
  396.0 16.8 %all-gather.24.cloned.1.call-done = bf16[512,1024]{1,0:T(8,128)(2,1)} async-done(((bf16[128,1024]{1,0:T(8,128)(2,1)}), bf16[512,1024]{1,0:T(8,128)(2,1)}) %all-gather.24.cloned.1.call-update) | async-done | bytes 1048592 | tf_op jit(solution)/shard_map/all_gather | solution.py:261
  415.5 15.7 %while.48 = (s32[]{:T(128)}, f32[512,4,64]{0,2,1:T(8,128)S(1)}, f32[1024,4,128]{0,2,1:T(8,128)S(1)}, s32[]{:T(128)}, bf16[1024,4,64]{0,2,1:T(8,128)(2,1)}, /*ind...) while((s32[]{:T(128)}, f32[512,4,64]{0,2,1:T(8,128)S(1)}, ...), condition=%wide.region_15.16_spmd.clone, body=%wide.region_14.15_spmd.clone.sunk | while | flops 689570816 | bytes 35165024 | solution.py:143
  434.3 23.3 %copy.69 = bf16[4,256,512]{0,2,1:T(8,128)(2,1)} copy(bf16[4,256,512]{1,0,2:T(4,128)(2,1)S(1)} %convert_element_type.205) | data formatting | bytes 2097152
  457.5 65.2 %reshape.312 = bf16[256,2048]{1,0:T(8,128)(2,1)} reshape(bf16[256,512,4]{2,1,0:T(8,128)(2,1)} %bitcast.165) | data formatting | bytes 2097152
  523.8 3.5 convolution_convert_fusion
  536.8 6.4 reduce-scatter.34.cloned.1.call-done
  543.2 37.9 %reshape.313 = bf16[128,512,4]{2,1,0:T(8,128)(2,1)} reshape(bf16[128,2048]{1,0:T(8,128)(2,1)} %reduce-scatter.34.cloned.1.call-done) | data formatting | bytes 1048576
  581.1 15.6 %copy.70 = bf16[4,128,512]{1,0,2:T(4,128)(2,1)S(1)} copy(bf16[4,128,512]{0,2,1:T(8,128)(2,1)} %bitcast.166) | data formatting | bytes 1048576
  604.0 4.4 reduce-scatter.40.cloned.1.call-done
  609.7 68.8 %reduce-scatter.42.cloned.1.call-done = bf16[128,1024]{1,0:T(8,128)(2,1)} async-done(((bf16[1024,1024]{1,0:T(8,128)(2,1)}), bf16[128,1024]{1,0:T(8,128)(2,1)}) %reduce-scatter.42.cloned.1.call-update) | async-done | bytes 262160
  680.5 68.0 %reduce-scatter.32.cloned.1.call-done = bf16[128,1024]{1,0:T(8,128)(2,1)} async-done(((bf16[1024,1024]{1,0:T(8,128)(2,1)}), bf16[128,1024]{1,0:T(8,128)(2,1)}) %reduce-scatter.32.cloned.1.call-update) | async-done | bytes 262160 | tf_op jit(solution)/shard_map/reduce_scatter | solution.py:307
  750.3 62.4 %reduce-scatter.38.cloned.1.call-done = bf16[128,256]{1,0:T(8,128)(2,1)} async-done(((bf16[1024,256]{1,0:T(8,128)(2,1)}), bf16[128,256]{1,0:T(8,128)(2,1)}) %reduce-scatter.38.cloned.1.call-update) | async-done | bytes 65552
  814.3 54.8 %reduce-scatter.36.cloned.1.call-done = bf16[16,4]{1,0:T(8,128)(2,1)} async-done(((bf16[128,4]{1,0:T(8,128)(2,1)}), bf16[16,4]{1,0:T(8,128)(2,1)}) %reduce-scatter.36.cloned.1.call-update) | async-done | bytes 144
  870.5 25.2 %reduce-scatter.28.cloned.1.call-done = bf16[128,1024]{1,0:T(8,128)(2,1)} async-done(((bf16[512,1024]{1,0:T(8,128)(2,1)}), bf16[128,1024]{1,0:T(8,128)(2,1)}) %reduce-scatter.28.cloned.1.call-update) | async-done | bytes 262160 | tf_op jit(solution)/shard_map/reduce_scatter | solution.py:291
  900.2 39.9 %all-reduce.12 = (f32[1024]{0:T(1024)S(1)}, f32[1024]{0:T(1024)S(1)}, f32[1024]{0:T(1024)S(1)}, f32[1024]{0:T(1024)S(1)}, f32[1024]{0:T(1024)S(1)}, /*index=5*/f32[1024]{0:T(1024)S(1)}) all-reduce(f32[1024]{0:T(1024)S(1)} %get-tuple-element.253, ...), channel_id=7, replica_groups=mesh['dp'=4,'seq'=4,'blk'=2] {'dp','seq','blk'}, use_global_device_ids=true, to_apply=%region_21.22.clone | all-reduce | flops 6144 | bytes 49152
  943.6 20.6 %reduce-scatter.30.cloned.1.call-done = bf16[128,768]{1,0:T(8,128)(2,1)} async-done(((bf16[1024,768]{1,0:T(8,128)(2,1)}), bf16[128,768]{1,0:T(8,128)(2,1)}) %reduce-scatter.30.cloned.1.call-update) | async-done | bytes 196624 | tf_op jit(solution)/shard_map/reduce_scatter | solution.py:298
  (243 shorter events, 99.5 us)
Async XLA Ops:
  7.2 73.2 %all-gather.10.cloned.1.call-start = ((), (), s32[]{:S(2)}) async-start(), calls=%async_computation.11 | async-start | bytes 1310720 | tf_op jit(solution)/shard_map/all_gather | solution.py:196
  8.3 51.2 %copy-start.15 = (f32[128]{0:T(128)}, f32[128]{0:T(128)S(1)}, u32[]{:S(2)}) copy-start(f32[128]{0:T(128)S(1)} %broadcast_multiply_fusion.1) | copy-start | bytes 1540
  9.5 112.3 %copy-start.17 = (f32[128]{0:T(128)}, f32[128]{0:T(128)S(1)}, u32[]{:S(2)}) copy-start(f32[128]{0:T(128)S(1)} %fusion.77) | copy-start | bytes 1540
  56.7 67.8 %copy-start.12 = (f32[1024]{0:T(1024)}, f32[1024]{0:T(1024)S(1)}, u32[]{:S(2)}) copy-start(f32[1024]{0:T(1024)S(1)} %convert_element_type.178) | copy-start | bytes 12292
  58.7 63.1 %all-gather.12.cloned.1.call-start = ((), (), s32[]{:S(2)}) async-start(), calls=%async_computation.12 | async-start | bytes 1769472 | tf_op jit(solution)/shard_map/all_gather | solution.py:186
  59.4 95.9 %all-gather.14.cloned.1.call-start = ((), (), s32[]{:S(2)}) async-start(), calls=%async_computation.13 | async-start | bytes 1572864 | tf_op jit(solution)/shard_map/all_gather | solution.py:203
  125.8 66.9 %reduce-scatter.22.cloned.1.call-start = ((), (), s32[]{:S(2)}) async-start(), calls=%async_computation.14 | async-start | bytes 1310720 | tf_op jit(solution)/shard_map/reduce_scatter | solution.py:217
  167.3 26.5 %copy-start.1 = (bf16[1024,4,64]{0,2,1:T(8,128)(2,1)}, bf16[1024,4,64]{0,2,1:T(8,128)(2,1)S(1)}, u32[]{:S(2)}) copy-start(bf16[1024,4,64]{0,2,1:T(8,128)(2,1)S(1)} %get-tuple-element.593) | copy-start | bytes 1572868
  167.3 26.5 %copy-start.9 = (bf16[1024,4,64]{0,2,1:T(8,128)(2,1)}, bf16[1024,4,64]{0,2,1:T(8,128)(2,1)S(1)}, u32[]{:S(2)}) copy-start(bf16[1024,4,64]{0,2,1:T(8,128)(2,1)S(1)} %get-tuple-element.630) | copy-start | bytes 1572868
  168.8 29.5 %copy-start.21 = (bf16[1,128]{1,0:T(2,128)(2,1)S(1)}, bf16[1,128]{1,0:T(2,128)(2,1)}, u32[]{:S(2)}) copy-start(bf16[1,128]{1,0:T(2,128)(2,1)} %param.28) | copy-start | bytes 772
  168.9 75.3 %all-gather.18.cloned.1.call-start = ((), (), s32[]{:S(2)}) async-start(), calls=%async_computation.16 | async-start | bytes 2359296 | tf_op jit(solution)/shard_map/all_gather | solution.py:191
  169.5 92.1 %all-gather.16.cloned.1.call-start = ((), (), s32[]{:S(2)}) async-start(), calls=%async_computation.15 | async-start | bytes 1310720 | tf_op jit(solution)/shard_map/all_gather | solution.py:223
  196.8 83.1 %all-gather.22.cloned.1.call-start = ((), (), s32[]{:S(2)}) async-start(), calls=%async_computation.19 | async-start | bytes 1310720 | tf_op jit(solution)/shard_map/all_gather | solution.py:224
  197.6 135.7 %all-gather.20.cloned.1.call-start = ((), (), s32[]{:S(2)}) async-start(), calls=%async_computation.17 | async-start | bytes 2359296 | tf_op jit(solution)/shard_map/all_gather | solution.py:193
  198.3 166.6 %reduce-scatter.26.cloned.1.call-start = ((), (), s32[]{:S(2)}) async-start(), calls=%async_computation.20 | async-start | bytes 1310720 | tf_op jit(solution)/shard_map/reduce_scatter | solution.py:253
  341.7 50.5 %reduce-scatter.24.cloned.1.call-start = ((), (), s32[]{:S(2)}) async-start(), calls=%async_computation.18 | async-start | bytes 1310720 | tf_op jit(solution)/shard_map/reduce_scatter | solution.py:231
  346.6 48.5 %copy-start.7 = (bf16[128,1024]{1,0:T(8,128)(2,1)S(1)}, bf16[128,1024]{1,0:T(8,128)(2,1)}, u32[]{:S(2)}) copy-start(bf16[128,1024]{1,0:T(8,128)(2,1)} %param.31) | copy-start | bytes 786436
  346.6 66.2 %all-gather.24.cloned.1.call-start = ((), (), s32[]{:S(2)}) async-start(), calls=%async_computation.21 | async-start | bytes 1310720 | tf_op jit(solution)/shard_map/all_gather | solution.py:261
  395.9 147.3 %reduce-scatter.34.cloned.1.call-start = ((), (), s32[]{:S(2)}) async-start(), calls=%async_computation.25 | async-start | bytes 1572864
  522.7 85.6 %reduce-scatter.40.cloned.1.call-start = ((), (), s32[]{:S(2)}) async-start(), calls=%async_computation.28 | async-start | bytes 294912
  523.7 154.8 %reduce-scatter.42.cloned.1.call-start = ((), (), s32[]{:S(2)}) async-start(), calls=%async_computation.29 | async-start | bytes 2359296
  529.9 218.7 %reduce-scatter.32.cloned.1.call-start = ((), (), s32[]{:S(2)}) async-start(), calls=%async_computation.24 | async-start | bytes 2359296 | tf_op jit(solution)/shard_map/reduce_scatter | solution.py:307
  534.0 278.7 %reduce-scatter.38.cloned.1.call-start = ((), (), s32[]{:S(2)}) async-start(), calls=%async_computation.27 | async-start | bytes 589824
  536.7 332.4 %reduce-scatter.36.cloned.1.call-start = ((), (), s32[]{:S(2)}) async-start(), calls=%async_computation.26 | async-start | bytes 36864
  598.1 297.6 %reduce-scatter.28.cloned.1.call-start = ((), (), s32[]{:S(2)}) async-start(), calls=%async_computation.22 | async-start | bytes 1310720 | tf_op jit(solution)/shard_map/reduce_scatter | solution.py:291
  601.7 362.5 %reduce-scatter.30.cloned.1.call-start = ((), (), s32[]{:S(2)}) async-start(), calls=%async_computation.23 | async-start | bytes 1769472 | tf_op jit(solution)/shard_map/reduce_scatter | solution.py:298
  603.9 291.7 %copy-start.13 = (f32[1024]{0:T(1024)S(1)}, f32[1024]{0:T(1024)}, u32[]{:S(2)}) copy-start(f32[1024]{0:T(1024)} %copy-done.12) | copy-start | bytes 12292
  603.9 291.7 %copy-start.16 = (f32[128]{0:T(128)S(1)}, f32[128]{0:T(128)}, u32[]{:S(2)}) copy-start(f32[128]{0:T(128)} %copy-done.15) | copy-start | bytes 1540
  603.9 292.9 %copy-start.20 = (f32[128]{0:T(128)S(1)}, f32[128]{0:T(128)}, u32[]{:S(2)}) copy-start(f32[128]{0:T(128)} %copy-done.19) | copy-start | bytes 1540
  603.9 292.9 %copy-start.18 = (f32[128]{0:T(128)S(1)}, f32[128]{0:T(128)}, u32[]{:S(2)}) copy-start(f32[128]{0:T(128)} %copy-done.17) | copy-start | bytes 1540
  604.0 294.2 %copy-start.5 = (f32[128,1024]{1,0:T(8,128)S(1)}, f32[128,1024]{1,0:T(8,128)}, u32[]{:S(2)}) copy-start(f32[128,1024]{1,0:T(8,128)} %copy-done.4) | copy-start | bytes 1572868
  604.0 294.2 %copy-start.8 = (bf16[128,1024]{1,0:T(8,128)(2,1)S(1)}, bf16[128,1024]{1,0:T(8,128)(2,1)}, u32[]{:S(2)}) copy-start(bf16[128,1024]{1,0:T(8,128)(2,1)} %param.31) | copy-start | bytes 786436
  (17 other events, 79.1 us)
Sparse Core Ops, SparseCore 0:
  58.8 16.5 all-gather.9
  77.6 44.1 all-gather.11
  125.9 28.0 all-gather.13
  169.0 23.6 reduce-scatter.21
  194.9 49.2 all-gather.17
  246.3 15.1 all-gather.15
  263.2 16.7 all-gather.21
  282.2 51.0 all-gather.19
  341.8 23.0 reduce-scatter.25
  367.3 24.8 reduce-scatter.23
  396.1 16.7 all-gather.23
  522.9 20.3 reduce-scatter.33
  547.1 61.2 reduce-scatter.39
  611.7 66.7 reduce-scatter.41
  681.9 66.5 reduce-scatter.31
  751.7 60.9 reduce-scatter.37
  816.6 52.5 reduce-scatter.35
  871.7 23.9 reduce-scatter.27
  899.1 65.0 reduce-scatter.29
where the time goes:
time: 982 us; the launch traced here: 973 us
  waiting for transfers between devices  549 us (56%)
  local copies, waits for them, and re-layouts  171 us (17%)
  blocking collectives  151 us (15%)
  matrix products  55 us (6%)
  other arithmetic  29.8 us (3%)
  between operations  15.6 us (2%)
    unnamed x24, waiting for transfers between devices  200 us
    unnamed x79, local copies, waits for them, and re-layouts  164 us
    unnamed x2, blocking collectives  82.1 us
    reduce_scatter x1, waiting for transfers between devices, local(): lax.psum_scatter(expand_grad.astype(jnp.bfloat16), ('dp', 'blk'), scatter...  68 us
    all_gather x1, waiting for transfers between devices, local(): lax.all_gather(reduce_weight, ('dp', 'blk'), axis=1, tiled=True)  53.4 us
    all_gather x1, waiting for transfers between devices, local(): lax.all_gather(joint_weight, ('dp', 'blk'), axis=0, tiled=True)  41.4 us
    all_gather x1, blocking collectives, local(): lax.all_gather(output_weight, ('dp', 'blk'), axis=1, tiled=True)  28 us
    reduce_scatter x1, waiting for transfers between devices, local(): lax.psum_scatter(result_part.astype(jnp.bfloat16), 'seq', scatter_dimensi...  26 us
  transfers between devices with their start and end apart: 19, of which 17 were waited for; matrix products, arithmetic and copies ran while one was open for 11% of the time, Pallas kernels for 0%

commit v1 on v0

--- a/solution.py
+++ b/solution.py
@@ -1,6 +1,10 @@
+import functools
+
 import jax
 import jax.numpy as jnp
 from jax import lax
+from jax.experimental import pallas as pl
+from jax.experimental.pallas import tpu as pltpu
 from jax.sharding import PartitionSpec as P
 
 H = 16
@@ -340,9 +344,807 @@
     )
 
 
+ALL = ("dp", "seq", "blk")
+PLANE = ("seq", "blk")
+
+
+def swap(value, axes, count, offset):
+    return lax.ppermute(value, axes, [(i, i ^ offset) for i in range(count)])
+
+
+def low(value):
+    return value.astype(jnp.bfloat16)
+
+
+def wide(value):
+    return value.astype(jnp.float32)
+
+
+ANY = pl.BlockSpec(memory_space=pl.ANY)
+VMEM = pl.BlockSpec(memory_space=pltpu.VMEM)
+SMEM = pl.BlockSpec(memory_space=pltpu.SMEM)
+STEP = 256
+PAIR = 2 * HD
+QKV = 3 * PAIR
+COLUMNS = QKV + PAIR
+SMALL = 16
+LANES = 128
+
+
+def struct(rows, columns, dtype):
+    return jax.ShapeDtypeStruct((rows, columns), dtype)
+
+
+def contract(left, right, left_dim, right_dim):
+    return lax.dot_general(
+        left, right, (((left_dim,), (right_dim,)), ((), ())), preferred_element_type=jnp.float32
+    )
+
+
+def call(kernel, outs, specs, operands, scratch=(), cost=1.0, room=24):
+    return pl.pallas_call(
+        kernel,
+        out_shape=outs,
+        in_specs=specs,
+        out_specs=[VMEM] * len(outs),
+        scratch_shapes=list(scratch),
+        compiler_params=pltpu.CompilerParams(vmem_limit_bytes=room * 2**20),
+        cost_estimate=pl.CostEstimate(flops=int(cost * 1.1e9), bytes_accessed=0, transcendentals=0),
+    )(*operands)
+
+
+def fetch(pairs, sems):
+    copies = [
+        pltpu.make_async_copy(source, target, sems.at[k])
+        for k, (source, target) in enumerate(pairs)
+    ]
+    for copy in copies:
+        copy.start()
+    for copy in copies:
+        copy.wait()
+
+
+def row_starts(place, order, rows):
+    return [pl.multiple_of((place ^ offset) * rows, rows) for offset in order]
+
+
+def head_lanes(shape):
+    return lax.broadcasted_iota(jnp.int32, shape, 1) // HD
+
+
+def normalise(values):
+    average = jnp.mean(values, -1, keepdims=True)
+    centred = values - average
+    variance = jnp.mean(centred * centred, -1, keepdims=True)
+    scale = lax.rsqrt(variance + epsilon)
+    return (centred * scale, scale)
+
+
+def norm_back(grad, xhat, scale, gain_row):
+    scaled = grad * gain_row
+    mean_scaled = jnp.mean(scaled, -1, keepdims=True)
+    mean_product = jnp.mean(scaled * xhat, -1, keepdims=True)
+    return scale * (scaled - mean_scaled - xhat * mean_product)
+
+
+def normalise_kernel(order, spots, *refs):
+    pieces, (xhat_ref, held, sems) = refs[: len(order)], refs[len(order) :]
+    rows = pieces[0].shape[0]
+    starts = row_starts(spots[3], order, rows)
+    fetch([(p, held.at[pl.ds(s, rows)]) for p, s in zip(pieces, starts)], sems)
+
+    @pl.loop(0, held.shape[0] // STEP)
+    def _(step):
+        block = pl.ds(pl.multiple_of(step * STEP, STEP), STEP)
+        xhat_ref[block] = normalise(wide(held[block]))[0]
+
+
+def reorder_columns(spots, source_ref, out_ref, count):
+    size = out_ref.shape[1] // count
+    for p in range(count):
+        start = pl.multiple_of((spots[0] ^ p) * size, size)
+        out_ref[:, p * size : (p + 1) * size] = source_ref[:, pl.ds(start, size)]
+
+
+def prepare_attention_kernel(dp_count, blk_count, spots, *refs):
+    joint_ref, output_ref, tokens_ref = refs[:3]
+    vectors, (pair_ref, expand_ref) = refs[3:9], refs[9:11]
+    outs = refs[11:]
+    blocks, (own_ref, small_ref, turned) = outs[:blk_count], outs[blk_count:]
+    turned[...] = low(wide(joint_ref[...]).T)
+    for b, block in enumerate(blocks):
+        first = (spots[2] ^ b) * 2
+        for head in range(2):
+            for part in range(3):
+                start = pl.multiple_of(((first + head) * 3 + part) * HD, HD)
+                row = part * PAIR + head * HD
+                block[row : row + HD] = turned[pl.ds(start, HD)]
+        start = pl.multiple_of(first * HD, PAIR)
+        block[QKV:] = output_ref[pl.ds(start, PAIR)]
+    reorder_columns(spots, tokens_ref, own_ref, dp_count)
+    small = jnp.zeros(small_ref.shape, jnp.float32)
+    row = lax.broadcasted_iota(jnp.int32, small.shape, 0)
+    for k, vector in enumerate(vectors):
+        piece = wide(vector[...])
+        line = jnp.concatenate([piece, jnp.zeros((1, LANES - piece.shape[1]), jnp.float32)], 1)
+        small = jnp.where(row == k, line, small)
+    pair = wide(pair_ref[...])
+    pair = jnp.concatenate([pair, jnp.zeros((pair.shape[0], LANES - pair.shape[1]), jnp.float32)], 1)
+    for k in range(pair.shape[0]):
+        small = jnp.where(row == 6 + k, pair[k : k + 1], small)
+    small = jnp.where(row == 6 + pair.shape[0], wide(expand_ref[...]), small)
+    small_ref[...] = low(small)
+
+
+def prepare_forward_kernel(dp_count, blk_count, spots, *refs):
+    expand_ref, reduce_ref, cot_ref, _ = refs[:4]
+    blocks, (own_ref, turned) = refs[4 : 4 + blk_count], refs[4 + blk_count :]
+    turned[...] = low(wide(expand_ref[...]).T)
+    units = turned.shape[0] // blk_count
+    for b, block in enumerate(blocks):
+        start = pl.multiple_of((spots[2] ^ b) * units, units)
+        block[:units] = turned[pl.ds(start, units)]
+        block[units:] = reduce_ref[pl.ds(start, units)]
+    reorder_columns(spots, cot_ref, own_ref, dp_count)
+
+
+def pack_kernel(blk_count, has_small, spots, *refs):
+    blocks, out_ref = refs[:blk_count], refs[-1]
+    rows = blocks[0].shape[0]
+    for b, block in enumerate(blocks):
+        start = pl.multiple_of((spots[2] ^ b) * LANES, LANES)
+        out_ref[:rows, pl.ds(start, LANES)] = block[...]
+    if has_small:
+        small_ref = refs[blk_count]
+        count = small_ref.shape[0] // SMALL
+        deep = count // blk_count
+        for m in range(count):
+            start = pl.multiple_of((spots[3] ^ m) * SMALL, SMALL)
+            row, lane = rows + m % deep * SMALL, m // deep * LANES
+            out_ref[row : row + SMALL, lane : lane + LANES] = small_ref[pl.ds(start, SMALL)]
+
+
+def unpack_kernel(dp_count, plane_count, blk_count, pair_rows, spots, *refs):
+    blocks = refs[:dp_count]
+    vector_ref, joint_ref, expand_ref, held, small, sems = refs[dp_count:]
+    dp, seq, blk = spots[0], spots[1], spots[2]
+    deep = held.shape[1]
+    fetch([(b.at[pl.ds(COLUMNS, deep)], held.at[d]) for d, b in enumerate(blocks)], sems)
+    for d in range(dp_count):
+        for b in range(blk_count):
+            start = (d * blk_count + b) * deep
+            small[start : start + deep] = wide(held[d, :, b * LANES : (b + 1) * LANES])
+    piece = vector_ref.shape[1] // (dp_count * plane_count)
+    group = LANES // piece
+    for first in range(0, dp_count * plane_count, group):
+        parts = [
+            small[(first + k) * SMALL : (first + k) * SMALL + 8, :piece] for k in range(group)
+        ]
+        vector_ref[:, first * piece : (first + group) * piece] = jnp.concatenate(parts, 1)
+
+    def line(owner, row):
+        start = ((dp ^ (owner // blk_count)) * plane_count + seq * blk_count + owner % blk_count)
+        return small[pl.ds(start * SMALL + row, 1)]
+
+    owners = dp_count * blk_count
+    width = 2 * HD // owners
+    pairs = [
+        jnp.concatenate([line(o, 6 + blk * 2 + head)[:, :width] for o in range(owners)], 1)
+        for head in range(2)
+    ]
+    joint = jnp.concatenate(
+        [pairs[0][:, :HD], pairs[1][:, :HD], jnp.zeros((1, PAIR), jnp.float32)]
+        + [pairs[0][:, HD:], pairs[1][:, HD:]],
+        1,
+    )
+    joint_ref[...] = jnp.broadcast_to(joint, joint_ref.shape)
+    mine = owners // blk_count
+    hidden = jnp.concatenate([line(blk * mine + k, 6 + pair_rows) for k in range(mine)], 1)
+    expand_ref[...] = jnp.broadcast_to(hidden, expand_ref.shape)
+
+
+def score_block(queries, keys, slope, first):
+    scores = contract(queries, keys, 1, 1)
+    column = lax.broadcasted_iota(jnp.int32, scores.shape, 1)
+    row = lax.broadcasted_iota(jnp.int32, scores.shape, 0) + first
+    places = lax.broadcasted_iota(jnp.int32, (1, scores.shape[1]), 1) - (first + STEP - 1)
+    return jnp.where(column <= row, scores + slope * wide(places), -1e30)
+
+
+def split_rows(part_of, order, starts, rows, own_ref, away_ref):
+    half = len(order) // 2
+    for k, start in enumerate(starts):
+        part = part_of(start)
+        if k < half:
+            own_ref[k * rows : (k + 1) * rows] = part
+        else:
+            away_ref[(k - half) * rows : (k - half + 1) * rows] = low(part)
+
+
+def attend_kernel(order, dp_count, spots, slope_ref, *refs):
+    blocks = refs[:dp_count]
+    xhat_ref, vector_ref, bias_ref = refs[dp_count : dp_count + 3]
+    mixed_ref, att_ref, lse_ref, weight_ref, own_ref, away_ref, sems = refs[dp_count + 3 :]
+    cut = weight_ref.shape[1] // dp_count
+    fetch(
+        [
+            (b.at[pl.ds(0, COLUMNS)], weight_ref.at[:, pl.ds(d * cut, cut)])
+            for d, b in enumerate(blocks)
+        ],
+        sems,
+    )
+    count = xhat_ref.shape[0]
+
+    @pl.loop(0, count // STEP)
+    def _(step):
+        block = pl.ds(pl.multiple_of(step * STEP, STEP), STEP)
+        normed = low(xhat_ref[block] * vector_ref[:1] + vector_ref[1:2])
+        mixed_ref[block] = low(contract(normed, weight_ref[:QKV], 1, 1) + bias_ref[:1])
+
+    lanes = head_lanes((STEP, PAIR))
+    for first in range(0, count, STEP):
+        stop = first + STEP
+        queries = mixed_ref[first:stop, :PAIR] * jnp.bfloat16(HD**-0.5)
+        keys, values = mixed_ref[:stop, PAIR : 2 * PAIR], mixed_ref[:stop, 2 * PAIR :]
+        attended = log_sums = None
+        for head in range(2):
+            chosen = jnp.where(lanes == head, queries, 0)
+            scores = score_block(chosen, keys, slope_ref[head], first)
+            top = jnp.max(scores, -1, keepdims=True)
+            weights = jnp.exp(scores - top)
+            total = jnp.sum(weights, -1, keepdims=True)
+            result = contract(low(weights), values, 1, 0) / total
+            log_sum = jnp.broadcast_to(top + jnp.log(total), result.shape)
+            attended = result if head == 0 else jnp.where(lanes == 1, result, attended)
+            log_sums = log_sum if head == 0 else jnp.where(lanes == 1, log_sum, log_sums)
+        att_ref[first:stop] = attended
+        lse_ref[first:stop] = log_sums
+    rows = count // len(order)
+    starts = row_starts(spots[3], order, rows)
+    split_rows(
+        lambda start: contract(low(att_ref[pl.ds(start, rows)]), weight_ref[QKV:], 1, 0),
+        order, starts, rows, own_ref, away_ref,
+    )
+
+
+def attend_back_kernel(order, spots, slope_ref, *refs):
+    pieces = refs[: len(order)]
+    mixed_ref, att_ref, lse_ref, weight_ref, _ = refs[len(order) : len(order) + 5]
+    grad_ref, own_ref, away_ref, held, pulled, key_sum, value_sum, sems = refs[len(order) + 5 :]
+    rows = pieces[0].shape[0]
+    starts = row_starts(spots[3], order, rows)
+    fetch([(p, held.at[pl.ds(s, rows)]) for p, s in zip(pieces, starts)], sems)
+    count = held.shape[0]
+
+    @pl.loop(0, count // STEP)
+    def _(step):
+        block = pl.ds(pl.multiple_of(step * STEP, STEP), STEP)
+        pulled[block] = low(contract(held[block], weight_ref[QKV:], 1, 1))
+
+    key_sum[...] = jnp.zeros_like(key_sum)
+    value_sum[...] = jnp.zeros_like(value_sum)
+    lanes = head_lanes((STEP, PAIR))
+    for first in range(0, count, STEP):
+        stop = first + STEP
+        queries = mixed_ref[first:stop, :PAIR] * jnp.bfloat16(HD**-0.5)
+        keys, values = mixed_ref[:stop, PAIR : 2 * PAIR], mixed_ref[:stop, 2 * PAIR :]
+        key_lanes = head_lanes(keys.shape)
+        grads = pulled[first:stop]
+        products = wide(grads) * att_ref[first:stop]
+        query_grad = None
+        for head in range(2):
+            chosen = jnp.where(lanes == head, queries, 0)
+            chosen_grads = jnp.where(lanes == head, grads, 0)
+            delta = jnp.sum(jnp.where(lanes == head, products, 0.0), -1, keepdims=True)
+            scores = score_block(chosen, keys, slope_ref[head], first)
+            probs = jnp.exp(scores - lse_ref[first:stop, head * HD : head * HD + 1])
+            prob_grad = contract(chosen_grads, values, 1, 1)
+            score_grad = low(probs * (prob_grad - delta))
+            term = contract(score_grad, jnp.where(key_lanes == head, keys, 0), 1, 0)
+            query_grad = term if head == 0 else query_grad + term
+            key_sum[:stop] += contract(score_grad, chosen, 0, 0)
+            value_sum[:stop] += contract(low(probs), chosen_grads, 0, 0)
+        grad_ref[first:stop, :PAIR] = low(query_grad * HD**-0.5)
+    grad_ref[:, PAIR : 2 * PAIR] = low(key_sum[...])
+    grad_ref[:, 2 * PAIR :] = low(value_sum[...])
+    split_rows(
+        lambda start: contract(grad_ref[pl.ds(start, rows)], weight_ref[:QKV], 1, 0),
+        order, starts, rows, own_ref, away_ref,
+    )
+
+
+def pack_small(spots, dp_count, blk_count, vectors, pairs, hidden, small):
+    dp, seq, blk = spots[0], spots[1], spots[2]
+    small[...] = jnp.zeros_like(small)
+    count = small.shape[0] // SMALL
+    plane_count = count // dp_count
+    width = vectors.shape[1]
+    piece = width // count
+    empty = jnp.zeros((8, LANES - piece), jnp.float32)
+    for k in range(count):
+        part = jnp.concatenate([vectors[:, k * piece : (k + 1) * piece], empty], 1)
+        small[k * SMALL : k * SMALL + 8] = part
+    owners = dp_count * blk_count
+    size = 2 * HD // owners
+    lane = lax.broadcasted_iota(jnp.int32, (1, LANES), 1)
+    mine = owners // blk_count
+    for owner in range(owners):
+        spot = (dp ^ (owner // blk_count)) * plane_count + seq * blk_count + owner % blk_count
+        for head in range(2):
+            part = pairs[head]
+            if owner:
+                part = jnp.concatenate([part[:, owner * size :], part[:, : owner * size]], 1)
+            row = spot * SMALL + 6 + blk * 2 + head
+            small[pl.ds(row, 1)] = jnp.where(lane < size, part, 0.0)
+        part = hidden[:, owner % mine * LANES : (owner % mine + 1) * LANES]
+        row = spot * SMALL + 6 + 2 * blk_count
+        small[pl.ds(row, 1)] = jnp.where(blk == owner // mine, part, 0.0)
+
+
+def attend_weights_kernel(order, dp_count, blk_count, spots, *refs):
+    pieces = refs[: len(order)]
+    xhat_ref, grad_ref, att_ref, weight_ref, vector_ref = refs[len(order) : len(order) + 5]
+    sums_ref, hidden_ref = refs[len(order) + 5 : len(order) + 7]
+    outs = refs[len(order) + 7 :]
+    parts, (held, small, sems) = outs[:dp_count], outs[dp_count:]
+    rows = pieces[0].shape[0]
+    starts = row_starts(spots[3], order, rows)
+    fetch([(p, held.at[pl.ds(s, rows)]) for p, s in zip(pieces, starts)], sems)
+    mixed_grad, attended = grad_ref[...], low(att_ref[...])
+    sums = jnp.sum(wide(mixed_grad), 0, keepdims=True)
+    column = jnp.broadcast_to(sums, (8, QKV)).T[:, :1]
+    cut = weight_ref.shape[1] // dp_count
+    lines = [[], []]
+    for d, part in enumerate(parts):
+        block = slice(d * cut, (d + 1) * cut)
+        plain = contract(mixed_grad, low(xhat_ref[:, block]), 0, 0)
+        joint_grad = vector_ref[:1, block] * plain + vector_ref[1:2, block] * column
+        part[:QKV] = joint_grad.astype(part.dtype)
+        part[QKV:COLUMNS] = contract(attended, held[:, block], 0, 0).astype(part.dtype)
+        weights = wide(weight_ref[:QKV, block])
+        for k, product in enumerate((weights * plain, weights * column)):
+            lines[k].append(jnp.sum(product, 0, keepdims=True))
+    lines = [jnp.concatenate(line, 1) for line in lines]
+    vectors = jnp.concatenate(lines + [sums_ref[:4], jnp.zeros_like(sums_ref[:2])], 0)
+    pairs = [
+        jnp.concatenate([sums[:, h * HD : (h + 1) * HD], sums[:, 2 * PAIR + h * HD : 2 * PAIR + (h + 1) * HD]], 1)
+        for h in range(2)
+    ]
+    pack_small(spots, dp_count, blk_count, vectors, pairs, hidden_ref[:1], small)
+    plane_rows = small.shape[0] // dp_count
+    deep = plane_rows // blk_count
+    for d, part in enumerate(parts):
+        for b in range(blk_count):
+            start = d * plane_rows + b * deep
+            part[COLUMNS:, b * LANES : (b + 1) * LANES] = small[start : start + deep].astype(part.dtype)
+
+
+def split_kernel(count, blk_count, has_small, spots, total_ref, *refs):
+    came, outs = refs[:count], refs[count:]
+    total = outs[-1]
+    total[...] = wide(summed(total_ref, came))
+    rows = outs[0].shape[0]
+    for b in range(blk_count):
+        start = pl.multiple_of((spots[2] ^ b) * LANES, LANES)
+        outs[b][...] = total[:rows, pl.ds(start, LANES)].astype(outs[b].dtype)
+    if has_small:
+        small_ref = outs[blk_count]
+        devices = small_ref.shape[0] // SMALL
+        deep = devices // blk_count
+        for m in range(devices):
+            start = pl.multiple_of((spots[3] ^ m) * SMALL, SMALL)
+            row, lane = rows + m % deep * SMALL, m // deep * LANES
+            small_ref[pl.ds(start, SMALL)] = total[row : row + SMALL, lane : lane + LANES]
+
+
+def attend_final_kernel(blk_count, spots, *refs):
+    blocks, (joint_ref, output_ref) = refs[:blk_count], refs[blk_count:]
+    for b, block in enumerate(blocks):
+        other = spots[2] ^ b
+        values = wide(block[...])
+        turned = values[:QKV].T
+        ordered = jnp.concatenate(
+            [turned[:, part * PAIR + h * HD : part * PAIR + (h + 1) * HD] for h in range(2) for part in range(3)],
+            1,
+        )
+        joint_ref[:, pl.ds(pl.multiple_of(other * QKV, LANES), QKV)] = ordered
+        output_ref[pl.ds(pl.multiple_of(other * PAIR, PAIR), PAIR)] = values[QKV:]
+
+
+def forward_final_kernel(blk_count, spots, *refs):
+    blocks, (expand_ref, reduce_ref) = refs[:blk_count], refs[blk_count:]
+    units = reduce_ref.shape[0] // blk_count
+    for b, block in enumerate(blocks):
+        start = pl.multiple_of((spots[2] ^ b) * units, units)
+        expand_ref[:, pl.ds(start, units)] = wide(block[:units]).T
+        reduce_ref[pl.ds(start, units)] = wide(block[units:])
+
+
+def forward_fetch(count, dp_count, spots, pieces, weights, left, right, held, sems):
+    rows, cut = pieces[0].shape[0], weights.shape[2]
+    fetch(
+        [(p, left.at[pl.ds(k * rows, rows)]) for k, p in enumerate(pieces[:count])]
+        + [(p, right.at[pl.ds(k * rows, rows)]) for k, p in enumerate(pieces[count:])]
+        + [
+            (weights.at[spots[0] ^ d], held.at[:, pl.ds(d * cut, cut)]) for d in range(dp_count)
+        ],
+        sems,
+    )
+
+
+def forward_kernel(count, dp_count, spots, *refs):
+    pieces, weights = refs[: 2 * count], refs[2 * count]
+    bias_ref, act_ref, grad_ref, own_ref, away_ref, sum_ref, left, right, held, sems = refs[2 * count + 1 :]
+    forward_fetch(count, dp_count, spots, pieces, weights, left, right, held, sems)
+    units = act_ref.shape[1]
+    half = left.shape[0] // 2
+    sum_ref[...] = jnp.zeros_like(sum_ref)
+    root = (2.0 / jnp.pi) ** 0.5
+    for first in range(0, left.shape[0], STEP):
+        stop = first + STEP
+        hidden = contract(left[first:stop], held[:units], 1, 1) + bias_ref[:1]
+        square = hidden * hidden
+        bend = jnp.tanh(root * hidden * (1.0 + 0.044715 * square))
+        act_ref[first:stop] = low(0.5 * hidden * (1.0 + bend))
+        slope = 0.5 * (1.0 + bend) + 0.5 * hidden * (1.0 - bend * bend) * root * (
+            1.0 + 3 * 0.044715 * square
+        )
+        hidden_grad = low(contract(right[first:stop], held[units:], 1, 1) * slope)
+        grad_ref[first:stop] = hidden_grad
+        sum_ref[...] += jnp.sum(wide(hidden_grad), 0, keepdims=True)
+        part = contract(hidden_grad, held[:units], 1, 0)
+        if first < half:
+            own_ref[first:stop] = part
+        else:
+            away_ref[first - half : stop - half] = low(part)
+
+
+def forward_weights_kernel(count, dp_count, spots, *refs):
+    pieces, weights = refs[: 2 * count], refs[2 * count]
+    act_ref, grad_ref, _ = refs[2 * count + 1 : 2 * count + 4]
+    part_ref, own_ref, away_ref, left, right, held, sems = refs[2 * count + 4 :]
+    forward_fetch(count, dp_count, spots, pieces, weights, left, right, held, sems)
+    units, cut = act_ref.shape[1], weights.shape[2]
+    for d in range(dp_count):
+        block = slice(d * cut, (d + 1) * cut)
+        spot = spots[0] ^ d
+        part_ref[spot, :units] = low(contract(grad_ref[...], left[:, block], 0, 0))
+        part_ref[spot, units:] = low(contract(act_ref[...], right[:, block], 0, 0))
+    half = left.shape[0] // 2
+    for first in range(0, left.shape[0], STEP):
+        stop = first + STEP
+        result = contract(act_ref[first:stop], held[units:], 1, 0)
+        if first < half:
+            own_ref[first:stop] = result
+        else:
+            away_ref[first - half : stop - half] = low(result)
+
+
+def add_kernel(own_ref, came_ref, after, total_ref, *pieces):
+    rows = total_ref.shape[0]
+    total_ref[...] = own_ref[:rows] + wide(came_ref[:rows])
+    for k, piece in enumerate(pieces):
+        block = slice((k + 1) * rows, (k + 2) * rows)
+        piece[...] = low(own_ref[block] + wide(came_ref[block]))
+
+
+def summed(total_ref, came):
+    total = total_ref[...]
+    for piece in came:
+        total = total + wide(piece[...])
+    return total
+
+
+def middle_kernel(count, total_ref, *refs):
+    came = refs[:count]
+    tokens_ref, vector_ref, middle_ref, normed_ref = refs[count:]
+    middle = wide(tokens_ref[...]) + (summed(total_ref, came) + vector_ref[2:3])
+    middle_ref[...] = middle
+    normed_ref[...] = low(normalise(middle)[0] * vector_ref[3:4] + vector_ref[4:5])
+
+
+def middle_back_kernel(count, total_ref, *refs):
+    came = refs[:count]
+    middle_ref, cot_ref, vector_ref, grad_ref, branch_ref, sums_ref = refs[count:]
+    grad = summed(total_ref, came)
+    xhat, scale = normalise(middle_ref[...])
+    upstream = wide(cot_ref[...])
+    total = upstream + norm_back(grad, xhat, scale, vector_ref[3:4])
+    grad_ref[...] = total
+    branch = low(total)
+    branch_ref[...] = branch
+    sums_ref[...] = jnp.zeros_like(sums_ref)
+    for k, values in enumerate((wide(branch), grad * xhat, grad, upstream)):
+        sums_ref[k : k + 1] = jnp.sum(values, 0, keepdims=True)
+
+
+def place_columns(spots, dp_count, values, out_ref):
+    size = out_ref.shape[1] // dp_count
+    for d in range(dp_count):
+        start = pl.multiple_of((spots[0] ^ d) * size, size)
+        out_ref[:, pl.ds(start, size)] = values[:, d * size : (d + 1) * size]
+
+
+def output_kernel(count, dp_count, spots, total_ref, *refs):
+    came = refs[:count]
+    middle_ref, vector_ref, out_ref = refs[count:]
+    result = middle_ref[...] + (summed(total_ref, came) + vector_ref[5:6])
+    place_columns(spots, dp_count, low(result), out_ref)
+
+
+def input_kernel(count, dp_count, spots, total_ref, *refs):
+    came = refs[:count]
+    grad_ref, tokens_ref, vector_ref, out_ref = refs[count:]
+    xhat, scale = normalise(wide(tokens_ref[...]))
+    result = grad_ref[...] + norm_back(summed(total_ref, came), xhat, scale, vector_ref[:1])
+    place_columns(spots, dp_count, low(result), out_ref)
+
+
+def local_heads(
+    tokens,
+    first_gain,
+    first_shift,
+    joint_weight,
+    joint_bias,
+    output_weight,
+    output_bias,
+    second_gain,
+    second_shift,
+    expand_weight,
+    expand_bias,
+    reduce_weight,
+    reduce_bias,
+    cotangent,
+):
+    dp_count, seq_count, blk_count = (lax.axis_size(axis) for axis in ALL)
+    dp, seq, blk = (lax.axis_index(axis) for axis in ALL)
+    plane_count = seq_count * blk_count
+    place = seq * blk_count + blk
+    spots = jnp.stack([dp, seq, blk, place]).astype(jnp.int32)
+    tok_rows, width = tokens.shape
+    units = expand_weight.shape[1] // blk_count
+    cut = width // dp_count
+    piece = first_gain.shape[0]
+    core = blk_count
+    chips = [p for p in range(plane_count) if not p & core]
+    order = chips + [p ^ core for p in chips]
+    chip_count = len(chips)
+    row_count, half_rows = plane_count * tok_rows, chip_count * tok_rows
+    f32, bf16 = jnp.float32, jnp.bfloat16
+    halves_out = [struct(half_rows, width, f32), struct(half_rows, width, bf16)]
+    own_out = [struct(tok_rows, width, f32)]
+    low_out = [struct(tok_rows, width, bf16)]
+    dma = lambda count: pltpu.SemaphoreType.DMA((count,))
+    held = lambda columns: pltpu.VMEM((row_count, columns), bf16)
+    kernel = functools.partial
+
+    def gather_plane(block):
+        mine = [block] + [swap(block, PLANE, plane_count, chip) for chip in chips[1:]]
+        return mine + [swap(p, PLANE, plane_count, core) for p in mine]
+
+    def scatter_plane(own, away, after=None):
+        came = swap(away, PLANE, plane_count, core)
+        after = own if after is None else after
+        outs = own_out + low_out * (chip_count - 1)
+        total, *pieces = call(add_kernel, outs, [VMEM, VMEM, ANY], [own, came, after])
+        pieces = [swap(p, PLANE, plane_count, chip) for chip, p in zip(chips[1:], pieces)]
+        return [total] + pieces
+
+    def exchange_blk(blocks):
+        return [swap(p, "blk", blk_count, b) if b else p for b, p in enumerate(blocks)]
+
+    *blocks, tokens_own, small = call(
+        kernel(prepare_attention_kernel, dp_count, blk_count),
+        [struct(COLUMNS, LANES, bf16)] * blk_count + low_out + [struct(SMALL, LANES, bf16)],
+        [SMEM] + [VMEM] * 11,
+        [spots, joint_weight, output_weight, tokens]
+        + [
+            v.reshape(1, -1)
+            for v in (first_gain, first_shift, output_bias, second_gain, second_shift, reduce_bias)
+        ]
+        + [joint_bias, expand_bias],
+        [pltpu.VMEM((joint_weight.shape[1], LANES), bf16)],
+        2,
+    )
+    bits = [1 << b for b in range(plane_count.bit_length() - 1)]
+    blocks = exchange_blk(blocks)
+    for bit in bits:
+        small = jnp.concatenate([small, swap(small, PLANE, plane_count, bit)], 0)
+    small_deep = plane_count * SMALL // blk_count
+    block = call(
+        kernel(pack_kernel, blk_count, True),
+        [struct(COLUMNS + small_deep, cut, bf16)],
+        [SMEM] + [VMEM] * (blk_count + 1),
+        [spots] + blocks + [small],
+    )[0]
+    blocks = [block] + [swap(block, "dp", dp_count, d) for d in range(1, dp_count)]
+    token_group = gather_plane(tokens_own)
+
+    *forward_blocks, cotangent_own = call(
+        kernel(prepare_forward_kernel, dp_count, blk_count),
+        [struct(2 * units, LANES, bf16)] * blk_count + low_out,
+        [SMEM] + [VMEM] * 3 + [ANY],
+        [spots, expand_weight, reduce_weight, cotangent, block],
+        [pltpu.VMEM((expand_weight.shape[1], LANES), bf16)],
+        2,
+    )
+    forward_block = call(
+        kernel(pack_kernel, blk_count, False),
+        [struct(2 * units, cut, bf16)],
+        [SMEM] + [VMEM] * blk_count,
+        [spots] + exchange_blk(forward_blocks),
+    )[0]
+    forward_weights = lax.all_gather(forward_block, "dp", axis=0, tiled=False)
+    cot_group = gather_plane(cotangent_own)
+
+    xhat = call(
+        kernel(normalise_kernel, order),
+        [struct(row_count, width, f32)],
+        [SMEM] + [ANY] * plane_count,
+        [spots] + token_group,
+        [held(width), dma(plane_count)],
+        2,
+    )[0]
+    vectors, joint_row, expand_row = call(
+        kernel(unpack_kernel, dp_count, plane_count, blk_count, joint_bias.shape[0]),
+        [struct(8, width, f32), struct(8, QKV, f32), struct(8, units, f32)],
+        [SMEM] + [ANY] * dp_count,
+        [spots] + blocks,
+        [
+            pltpu.VMEM((dp_count, small_deep, cut), bf16),
+            pltpu.VMEM((dp_count * plane_count * SMALL, LANES), f32),
+            dma(dp_count),
+        ],
+    )
+    head_ids = place * 2 + jnp.arange(2, dtype=jnp.int32)
+    slopes = jnp.exp2(-8.0 * (head_ids + 1).astype(f32) / H)
+    mixed, attended, log_sums, weights, own, away = call(
+        kernel(attend_kernel, order, dp_count),
+        [struct(row_count, QKV, bf16), struct(row_count, PAIR, f32)]
+        + [struct(row_count, PAIR, f32), struct(COLUMNS, width, bf16)]
+        + halves_out,
+        [SMEM, SMEM] + [ANY] * dp_count + [VMEM] * 3,
+        [spots, slopes] + blocks + [xhat, vectors, joint_row],
+        [dma(dp_count)],
+        10,
+    )
+    branch = scatter_plane(own, away)
+
+    middle, normed_two = call(
+        kernel(middle_kernel, chip_count - 1),
+        own_out + low_out,
+        [VMEM] * (chip_count + 2),
+        branch + [tokens_own, vectors],
+    )
+    normed_group = gather_plane(normed_two)
+    forward_operands = [spots] + normed_group + cot_group + [forward_weights]
+    forward_specs = [SMEM] + [ANY] * (2 * plane_count + 1)
+    forward_scratch = [held(width), held(width), pltpu.VMEM((2 * units, width), bf16)]
+    forward_scratch.append(dma(2 * plane_count + dp_count))
+    activated, hidden_grad, own, away, hidden_sums = call(
+        kernel(forward_kernel, plane_count, dp_count),
+        [struct(row_count, units, bf16)] * 2 + halves_out + [struct(8, units, f32)],
+        forward_specs + [VMEM],
+        forward_operands + [expand_row],
+        forward_scratch,
+        8,
+    )
+    normed_two_grad = scatter_plane(own, away)
+    middle_grad, branch_grad, middle_sums = call(
+        kernel(middle_back_kernel, chip_count - 1),
+        own_out + low_out + [struct(8, width, f32)],
+        [VMEM] * (chip_count + 3),
+        normed_two_grad + [middle, cotangent_own, vectors],
+    )
+    forward_grad, own, away = call(
+        kernel(forward_weights_kernel, plane_count, dp_count),
+        [jax.ShapeDtypeStruct((dp_count, 2 * units, cut), bf16)] + halves_out,
+        forward_specs + [VMEM, VMEM, ANY],
+        forward_operands + [activated, hidden_grad, normed_two_grad[0]],
+        forward_scratch,
+        8,
+    )
+    forward_grad = lax.psum_scatter(forward_grad, "dp", scatter_dimension=0, tiled=False)
+    forward_grad = call(
+        kernel(split_kernel, 0, blk_count, False),
+        [struct(2 * units, LANES, f32)] + [struct(2 * units, LANES, bf16)] * (blk_count - 1),
+        [SMEM, VMEM],
+        [spots, forward_grad],
+        [pltpu.VMEM((2 * units, cut), f32)],
+    )
+    expand_grad, reduce_grad = call(
+        kernel(forward_final_kernel, blk_count),
+        [struct(LANES, blk_count * units, f32), struct(blk_count * units, LANES, f32)],
+        [SMEM] + [VMEM] * blk_count,
+        [spots] + exchange_blk(forward_grad),
+    )
+
+    branch_group = gather_plane(branch_grad)
+    result = scatter_plane(own, away, branch_group[-1])
+    layer_output = call(
+        kernel(output_kernel, chip_count - 1, dp_count),
+        low_out,
+        [SMEM] + [VMEM] * (chip_count + 2),
+        [spots] + result + [middle, vectors],
+    )[0]
+    mixed_grad, own, away = call(
+        kernel(attend_back_kernel, order),
+        [struct(row_count, QKV, bf16)] + halves_out,
+        [SMEM, SMEM] + [ANY] * plane_count + [VMEM] * 4 + [ANY],
+        [spots, slopes] + branch_group + [mixed, attended, log_sums, weights, result[0]],
+        [held(width), held(PAIR)]
+        + [pltpu.VMEM((row_count, PAIR), f32)] * 2
+        + [dma(plane_count)],
+        10,
+    )
+    block_out = lambda dtype: struct(COLUMNS + small_deep, cut, dtype)
+    attention_grad = call(
+        kernel(attend_weights_kernel, order, dp_count, blk_count),
+        [block_out(f32)] + [block_out(bf16)] * (dp_count - 1),
+        [SMEM] + [ANY] * plane_count + [VMEM] * 7,
+        [spots]
+        + branch_group
+        + [xhat, mixed_grad, attended, weights, vectors, middle_sums, hidden_sums],
+        [held(width), pltpu.VMEM((dp_count * plane_count * SMALL, LANES), f32), dma(plane_count)],
+        8,
+    )
+    normed_one_grad = scatter_plane(own, away)
+    input_grad = call(
+        kernel(input_kernel, chip_count - 1, dp_count),
+        low_out,
+        [SMEM] + [VMEM] * (chip_count + 3),
+        [spots] + normed_one_grad + [middle_grad, tokens_own, vectors],
+    )[0]
+    attention_grad = [attention_grad[0]] + [
+        swap(attention_grad[d], "dp", dp_count, d) for d in range(1, dp_count)
+    ]
+    *attention_grad, small = call(
+        kernel(split_kernel, dp_count - 1, blk_count, True),
+        [struct(COLUMNS, LANES, f32)]
+        + [struct(COLUMNS, LANES, bf16)] * (blk_count - 1)
+        + [struct(plane_count * SMALL, LANES, f32)],
+        [SMEM] + [VMEM] * dp_count,
+        [spots] + attention_grad,
+        [pltpu.VMEM((COLUMNS + small_deep, cut), f32)],
+    )
+    joint_grad, output_grad = call(
+        kernel(attend_final_kernel, blk_count),
+        [struct(LANES, blk_count * QKV, f32), struct(blk_count * PAIR, LANES, f32)],
+        [SMEM] + [VMEM] * blk_count,
+        [spots] + exchange_blk(attention_grad),
+    )
+    for bit in reversed(bits):
+        small = small[: bit * SMALL] + swap(small[bit * SMALL :], PLANE, plane_count, bit)
+    pair_rows, pair_columns = joint_bias.shape
+    return (
+        layer_output,
+        input_grad,
+        small[0, :piece],
+        small[1, :piece],
+        joint_grad,
+        small[6 : 6 + pair_rows, :pair_columns],
+        output_grad,
+        small[2, :piece],
+        small[3, :piece],
+        small[4, :piece],
+        expand_grad,
+        small[6 + pair_rows : 7 + pair_rows],
+        reduce_grad,
+        small[5, :piece],
+    )
+
+
+def local_any(*arrays):
+    dp_count, seq_count, blk_count = (lax.axis_size(axis) for axis in ALL)
+    own_width = arrays[0].shape[1] // (dp_count * blk_count)
+    if H == 2 * seq_count * blk_count and own_width == LANES and blk_count == 2:
+        return local_heads(*arrays)
+    return local(*arrays)
+
+
 def solution(mesh):
     return jax.shard_map(
-        local,
+        local_heads if H == 2 * mesh.shape["seq"] * mesh.shape["blk"] else local,
         mesh=mesh,
         in_specs=(
             P(("dp", "seq", "blk"), None),

time: 982 us -> 263 us (0.27)
  waiting for transfers between devices: 549 us -> 109 us
  blocking collectives: 151 us -> 0 us
  local copies, waits for them, and re-layouts: 171 us -> 28.8 us
  starting transfers between devices: 1.03 us -> 60.3 us
  matrix products: 55 us -> 0 us
  Pallas kernels: 0 us -> 45.4 us
  other arithmetic: 29.8 us -> 0.11 us
    unnamed x24 -> x2, waiting for transfers between devices: 200 us -> 0.03 us
    reduce_scatter x6 -> x1, waiting for transfers between devices: 181 us -> 0.01 us  [local_heads(): lax.psum_scatter(forward_grad, 'dp', scatter_dimension=0, tiled=False)]
    all_gather x8 -> x1, waiting for transfers between devices: 168 us -> 0.01 us  [local_heads(): forward_weights = lax.all_gather(forward_block, 'dp', axis=0, tiled=False)]
    unnamed x79 -> x128, local copies, waits for them, and re-layouts: 164 us -> 27.2 us
    ppermute x0 -> x60, waiting for transfers between devices: none -> 109 us  [swap(): return lax.ppermute(value, axes, [(i, i ^ offset) for i in range(count)])]
    unnamed x2 -> x0, blocking collectives: 82.1 us -> none
    all_gather x3 -> x0, blocking collectives: 69.1 us -> none  [the longest x1 28 us: local(): lax.all_gather(output_weight, ('dp', 'blk'), axis=1, tiled=True)]
    ppermute x0 -> x60, starting transfers between devices: none -> 60.2 us  [swap(): return lax.ppermute(value, axes, [(i, i ^ offset) for i in range(count)])]
  transfers between devices with their start and end apart: 19 -> 62, of which waited for: 17 -> 30; matrix products, arithmetic and copies ran while one was open for 11% -> 1% of each run, Pallas kernels for 0% -> 12%
where the time goes in v1:
time: 263 us; the launch traced here: 259 us
  waiting for transfers between devices  109 us (41%)
  starting transfers between devices  60.3 us (23%)
  Pallas kernels  45.4 us (17%)
  local copies, waits for them, and re-layouts  28.8 us (11%)
  between operations  14.7 us (6%)
    ppermute x60, waiting for transfers between devices, swap(): return lax.ppermute(value, axes, [(i, i ^ offset) for i in range(count)])  109 us
    ppermute x60, starting transfers between devices, swap(): return lax.ppermute(value, axes, [(i, i ^ offset) for i in range(count)])  60.2 us
    pallas_call x23, Pallas kernels, call(): pl.pallas_call(kernel, out_shape=outs, in_specs=specs, out_specs=[VMEM] *...  45.4 us
    unnamed x128, local copies, waits for them, and re-layouts  27.2 us
  transfers between devices with their start and end apart: 62, of which 30 were waited for; matrix products, arithmetic and copies ran while one was open for 1% of the time, Pallas kernels for 12%

profile of v1, /device:TPU:0, one launch (start us, length us, event | category | flops | bytes accessed | tf_op | source)
XLA Modules:
  0.0 258.7 jit_solution(10571119327931555427)
XLA Ops:
  16.0 3.0 %collective-permute-start.1 = (bf16[16,128]{1,0:T(8,128)(2,1)S(1)}, bf16[16,128]{1,0:T(8,128)(2,1)S(1)}, u32[]{:S(2)}, u32[]{:S(2)}) collective-permute-start(bf16[16,128]{1,0:T(8,128)(2,1)S(1)} %get-tuple-element.77), channel_id=1, source_target_pairs={{0,1},{1,0},{2,3},{3,2},{4,5},{5,4},{6,7},{7,6},{8,9},{9,8},{10,11... | collective-permute-start | bytes 12296 | tf_op jit(solution)/shard_map/ppermute | solution.py:352
  28.3 3.7 %collective-permute-start.6 = (bf16[576,256]{1,0:T(8,128)(2,1)S(1)}, bf16[576,256]{1,0:T(8,128)(2,1)S(1)}, u32[]{:S(2)}, u32[]{:S(2)}) collective-permute-start(bf16[576,256]{1,0:T(8,128)(2,1)S(1)} %shard_map.246.refs_0_.refs_3_), channel_id=1, source_target_pairs={{0,24},{8,16},{16,8},{24,0},{1,25},{9,17},{17,9},{25,1},{2,26},{10... | collective-permute-start | bytes 884744 | tf_op jit(solution)/shard_map/ppermute | solution.py:352
  35.5 3.1 %collective-permute-done.8.refs_2_ = bf16[128,1024]{1,0:T(8,128)(2,1)S(1)} collective-permute-done((bf16[128,1024]{1,0:T(8,128)(2,1)S(1)}, bf16[128,1024]{1,0:T(8,128)(2,1)S(1)}, u32[]{:S(2)}, u32[]{:S(2)}) %collective-permute-start.8) | collective-permute-done | bytes 262176 | tf_op jit(solution)/shard_map/ppermute | solution.py:352
  40.1 4.3 %collective-permute-done.32.refs_1_ = bf16[1024,128]{1,0:T(8,128)(2,1)S(1)} collective-permute-done((bf16[1024,128]{1,0:T(8,128)(2,1)S(1)}, bf16[1024,128]{1,0:T(8,128)(2,1)S(1)}, u32[]{:S(2)}, u32[]{:S(2)}) %collective-permute-start.32) | collective-permute-done | bytes 262176 | tf_op jit(solution)/shard_map/ppermute | solution.py:352
  45.0 11.4 %collective-permute-done.5.refs_2_ = bf16[576,256]{1,0:T(8,128)(2,1)S(1)} collective-permute-done((bf16[576,256]{1,0:T(8,128)(2,1)S(1)}, bf16[576,256]{1,0:T(8,128)(2,1)S(1)}, u32[]{:S(2)}, u32[]{:S(2)}) %collective-permute-start.5) | collective-permute-done | bytes 294944 | tf_op jit(solution)/shard_map/ppermute | solution.py:352
  59.8 2.9 %shard_map.247.refs_4_.refs_8_ = f32[1024,1024]{1,0:T(8,128)S(1)} custom-call(s32[4]{0:T(128)S(1)} %pad_add_fusion.spots, bf16[128,1024]{1,0:T(8,128)(2,1)S(1)} %get-tuple-element.78.refs_0_.refs_3_.refs_4_, bf16[128,1024]{1,0:T(8,128)(2,1)S(1)} %collective-permute-done.7.refs_1_, bf16[128,1024]{1,0:T(8,128)(2,1)S(1)} %collective-permute-done.8.refs_2_, ...), custom_call_target="tpu_custom_call" | custom-call | flops 2200000000 | tf_op jit(solution)/shard_map/pallas_call | solution.py:385
  62.7 6.6 %shard_map.249 = (bf16[1024,384]{1,0:T(8,128)(2,1)S(1)}, f32[1024,128]{1,0:T(8,128)S(1)}, f32[1024,128]{1,0:T(8,128)S(1)}, bf16[512,1024]{1,0:T(8,128)(2,1)S(1)}...) custom-call(s32[4]{0:T(128)S(1)} %pad_add_fusion.spots, f32[2]{0:T(128)S(1)} %multiply_exponential_fusion.slope_ref, ...), custom_call_target="tpu_custom_call" | custom-call | flops 11000000512 | tf_op jit(solution)/shard_map/pallas_call | solution.py:385
  72.6 7.4 %collective-permute-start.27 = (bf16[128,1024]{1,0:T(8,128)(2,1)S(1)}, bf16[128,1024]{1,0:T(8,128)(2,1)S(1)}, u32[]{:S(2)}, u32[]{:S(2)}) collective-permute-start(bf16[128,1024]{1,0:T(8,128)(2,1)S(1)} %get-tuple-element.88.refs_8_.refs_4_), channel_id=1, source_target_pairs={{0,5},{1,4},{2,7},{3,6},{4,1},{5,0},{6,3},{7,2},{8,13},{9,12},{10,... | collective-permute-start | bytes 786440 | tf_op jit(solution)/shard_map/ppermute | solution.py:352
  80.8 2.3 collective-permute-start.16
  83.7 3.4 %collective-permute-done.27.refs_11_ = bf16[128,1024]{1,0:T(8,128)(2,1)S(1)} collective-permute-done((bf16[128,1024]{1,0:T(8,128)(2,1)S(1)}, bf16[128,1024]{1,0:T(8,128)(2,1)S(1)}, u32[]{:S(2)}, u32[]{:S(2)}) %collective-permute-start.27) | collective-permute-done | bytes 262176 | tf_op jit(solution)/shard_map/ppermute | solution.py:352
  87.1 5.2 %collective-permute-done.26.refs_10_ = bf16[128,1024]{1,0:T(8,128)(2,1)S(1)} collective-permute-done((bf16[128,1024]{1,0:T(8,128)(2,1)S(1)}, bf16[128,1024]{1,0:T(8,128)(2,1)S(1)}, u32[]{:S(2)}, u32[]{:S(2)}) %collective-permute-start.26) | collective-permute-done | bytes 262176 | tf_op jit(solution)/shard_map/ppermute | solution.py:352
  93.3 4.6 %collective-permute-done.16.refs_1_ = bf16[128,1024]{1,0:T(8,128)(2,1)S(1)} collective-permute-done((bf16[128,1024]{1,0:T(8,128)(2,1)S(1)}, bf16[128,1024]{1,0:T(8,128)(2,1)S(1)}, u32[]{:S(2)}, u32[]{:S(2)}) %collective-permute-start.16) | collective-permute-done | bytes 262176 | tf_op jit(solution)/shard_map/ppermute | solution.py:352
  97.9 5.5 %collective-permute-done.17.refs_2_ = bf16[128,1024]{1,0:T(8,128)(2,1)S(1)} collective-permute-done((bf16[128,1024]{1,0:T(8,128)(2,1)S(1)}, bf16[128,1024]{1,0:T(8,128)(2,1)S(1)}, u32[]{:S(2)}, u32[]{:S(2)}) %collective-permute-start.17) | collective-permute-done | bytes 262176 | tf_op jit(solution)/shard_map/ppermute | solution.py:352
  104.6 2.6 %collective-permute-start.20 = (bf16[128,1024]{1,0:T(8,128)(2,1)S(1)}, bf16[128,1024]{1,0:T(8,128)(2,1)S(1)}, u32[]{:S(2)}, u32[]{:S(2)}) collective-permute-start(bf16[128,1024]{1,0:T(8,128)(2,1)S(1)} %get-tuple-element.87.refs_0_), channel_id=1, source_target_pairs={{0,5},{1,4},{2,7},{3,6},{4,1},{5,0},{6,3},{7,2},{8,13},{9,12},{10,... | collective-permute-start | bytes 786440 | tf_op jit(solution)/shard_map/ppermute | solution.py:352
  108.6 2.5 collective-permute-start.18
  111.6 3.1 %collective-permute-done.20.refs_3_ = bf16[128,1024]{1,0:T(8,128)(2,1)S(1)} collective-permute-done((bf16[128,1024]{1,0:T(8,128)(2,1)S(1)}, bf16[128,1024]{1,0:T(8,128)(2,1)S(1)}, u32[]{:S(2)}, u32[]{:S(2)}) %collective-permute-start.20) | collective-permute-done | bytes 262176 | tf_op jit(solution)/shard_map/ppermute | solution.py:352
  114.7 3.1 %collective-permute-done.19.refs_2_ = bf16[128,1024]{1,0:T(8,128)(2,1)S(1)} collective-permute-done((bf16[128,1024]{1,0:T(8,128)(2,1)S(1)}, bf16[128,1024]{1,0:T(8,128)(2,1)S(1)}, u32[]{:S(2)}, u32[]{:S(2)}) %collective-permute-start.19) | collective-permute-done | bytes 262176 | tf_op jit(solution)/shard_map/ppermute | solution.py:352
  127.2 6.0 %shard_map.254 = (bf16[1024,512]{1,0:T(8,128)(2,1)S(1)}, bf16[1024,512]{1,0:T(8,128)(2,1)S(1)}, f32[512,1024]{1,0:T(8,128)S(1)}, bf16[512,1024]{1,0:T(8,128)(2,1)S(1)}, f32[8,512]{1,0:T(8,128)S(1)}) custom-call(s32[4]{0:T(128)S(1)} %pad_add_fusion.spots, bf16[128,1024]{1,0:T(8,128)(2,1)S(1)} %get-tuple-element.87.refs_0_, ...), custom_call_target="tpu_custom_call" | custom-call | flops 8800000000 | tf_op jit(solution)/shard_map/pallas_call | solution.py:385
  138.5 5.4 %shard_map.256 = (bf16[4,1024,256]{2,1,0:T(8,128)(2,1)}, f32[512,1024]{1,0:T(8,128)S(1)}, bf16[512,1024]{1,0:T(8,128)(2,1)S(1)}) custom-call(s32[4]{0:T(128)S(1)} %pad_add_fusion.spots, bf16[128,1024]{1,0:T(8,128)(2,1)S(1)} %copy-done.10, bf16[128,1024]{1,0:T(8,128)(2,1)S(1)} %copy-done.16, bf16[128,1024]{1,0:T(8,128)(2,1)S(1)} %copy-done.14, ...), custom_call_target="tpu_custom_call" | custom-call | flops 8800000000 | tf_op jit(solution)/shard_map/pallas_call | solution.py:385
  149.3 5.1 %collective-permute-done.35.refs_0_ = bf16[128,1024]{1,0:T(8,128)(2,1)S(1)} collective-permute-done((bf16[128,1024]{1,0:T(8,128)(2,1)}, bf16[128,1024]{1,0:T(8,128)(2,1)S(1)}, u32[]{:S(2)}, u32[]{:S(2)}) %collective-permute-start.35) | collective-permute-done | bytes 262176 | tf_op jit(solution)/shard_map/ppermute | solution.py:352
  156.0 5.2 %collective-permute-done.37.refs_2_ = bf16[128,1024]{1,0:T(8,128)(2,1)S(1)} collective-permute-done((bf16[128,1024]{1,0:T(8,128)(2,1)S(1)}, bf16[128,1024]{1,0:T(8,128)(2,1)S(1)}, u32[]{:S(2)}, u32[]{:S(2)}) %collective-permute-start.37) | collective-permute-done | bytes 262176 | tf_op jit(solution)/shard_map/ppermute | solution.py:352
  163.0 2.3 collective-permute-start.38
  166.6 6.7 %collective-permute-done.38.refs_3_ = bf16[128,1024]{1,0:T(8,128)(2,1)S(1)} collective-permute-done((bf16[128,1024]{1,0:T(8,128)(2,1)S(1)}, bf16[128,1024]{1,0:T(8,128)(2,1)S(1)}, u32[]{:S(2)}, u32[]{:S(2)}) %collective-permute-start.38) | collective-permute-done | bytes 262176 | tf_op jit(solution)/shard_map/ppermute | solution.py:352
  173.8 3.1 %collective-permute-done.44.refs_2_ = bf16[128,1024]{1,0:T(8,128)(2,1)S(1)} collective-permute-done((bf16[128,1024]{1,0:T(8,128)(2,1)S(1)}, bf16[128,1024]{1,0:T(8,128)(2,1)S(1)}, u32[]{:S(2)}, u32[]{:S(2)}) %collective-permute-start.44) | collective-permute-done | bytes 262176 | tf_op jit(solution)/shard_map/ppermute | solution.py:352
  178.8 8.0 %shard_map.260 = (bf16[1024,384]{1,0:T(8,128)(2,1)S(1)}, f32[512,1024]{1,0:T(8,128)S(1)}, bf16[512,1024]{1,0:T(8,128)(2,1)S(1)}) custom-call(s32[4]{0:T(128)S(1)} %pad_add_fusion.spots, f32[2]{0:T(128)S(1)} %multiply_exponential_fusion.slope_ref, bf16[128,1024]{1,0:T(8,128)(2,1)S(1)} %get-tuple-element.103.refs_0_, ...), custom_call_target="tpu_custom_call" | custom-call | flops 11000000512 | tf_op jit(solution)/shard_map/pallas_call | solution.py:385
  186.8 2.6 %shard_map.263 = (f32[576,256]{1,0:T(8,128)S(1)}, bf16[576,256]{1,0:T(8,128)(2,1)S(1)}, bf16[576,256]{1,0:T(8,128)(2,1)S(1)}, bf16[576,256]{1,0:T(8,128)(2,1)S(1)}) custom-call(s32[4]{0:T(128)S(1)} %pad_add_fusion.spots, bf16[128,1024]{1,0:T(8,128)(2,1)S(1)} %get-tuple-element.103.refs_0_, bf16[128,1024]{1,0:T(8,128)(2,1)S(1)} %collective-permute-done.43.refs_1_, ...), custom_call_target="tpu_custom_call" | custom-call | flops 8800000000 | tf_op jit(solution)/shard_map/pallas_call | solution.py:385
  189.6 2.9 %collective-permute-start.53 = (bf16[576,256]{1,0:T(8,128)(2,1)S(1)}, bf16[576,256]{1,0:T(8,128)(2,1)S(1)}, u32[]{:S(2)}, u32[]{:S(2)}) collective-permute-start(bf16[576,256]{1,0:T(8,128)(2,1)S(1)} %get-tuple-element.124), channel_id=1, source_target_pairs={{0,16},{8,24},{16,0},{24,8},{1,17},{9,25},{17,1},{25,9},{2,18},{10... | collective-permute-start | bytes 884744 | tf_op jit(solution)/shard_map/ppermute | solution.py:352
  193.9 10.4 %collective-permute-done.52.refs_0_ = bf16[576,256]{1,0:T(8,128)(2,1)S(1)} collective-permute-done((bf16[576,256]{1,0:T(8,128)(2,1)S(1)}, bf16[576,256]{1,0:T(8,128)(2,1)S(1)}, u32[]{:S(2)}, u32[]{:S(2)}) %collective-permute-start.52) | collective-permute-done | bytes 294944 | tf_op jit(solution)/shard_map/ppermute | solution.py:352
  204.4 8.7 %collective-permute-done.53.refs_1_ = bf16[576,256]{1,0:T(8,128)(2,1)S(1)} collective-permute-done((bf16[576,256]{1,0:T(8,128)(2,1)S(1)}, bf16[576,256]{1,0:T(8,128)(2,1)S(1)}, u32[]{:S(2)}, u32[]{:S(2)}) %collective-permute-start.53) | collective-permute-done | bytes 294944 | tf_op jit(solution)/shard_map/ppermute | solution.py:352
  223.1 2.6 collective-permute-done.41.refs_1_
  225.7 3.4 %collective-permute-done.42.refs_2_ = bf16[128,1024]{1,0:T(8,128)(2,1)S(1)} collective-permute-done((bf16[128,1024]{1,0:T(8,128)(2,1)S(1)}, bf16[128,1024]{1,0:T(8,128)(2,1)S(1)}, u32[]{:S(2)}, u32[]{:S(2)}) %collective-permute-start.42) | collective-permute-done | bytes 262176 | tf_op jit(solution)/shard_map/ppermute | solution.py:352
  241.3 6.1 %collective-permute-done.49.refs_0_ = bf16[128,1024]{1,0:T(8,128)(2,1)S(1)} collective-permute-done((bf16[128,1024]{1,0:T(8,128)(2,1)S(1)}, bf16[128,1024]{1,0:T(8,128)(2,1)S(1)}, u32[]{:S(2)}, u32[]{:S(2)}) %collective-permute-start.49) | collective-permute-done | bytes 262176 | tf_op jit(solution)/shard_map/ppermute | solution.py:352
  (259 shorter events, 90.7 us)
Async XLA Ops:
  7.2 114.6 %all-gather.3.cloned.1.call-start = ((), (), s32[]{:S(2)}) async-start(), calls=%async_computation.2 | async-start | bytes 2621440 | tf_op jit(solution)/shard_map/all_gather | solution.py:977
  25.3 13.2 %collective-permute-start.8 = (bf16[128,1024]{1,0:T(8,128)(2,1)S(1)}, bf16[128,1024]{1,0:T(8,128)(2,1)S(1)}, u32[]{:S(2)}, u32[]{:S(2)}) collective-permute-start(bf16[128,1024]{1,0:T(8,128)(2,1)S(1)} %get-tuple-element.78.refs_0_.refs_3_.refs_4_), channel_id=1, source_target_pairs={{0,4},{1,5},{2,6},{3,7},{4,0},{5,1},{6,2},{7,3},{8,12},{9,13},{10,... | collective-permute-start | bytes 786440 | tf_op jit(solution)/shard_map/ppermute | solution.py:352
  26.8 13.3 %collective-permute-start.7 = (bf16[128,1024]{1,0:T(8,128)(2,1)S(1)}, bf16[128,1024]{1,0:T(8,128)(2,1)S(1)}, u32[]{:S(2)}, u32[]{:S(2)}) collective-permute-start(bf16[128,1024]{1,0:T(8,128)(2,1)S(1)} %get-tuple-element.78.refs_0_.refs_3_.refs_4_), channel_id=1, source_target_pairs={{0,1},{1,0},{2,3},{3,2},{4,5},{5,4},{6,7},{7,6},{8,9},{9,8},{10,11... | collective-permute-start | bytes 786440 | tf_op jit(solution)/shard_map/ppermute | solution.py:352
  28.3 16.2 %collective-permute-start.6 = (bf16[576,256]{1,0:T(8,128)(2,1)S(1)}, bf16[576,256]{1,0:T(8,128)(2,1)S(1)}, u32[]{:S(2)}, u32[]{:S(2)}) collective-permute-start(bf16[576,256]{1,0:T(8,128)(2,1)S(1)} %shard_map.246.refs_0_.refs_3_), channel_id=1, source_target_pairs={{0,24},{8,16},{16,8},{24,0},{1,25},{9,17},{17,9},{25,1},{2,26},{10... | collective-permute-start | bytes 884744 | tf_op jit(solution)/shard_map/ppermute | solution.py:352
  32.0 24.4 %collective-permute-start.5 = (bf16[576,256]{1,0:T(8,128)(2,1)S(1)}, bf16[576,256]{1,0:T(8,128)(2,1)S(1)}, u32[]{:S(2)}, u32[]{:S(2)}) collective-permute-start(bf16[576,256]{1,0:T(8,128)(2,1)S(1)} %shard_map.246.refs_0_.refs_3_), channel_id=1, source_target_pairs={{0,16},{8,24},{16,0},{24,8},{1,17},{9,25},{17,1},{25,9},{2,18},{10... | collective-permute-start | bytes 884744 | tf_op jit(solution)/shard_map/ppermute | solution.py:352
  38.5 20.3 %collective-permute-start.4 = (bf16[576,256]{1,0:T(8,128)(2,1)S(1)}, bf16[576,256]{1,0:T(8,128)(2,1)S(1)}, u32[]{:S(2)}, u32[]{:S(2)}) collective-permute-start(bf16[576,256]{1,0:T(8,128)(2,1)S(1)} %shard_map.246.refs_0_.refs_3_), channel_id=1, source_target_pairs={{0,8},{8,0},{16,24},{24,16},{1,9},{9,1},{17,25},{25,17},{2,10},{10... | collective-permute-start | bytes 884744 | tf_op jit(solution)/shard_map/ppermute | solution.py:352
  40.1 19.7 %collective-permute-start.10 = (bf16[128,1024]{1,0:T(8,128)(2,1)S(1)}, bf16[128,1024]{1,0:T(8,128)(2,1)S(1)}, u32[]{:S(2)}, u32[]{:S(2)}) collective-permute-start(bf16[128,1024]{1,0:T(8,128)(2,1)S(1)} %get-tuple-element.78.refs_0_.refs_3_.refs_4_), channel_id=1, source_target_pairs={{0,2},{1,3},{2,0},{3,1},{4,6},{5,7},{6,4},{7,5},{8,10},{9,11},{10,... | collective-permute-start | bytes 786440 | tf_op jit(solution)/shard_map/ppermute | solution.py:352
  44.5 15.3 %collective-permute-start.13 = (bf16[128,1024]{1,0:T(8,128)(2,1)S(1)}, bf16[128,1024]{1,0:T(8,128)(2,1)S(1)}, u32[]{:S(2)}, u32[]{:S(2)}) collective-permute-start(bf16[128,1024]{1,0:T(8,128)(2,1)S(1)} %collective-permute-done.9.refs_3_), channel_id=1, source_target_pairs={{0,2},{1,3},{2,0},{3,1},{4,6},{5,7},{6,4},{7,5},{8,10},{9,11},{10,... | collective-permute-start | bytes 786440 | tf_op jit(solution)/shard_map/ppermute | solution.py:352
  44.5 15.3 %collective-permute-start.12 = (bf16[128,1024]{1,0:T(8,128)(2,1)S(1)}, bf16[128,1024]{1,0:T(8,128)(2,1)S(1)}, u32[]{:S(2)}, u32[]{:S(2)}) collective-permute-start(bf16[128,1024]{1,0:T(8,128)(2,1)S(1)} %collective-permute-done.8.refs_2_), channel_id=1, source_target_pairs={{0,2},{1,3},{2,0},{3,1},{4,6},{5,7},{6,4},{7,5},{8,10},{9,11},{10,... | collective-permute-start | bytes 786440 | tf_op jit(solution)/shard_map/ppermute | solution.py:352
  58.8 176.5 %reduce-scatter.2.cloned.1.call-start = ((), (), s32[]{:S(2)}) async-start(), calls=%async_computation.1 | async-start | bytes 2621440 | tf_op jit(solution)/shard_map/reduce_scatter | solution.py:1047
  72.6 14.5 %collective-permute-start.27 = (bf16[128,1024]{1,0:T(8,128)(2,1)S(1)}, bf16[128,1024]{1,0:T(8,128)(2,1)S(1)}, u32[]{:S(2)}, u32[]{:S(2)}) collective-permute-start(bf16[128,1024]{1,0:T(8,128)(2,1)S(1)} %get-tuple-element.88.refs_8_.refs_4_), channel_id=1, source_target_pairs={{0,5},{1,4},{2,7},{3,6},{4,1},{5,0},{6,3},{7,2},{8,13},{9,12},{10,... | collective-permute-start | bytes 786440 | tf_op jit(solution)/shard_map/ppermute | solution.py:352
  79.9 12.4 %collective-permute-start.26 = (bf16[128,1024]{1,0:T(8,128)(2,1)S(1)}, bf16[128,1024]{1,0:T(8,128)(2,1)S(1)}, u32[]{:S(2)}, u32[]{:S(2)}) collective-permute-start(bf16[128,1024]{1,0:T(8,128)(2,1)S(1)} %get-tuple-element.88.refs_8_.refs_4_), channel_id=1, source_target_pairs={{0,4},{1,5},{2,6},{3,7},{4,0},{5,1},{6,2},{7,3},{8,12},{9,13},{10,... | collective-permute-start | bytes 786440 | tf_op jit(solution)/shard_map/ppermute | solution.py:352
  80.1 13.1 %collective-permute-start.15 = (bf16[128,1024]{1,0:T(8,128)(2,1)S(1)}, bf16[128,1024]{1,0:T(8,128)(2,1)S(1)}, u32[]{:S(2)}, u32[]{:S(2)}) collective-permute-start(bf16[128,1024]{1,0:T(8,128)(2,1)S(1)} %get-tuple-element.84), channel_id=1, source_target_pairs={{0,1},{1,0},{2,3},{3,2},{4,5},{5,4},{6,7},{7,6},{8,9},{9,8},{10,11... | collective-permute-start | bytes 786440 | tf_op jit(solution)/shard_map/ppermute | solution.py:352
  80.8 17.1 %collective-permute-start.16 = (bf16[128,1024]{1,0:T(8,128)(2,1)S(1)}, bf16[128,1024]{1,0:T(8,128)(2,1)S(1)}, u32[]{:S(2)}, u32[]{:S(2)}) collective-permute-start(bf16[128,1024]{1,0:T(8,128)(2,1)S(1)} %get-tuple-element.85), channel_id=1, source_target_pairs={{0,4},{1,5},{2,6},{3,7},{4,0},{5,1},{6,2},{7,3},{8,12},{9,13},{10,... | collective-permute-start | bytes 786440 | tf_op jit(solution)/shard_map/ppermute | solution.py:352
  83.1 20.4 %collective-permute-start.17 = (bf16[128,1024]{1,0:T(8,128)(2,1)S(1)}, bf16[128,1024]{1,0:T(8,128)(2,1)S(1)}, u32[]{:S(2)}, u32[]{:S(2)}) collective-permute-start(bf16[128,1024]{1,0:T(8,128)(2,1)S(1)} %get-tuple-element.86), channel_id=1, source_target_pairs={{0,5},{1,4},{2,7},{3,6},{4,1},{5,0},{6,3},{7,2},{8,13},{9,12},{10,... | collective-permute-start | bytes 786440 | tf_op jit(solution)/shard_map/ppermute | solution.py:352
  87.1 20.1 %collective-permute-start.28 = (bf16[128,1024]{1,0:T(8,128)(2,1)S(1)}, bf16[128,1024]{1,0:T(8,128)(2,1)S(1)}, u32[]{:S(2)}, u32[]{:S(2)}) collective-permute-start(bf16[128,1024]{1,0:T(8,128)(2,1)S(1)} %get-tuple-element.88.refs_8_.refs_4_), channel_id=1, source_target_pairs={{0,2},{1,3},{2,0},{3,1},{4,6},{5,7},{6,4},{7,5},{8,10},{9,11},{10,... | collective-permute-start | bytes 786440 | tf_op jit(solution)/shard_map/ppermute | solution.py:352
  92.3 16.3 %collective-permute-start.25 = (bf16[128,1024]{1,0:T(8,128)(2,1)S(1)}, bf16[128,1024]{1,0:T(8,128)(2,1)S(1)}, u32[]{:S(2)}, u32[]{:S(2)}) collective-permute-start(bf16[128,1024]{1,0:T(8,128)(2,1)S(1)} %get-tuple-element.88.refs_8_.refs_4_), channel_id=1, source_target_pairs={{0,1},{1,0},{2,3},{3,2},{4,5},{5,4},{6,7},{7,6},{8,9},{9,8},{10,11... | collective-permute-start | bytes 786440 | tf_op jit(solution)/shard_map/ppermute | solution.py:352
  93.3 17.8 %collective-permute-start.31 = (bf16[128,1024]{1,0:T(8,128)(2,1)S(1)}, bf16[128,1024]{1,0:T(8,128)(2,1)S(1)}, u32[]{:S(2)}, u32[]{:S(2)}) collective-permute-start(bf16[128,1024]{1,0:T(8,128)(2,1)S(1)} %collective-permute-done.27.refs_11_), channel_id=1, source_target_pairs={{0,2},{1,3},{2,0},{3,1},{4,6},{5,7},{6,4},{7,5},{8,10},{9,11},{10,... | collective-permute-start | bytes 786440 | tf_op jit(solution)/shard_map/ppermute | solution.py:352
  97.9 13.2 %collective-permute-start.30 = (bf16[128,1024]{1,0:T(8,128)(2,1)S(1)}, bf16[128,1024]{1,0:T(8,128)(2,1)S(1)}, u32[]{:S(2)}, u32[]{:S(2)}) collective-permute-start(bf16[128,1024]{1,0:T(8,128)(2,1)S(1)} %collective-permute-done.26.refs_10_), channel_id=1, source_target_pairs={{0,2},{1,3},{2,0},{3,1},{4,6},{5,7},{6,4},{7,5},{8,10},{9,11},{10,... | collective-permute-start | bytes 786440 | tf_op jit(solution)/shard_map/ppermute | solution.py:352
  145.3 32.0 %collective-permute-start.34 = (bf16[512,1024]{1,0:T(8,128)(2,1)S(1)}, bf16[512,1024]{1,0:T(8,128)(2,1)S(1)}, u32[]{:S(2)}, u32[]{:S(2)}) collective-permute-start(bf16[512,1024]{1,0:T(8,128)(2,1)S(1)} %get-tuple-element.98), channel_id=1, source_target_pairs={{0,2},{1,3},{2,0},{3,1},{4,6},{5,7},{6,4},{7,5},{8,10},{9,11},{10,... | collective-permute-start | bytes 3145736 | tf_op jit(solution)/shard_map/ppermute | solution.py:352
  148.7 12.6 %collective-permute-start.37 = (bf16[128,1024]{1,0:T(8,128)(2,1)S(1)}, bf16[128,1024]{1,0:T(8,128)(2,1)S(1)}, u32[]{:S(2)}, u32[]{:S(2)}) collective-permute-start(bf16[128,1024]{1,0:T(8,128)(2,1)S(1)} %copy-done.32), channel_id=1, source_target_pairs={{0,5},{1,4},{2,7},{3,6},{4,1},{5,0},{6,3},{7,2},{8,13},{9,12},{10,... | collective-permute-start | bytes 786440 | tf_op jit(solution)/shard_map/ppermute | solution.py:352
  165.3 11.5 %collective-permute-start.44 = (bf16[128,1024]{1,0:T(8,128)(2,1)S(1)}, bf16[128,1024]{1,0:T(8,128)(2,1)S(1)}, u32[]{:S(2)}, u32[]{:S(2)}) collective-permute-start(bf16[128,1024]{1,0:T(8,128)(2,1)S(1)} %get-tuple-element.103.refs_0_), channel_id=1, source_target_pairs={{0,4},{1,5},{2,6},{3,7},{4,0},{5,1},{6,2},{7,3},{8,12},{9,13},{10,... | collective-permute-start | bytes 786440 | tf_op jit(solution)/shard_map/ppermute | solution.py:352
  165.6 11.4 %collective-permute-start.43 = (bf16[128,1024]{1,0:T(8,128)(2,1)S(1)}, bf16[128,1024]{1,0:T(8,128)(2,1)S(1)}, u32[]{:S(2)}, u32[]{:S(2)}) collective-permute-start(bf16[128,1024]{1,0:T(8,128)(2,1)S(1)} %get-tuple-element.103.refs_0_), channel_id=1, source_target_pairs={{0,1},{1,0},{2,3},{3,2},{4,5},{5,4},{6,7},{7,6},{8,9},{9,8},{10,11... | collective-permute-start | bytes 786440 | tf_op jit(solution)/shard_map/ppermute | solution.py:352
  189.5 14.9 %collective-permute-start.52 = (bf16[576,256]{1,0:T(8,128)(2,1)S(1)}, bf16[576,256]{1,0:T(8,128)(2,1)S(1)}, u32[]{:S(2)}, u32[]{:S(2)}) collective-permute-start(bf16[576,256]{1,0:T(8,128)(2,1)S(1)} %get-tuple-element.123), channel_id=1, source_target_pairs={{0,8},{8,0},{16,24},{24,16},{1,9},{9,1},{17,25},{25,17},{2,10},{10... | collective-permute-start | bytes 884744 | tf_op jit(solution)/shard_map/ppermute | solution.py:352
  189.6 23.5 %collective-permute-start.53 = (bf16[576,256]{1,0:T(8,128)(2,1)S(1)}, bf16[576,256]{1,0:T(8,128)(2,1)S(1)}, u32[]{:S(2)}, u32[]{:S(2)}) collective-permute-start(bf16[576,256]{1,0:T(8,128)(2,1)S(1)} %get-tuple-element.124), channel_id=1, source_target_pairs={{0,16},{8,24},{16,0},{24,8},{1,17},{9,25},{17,1},{25,9},{2,18},{10... | collective-permute-start | bytes 884744 | tf_op jit(solution)/shard_map/ppermute | solution.py:352
  192.5 20.6 %collective-permute-start.54 = (bf16[576,256]{1,0:T(8,128)(2,1)S(1)}, bf16[576,256]{1,0:T(8,128)(2,1)S(1)}, u32[]{:S(2)}, u32[]{:S(2)}) collective-permute-start(bf16[576,256]{1,0:T(8,128)(2,1)S(1)} %get-tuple-element.125), channel_id=1, source_target_pairs={{0,24},{8,16},{16,8},{24,0},{1,25},{9,17},{17,9},{25,1},{2,26},{10... | collective-permute-start | bytes 884744 | tf_op jit(solution)/shard_map/ppermute | solution.py:352
  193.9 37.6 %collective-permute-start.48 = (bf16[512,1024]{1,0:T(8,128)(2,1)S(1)}, bf16[512,1024]{1,0:T(8,128)(2,1)S(1)}, u32[]{:S(2)}, u32[]{:S(2)}) collective-permute-start(bf16[512,1024]{1,0:T(8,128)(2,1)S(1)} %get-tuple-element.113), channel_id=1, source_target_pairs={{0,2},{1,3},{2,0},{3,1},{4,6},{5,7},{6,4},{7,5},{8,10},{9,11},{10,... | collective-permute-start | bytes 3145736 | tf_op jit(solution)/shard_map/ppermute | solution.py:352
  217.0 12.1 %collective-permute-start.42 = (bf16[128,1024]{1,0:T(8,128)(2,1)S(1)}, bf16[128,1024]{1,0:T(8,128)(2,1)S(1)}, u32[]{:S(2)}, u32[]{:S(2)}) collective-permute-start(bf16[128,1024]{1,0:T(8,128)(2,1)S(1)} %get-tuple-element.107), channel_id=1, source_target_pairs={{0,5},{1,4},{2,7},{3,6},{4,1},{5,0},{6,3},{7,2},{8,13},{9,12},{10,... | collective-permute-start | bytes 786440 | tf_op jit(solution)/shard_map/ppermute | solution.py:352
  231.8 15.6 %collective-permute-start.49 = (bf16[128,1024]{1,0:T(8,128)(2,1)S(1)}, bf16[128,1024]{1,0:T(8,128)(2,1)S(1)}, u32[]{:S(2)}, u32[]{:S(2)}) collective-permute-start(bf16[128,1024]{1,0:T(8,128)(2,1)S(1)} %get-tuple-element.115), channel_id=1, source_target_pairs={{0,1},{1,0},{2,3},{3,2},{4,5},{5,4},{6,7},{7,6},{8,9},{9,8},{10,11... | collective-permute-start | bytes 786440 | tf_op jit(solution)/shard_map/ppermute | solution.py:352
  232.8 14.5 %collective-permute-start.50 = (bf16[128,1024]{1,0:T(8,128)(2,1)S(1)}, bf16[128,1024]{1,0:T(8,128)(2,1)S(1)}, u32[]{:S(2)}, u32[]{:S(2)}) collective-permute-start(bf16[128,1024]{1,0:T(8,128)(2,1)S(1)} %get-tuple-element.116), channel_id=1, source_target_pairs={{0,4},{1,5},{2,6},{3,7},{4,0},{5,1},{6,2},{7,3},{8,12},{9,13},{10,... | collective-permute-start | bytes 786440 | tf_op jit(solution)/shard_map/ppermute | solution.py:352
  233.2 14.2 %collective-permute-start.51 = (bf16[128,1024]{1,0:T(8,128)(2,1)S(1)}, bf16[128,1024]{1,0:T(8,128)(2,1)S(1)}, u32[]{:S(2)}, u32[]{:S(2)}) collective-permute-start(bf16[128,1024]{1,0:T(8,128)(2,1)S(1)} %get-tuple-element.117), channel_id=1, source_target_pairs={{0,5},{1,4},{2,7},{3,6},{4,1},{5,0},{6,3},{7,2},{8,13},{9,12},{10,... | collective-permute-start | bytes 786440 | tf_op jit(solution)/shard_map/ppermute | solution.py:352
  237.1 13.1 %collective-permute-start.59 = (bf16[1024,128]{1,0:T(8,128)(2,1)S(1)}, bf16[1024,128]{1,0:T(8,128)(2,1)S(1)}, u32[]{:S(2)}, u32[]{:S(2)}) collective-permute-start(bf16[1024,128]{1,0:T(8,128)(2,1)S(1)} %get-tuple-element.133), channel_id=1, source_target_pairs={{0,1},{1,0},{2,3},{3,2},{4,5},{5,4},{6,7},{7,6},{8,9},{9,8},{10,11... | collective-permute-start | bytes 786440 | tf_op jit(solution)/shard_map/ppermute | solution.py:352
  (94 other events, 572.2 us)
Sparse Core Ops, SparseCore 0:
  58.9 51.1 all-gather.2
  145.9 43.8 reduce-scatter.1

commit v2 on v1

--- a/solution.py
+++ b/solution.py
@@ -361,6 +361,7 @@
 
 
 ANY = pl.BlockSpec(memory_space=pl.ANY)
+HBM = pl.BlockSpec(memory_space=pltpu.HBM)
 VMEM = pl.BlockSpec(memory_space=pltpu.VMEM)
 SMEM = pl.BlockSpec(memory_space=pltpu.SMEM)
 STEP = 256
@@ -381,7 +382,7 @@
     )
 
 
-def call(kernel, outs, specs, operands, scratch=(), cost=1.0, room=24):
+def call(kernel, outs, specs, operands, scratch=(), cost=1.0, room=16):
     return pl.pallas_call(
         kernel,
         out_shape=outs,
@@ -389,7 +390,7 @@
         out_specs=[VMEM] * len(outs),
         scratch_shapes=list(scratch),
         compiler_params=pltpu.CompilerParams(vmem_limit_bytes=room * 2**20),
-        cost_estimate=pl.CostEstimate(flops=int(cost * 1.1e9), bytes_accessed=0, transcendentals=0),
+        cost_estimate=pl.CostEstimate(flops=int(cost * 1.0 * 1.1e9), bytes_accessed=0, transcendentals=0),
     )(*operands)
 
 
@@ -404,6 +405,22 @@
         copy.wait()
 
 
+def gathered(spots, pieces, order, target):
+    half = len(order) // 2
+    rows = target.shape[0] // len(order)
+    pairs = []
+    for k in range(len(order)):
+        source = pl.multiple_of((spots[4] ^ (k % half)) * rows, rows)
+        pairs.append((pieces[k // half].at[pl.ds(source, rows)], target.at[pl.ds(k * rows, rows)]))
+    return pairs
+
+
+def copies(out_ref, values):
+    rows = values.shape[0]
+    for k in range(out_ref.shape[0] // rows):
+        out_ref[k * rows : (k + 1) * rows] = values
+
+
 def row_starts(place, order, rows):
     return [pl.multiple_of((place ^ offset) * rows, rows) for offset in order]
 
@@ -429,7 +446,7 @@
 
 def normalise_kernel(order, spots, *refs):
     pieces, (xhat_ref, held, sems) = refs[: len(order)], refs[len(order) :]
-    rows = pieces[0].shape[0]
+    rows = held.shape[0] // len(order)
     starts = row_starts(spots[3], order, rows)
     fetch([(p, held.at[pl.ds(s, rows)]) for p, s in zip(pieces, starts)], sems)
 
@@ -447,10 +464,13 @@
 
 
 def prepare_attention_kernel(dp_count, blk_count, spots, *refs):
-    joint_ref, output_ref, tokens_ref = refs[:3]
-    vectors, (pair_ref, expand_ref) = refs[3:9], refs[9:11]
-    outs = refs[11:]
-    blocks, (own_ref, small_ref, turned) = outs[:blk_count], outs[blk_count:]
+    count = 11
+    sources, outs = refs[:count], refs[count:]
+    blocks, (own_ref, small_ref) = outs[:blk_count], outs[blk_count : blk_count + 2]
+    turned, *kept, sems = outs[blk_count + 2 :]
+    fetch(list(zip(sources, kept)), sems)
+    joint_ref, output_ref, tokens_ref = kept[:3]
+    vectors, (pair_ref, shift_ref) = kept[3:9], kept[9:]
     turned[...] = low(wide(joint_ref[...]).T)
     for b, block in enumerate(blocks):
         first = (spots[2] ^ b) * 2
@@ -472,20 +492,25 @@
     pair = jnp.concatenate([pair, jnp.zeros((pair.shape[0], LANES - pair.shape[1]), jnp.float32)], 1)
     for k in range(pair.shape[0]):
         small = jnp.where(row == 6 + k, pair[k : k + 1], small)
-    small = jnp.where(row == 6 + pair.shape[0], wide(expand_ref[...]), small)
+    small = jnp.where(row == 6 + pair.shape[0], wide(shift_ref[...]), small)
     small_ref[...] = low(small)
 
 
-def prepare_forward_kernel(dp_count, blk_count, spots, *refs):
-    expand_ref, reduce_ref, cot_ref, _ = refs[:4]
-    blocks, (own_ref, turned) = refs[4 : 4 + blk_count], refs[4 + blk_count :]
+def cotangent_kernel(dp_count, spots, cot_ref, *refs):
+    own_ref, rows = refs[-1], cot_ref.shape[0]
+    for first in range(0, own_ref.shape[0], rows):
+        reorder_columns(spots, cot_ref, own_ref.at[first : first + rows], dp_count)
+
+
+def prepare_forward_kernel(blk_count, spots, *refs):
+    expand_ref, reduce_ref = refs[:2]
+    blocks, turned = refs[-blk_count - 1 : -1], refs[-1]
     turned[...] = low(wide(expand_ref[...]).T)
     units = turned.shape[0] // blk_count
     for b, block in enumerate(blocks):
         start = pl.multiple_of((spots[2] ^ b) * units, units)
         block[:units] = turned[pl.ds(start, units)]
         block[units:] = reduce_ref[pl.ds(start, units)]
-    reorder_columns(spots, cot_ref, own_ref, dp_count)
 
 
 def pack_kernel(blk_count, has_small, spots, *refs):
@@ -506,7 +531,7 @@
 
 def unpack_kernel(dp_count, plane_count, blk_count, pair_rows, spots, *refs):
     blocks = refs[:dp_count]
-    vector_ref, joint_ref, expand_ref, held, small, sems = refs[dp_count:]
+    vector_ref, joint_ref, expand_ref, held, small, sems = refs[dp_count + 2 :]
     dp, seq, blk = spots[0], spots[1], spots[2]
     deep = held.shape[1]
     fetch([(b.at[pl.ds(COLUMNS, deep)], held.at[d]) for d, b in enumerate(blocks)], sems)
@@ -564,7 +589,7 @@
 def attend_kernel(order, dp_count, spots, slope_ref, *refs):
     blocks = refs[:dp_count]
     xhat_ref, vector_ref, bias_ref = refs[dp_count : dp_count + 3]
-    mixed_ref, att_ref, lse_ref, weight_ref, own_ref, away_ref, sems = refs[dp_count + 3 :]
+    mixed_ref, att_ref, lse_ref, weight_ref, own_ref, away_ref, sems = refs[dp_count + 5 :]
     cut = weight_ref.shape[1] // dp_count
     fetch(
         [
@@ -719,10 +744,10 @@
             part[COLUMNS:, b * LANES : (b + 1) * LANES] = small[start : start + deep].astype(part.dtype)
 
 
-def split_kernel(count, blk_count, has_small, spots, total_ref, *refs):
-    came, outs = refs[:count], refs[count:]
+def split_kernel(count, blk_count, has_small, after, spots, *refs):
+    parts, outs = refs[:count], refs[count + after :]
     total = outs[-1]
-    total[...] = wide(summed(total_ref, came))
+    total[...] = wide(summed(parts[0], parts[1:]))
     rows = outs[0].shape[0]
     for b in range(blk_count):
         start = pl.multiple_of((spots[2] ^ b) * LANES, LANES)
@@ -760,11 +785,11 @@
         reduce_ref[pl.ds(start, units)] = wide(block[units:])
 
 
-def forward_fetch(count, dp_count, spots, pieces, weights, left, right, held, sems):
-    rows, cut = pieces[0].shape[0], weights.shape[2]
+def forward_fetch(order, dp_count, spots, pieces, weights, left, right, held, sems):
+    cut = weights.shape[2]
     fetch(
-        [(p, left.at[pl.ds(k * rows, rows)]) for k, p in enumerate(pieces[:count])]
-        + [(p, right.at[pl.ds(k * rows, rows)]) for k, p in enumerate(pieces[count:])]
+        gathered(spots, pieces[:2], order, left)
+        + gathered(spots, pieces[2:], order, right)
         + [
             (weights.at[spots[0] ^ d], held.at[:, pl.ds(d * cut, cut)]) for d in range(dp_count)
         ],
@@ -772,10 +797,10 @@
     )
 
 
-def forward_kernel(count, dp_count, spots, *refs):
-    pieces, weights = refs[: 2 * count], refs[2 * count]
-    bias_ref, act_ref, grad_ref, own_ref, away_ref, sum_ref, left, right, held, sems = refs[2 * count + 1 :]
-    forward_fetch(count, dp_count, spots, pieces, weights, left, right, held, sems)
+def forward_kernel(order, dp_count, spots, *refs):
+    pieces, weights = refs[:4], refs[4]
+    bias_ref, act_ref, grad_ref, own_ref, away_ref, sum_ref, left, right, held, sems = refs[5:]
+    forward_fetch(order, dp_count, spots, pieces, weights, left, right, held, sems)
     units = act_ref.shape[1]
     half = left.shape[0] // 2
     sum_ref[...] = jnp.zeros_like(sum_ref)
@@ -799,11 +824,11 @@
             away_ref[first - half : stop - half] = low(part)
 
 
-def forward_weights_kernel(count, dp_count, spots, *refs):
-    pieces, weights = refs[: 2 * count], refs[2 * count]
-    act_ref, grad_ref, _ = refs[2 * count + 1 : 2 * count + 4]
-    part_ref, own_ref, away_ref, left, right, held, sems = refs[2 * count + 4 :]
-    forward_fetch(count, dp_count, spots, pieces, weights, left, right, held, sems)
+def forward_weights_kernel(order, dp_count, spots, *refs):
+    pieces, weights = refs[:4], refs[4]
+    act_ref, grad_ref, _ = refs[5:8]
+    part_ref, own_ref, away_ref, left, right, held, sems = refs[8:]
+    forward_fetch(order, dp_count, spots, pieces, weights, left, right, held, sems)
     units, cut = act_ref.shape[1], weights.shape[2]
     for d in range(dp_count):
         block = slice(d * cut, (d + 1) * cut)
@@ -820,7 +845,8 @@
             away_ref[first - half : stop - half] = low(result)
 
 
-def add_kernel(own_ref, came_ref, after, total_ref, *pieces):
+def add_kernel(count, own_ref, came_ref, *refs):
+    total_ref, *pieces = refs[count:]
     rows = total_ref.shape[0]
     total_ref[...] = own_ref[:rows] + wide(came_ref[:rows])
     for k, piece in enumerate(pieces):
@@ -840,7 +866,7 @@
     tokens_ref, vector_ref, middle_ref, normed_ref = refs[count:]
     middle = wide(tokens_ref[...]) + (summed(total_ref, came) + vector_ref[2:3])
     middle_ref[...] = middle
-    normed_ref[...] = low(normalise(middle)[0] * vector_ref[3:4] + vector_ref[4:5])
+    copies(normed_ref, low(normalise(middle)[0] * vector_ref[3:4] + vector_ref[4:5]))
 
 
 def middle_back_kernel(count, total_ref, *refs):
@@ -848,7 +874,7 @@
     middle_ref, cot_ref, vector_ref, grad_ref, branch_ref, sums_ref = refs[count:]
     grad = summed(total_ref, came)
     xhat, scale = normalise(middle_ref[...])
-    upstream = wide(cot_ref[...])
+    upstream = wide(cot_ref[: grad_ref.shape[0]])
     total = upstream + norm_back(grad, xhat, scale, vector_ref[3:4])
     grad_ref[...] = total
     branch = low(total)
@@ -865,19 +891,24 @@
         out_ref[:, pl.ds(start, size)] = values[:, d * size : (d + 1) * size]
 
 
-def output_kernel(count, dp_count, spots, total_ref, *refs):
-    came = refs[:count]
-    middle_ref, vector_ref, out_ref = refs[count:]
-    result = middle_ref[...] + (summed(total_ref, came) + vector_ref[5:6])
-    place_columns(spots, dp_count, low(result), out_ref)
-
-
-def input_kernel(count, dp_count, spots, total_ref, *refs):
-    came = refs[:count]
-    grad_ref, tokens_ref, vector_ref, out_ref = refs[count:]
+def add_rows_kernel(count, spots, own_ref, came_ref, result_own, result_came, _, out_ref):
+    rows, width = own_ref.shape[0] // count, own_ref.shape[1]
+    for k in range(count):
+        block = slice(k * rows, (k + 1) * rows)
+        start = pl.multiple_of((spots[4] ^ k) * rows, rows)
+        out_ref[pl.ds(start, rows), :width] = low(own_ref[block] + wide(came_ref[block]))
+        out_ref[pl.ds(start, rows), width:] = low(result_own[block] + wide(result_came[block]))
+
+
+def final_kernel(dp_count, spots, parts_ref, grad_ref, tokens_ref, middle_ref, vector_ref, input_ref, output_ref):
+    width = grad_ref.shape[1]
+    grad = jnp.sum(wide(parts_ref[:, :, :width]), 0)
     xhat, scale = normalise(wide(tokens_ref[...]))
-    result = grad_ref[...] + norm_back(summed(total_ref, came), xhat, scale, vector_ref[:1])
-    place_columns(spots, dp_count, low(result), out_ref)
+    result = grad_ref[...] + norm_back(grad, xhat, scale, vector_ref[:1])
+    place_columns(spots, dp_count, low(result), input_ref)
+    result = jnp.sum(wide(parts_ref[:, :, width:]), 0)
+    result = middle_ref[...] + (result + vector_ref[5:6])
+    place_columns(spots, dp_count, low(result), output_ref)
 
 
 def local_heads(
@@ -900,7 +931,8 @@
     dp, seq, blk = (lax.axis_index(axis) for axis in ALL)
     plane_count = seq_count * blk_count
     place = seq * blk_count + blk
-    spots = jnp.stack([dp, seq, blk, place]).astype(jnp.int32)
+    chip = seq // 2 * blk_count + blk
+    spots = jnp.stack([dp, seq, blk, place, chip]).astype(jnp.int32)
     tok_rows, width = tokens.shape
     units = expand_weight.shape[1] // blk_count
     cut = width // dp_count
@@ -914,6 +946,7 @@
     halves_out = [struct(half_rows, width, f32), struct(half_rows, width, bf16)]
     own_out = [struct(tok_rows, width, f32)]
     low_out = [struct(tok_rows, width, bf16)]
+    copies_out = [struct(half_rows, width, bf16)]
     dma = lambda count: pltpu.SemaphoreType.DMA((count,))
     held = lambda columns: pltpu.VMEM((row_count, columns), bf16)
     kernel = functools.partial
@@ -922,29 +955,46 @@
         mine = [block] + [swap(block, PLANE, plane_count, chip) for chip in chips[1:]]
         return mine + [swap(p, PLANE, plane_count, core) for p in mine]
 
-    def scatter_plane(own, away, after=None):
+    groups = [[p ^ side for p in chips] for side in (0, core)]
+
+    def between_chips(blocks):
+        blocks = blocks.reshape(chip_count, tok_rows, blocks.shape[1])
+        return lax.all_to_all(blocks, PLANE, 0, 0, axis_index_groups=groups, tiled=True)
+
+    def gather_copies(copies):
+        mine = between_chips(copies).reshape(half_rows, width)
+        return [mine, swap(mine, PLANE, plane_count, core)]
+
+    def scatter_plane(own, away, after=()):
         came = swap(away, PLANE, plane_count, core)
-        after = own if after is None else after
         outs = own_out + low_out * (chip_count - 1)
-        total, *pieces = call(add_kernel, outs, [VMEM, VMEM, ANY], [own, came, after])
+        total, *pieces = call(
+            kernel(add_kernel, len(after)),
+            outs,
+            [VMEM, VMEM] + [ANY] * len(after),
+            [own, came] + list(after),
+        )
         pieces = [swap(p, PLANE, plane_count, chip) for chip, p in zip(chips[1:], pieces)]
         return [total] + pieces
 
     def exchange_blk(blocks):
         return [swap(p, "blk", blk_count, b) if b else p for b, p in enumerate(blocks)]
 
+    sources = [joint_weight, output_weight, tokens]
+    sources += [
+        v.reshape(1, -1)
+        for v in (first_gain, first_shift, output_bias, second_gain, second_shift, reduce_bias)
+    ]
+    sources += [joint_bias, expand_bias]
     *blocks, tokens_own, small = call(
         kernel(prepare_attention_kernel, dp_count, blk_count),
         [struct(COLUMNS, LANES, bf16)] * blk_count + low_out + [struct(SMALL, LANES, bf16)],
-        [SMEM] + [VMEM] * 11,
-        [spots, joint_weight, output_weight, tokens]
-        + [
-            v.reshape(1, -1)
-            for v in (first_gain, first_shift, output_bias, second_gain, second_shift, reduce_bias)
-        ]
-        + [joint_bias, expand_bias],
-        [pltpu.VMEM((joint_weight.shape[1], LANES), bf16)],
-        2,
+        [SMEM] + [HBM] * len(sources),
+        [spots] + sources,
+        [pltpu.VMEM((joint_weight.shape[1], LANES), bf16)]
+        + [pltpu.VMEM(v.shape, v.dtype) for v in sources]
+        + [dma(len(sources))],
+        room=60,
     )
     bits = [1 << b for b in range(plane_count.bit_length() - 1)]
     blocks = exchange_blk(blocks)
@@ -960,13 +1010,18 @@
     blocks = [block] + [swap(block, "dp", dp_count, d) for d in range(1, dp_count)]
     token_group = gather_plane(tokens_own)
 
-    *forward_blocks, cotangent_own = call(
-        kernel(prepare_forward_kernel, dp_count, blk_count),
-        [struct(2 * units, LANES, bf16)] * blk_count + low_out,
-        [SMEM] + [VMEM] * 3 + [ANY],
-        [spots, expand_weight, reduce_weight, cotangent, block],
+    cotangent_own = call(
+        kernel(cotangent_kernel, dp_count),
+        copies_out,
+        [SMEM, VMEM] + [ANY] * 2,
+        [spots, cotangent] + blocks[1:3],
+    )[0]
+    forward_blocks = call(
+        kernel(prepare_forward_kernel, blk_count),
+        [struct(2 * units, LANES, bf16)] * blk_count,
+        [SMEM] + [VMEM] * 2 + [ANY],
+        [spots, expand_weight, reduce_weight, blocks[1]],
         [pltpu.VMEM((expand_weight.shape[1], LANES), bf16)],
-        2,
     )
     forward_block = call(
         kernel(pack_kernel, blk_count, False),
@@ -975,12 +1030,12 @@
         [spots] + exchange_blk(forward_blocks),
     )[0]
     forward_weights = lax.all_gather(forward_block, "dp", axis=0, tiled=False)
-    cot_group = gather_plane(cotangent_own)
+    cot_group = gather_copies(cotangent_own)
 
     xhat = call(
         kernel(normalise_kernel, order),
         [struct(row_count, width, f32)],
-        [SMEM] + [ANY] * plane_count,
+        [SMEM] + [HBM] * plane_count,
         [spots] + token_group,
         [held(width), dma(plane_count)],
         2,
@@ -988,8 +1043,8 @@
     vectors, joint_row, expand_row = call(
         kernel(unpack_kernel, dp_count, plane_count, blk_count, joint_bias.shape[0]),
         [struct(8, width, f32), struct(8, QKV, f32), struct(8, units, f32)],
-        [SMEM] + [ANY] * dp_count,
-        [spots] + blocks,
+        [SMEM] + [HBM] * dp_count + [ANY] * 2,
+        [spots] + blocks + [xhat, tokens_own],
         [
             pltpu.VMEM((dp_count, small_deep, cut), bf16),
             pltpu.VMEM((dp_count * plane_count * SMALL, LANES), f32),
@@ -1003,31 +1058,33 @@
         [struct(row_count, QKV, bf16), struct(row_count, PAIR, f32)]
         + [struct(row_count, PAIR, f32), struct(COLUMNS, width, bf16)]
         + halves_out,
-        [SMEM, SMEM] + [ANY] * dp_count + [VMEM] * 3,
-        [spots, slopes] + blocks + [xhat, vectors, joint_row],
+        [SMEM, SMEM] + [HBM] * dp_count + [VMEM] * 3 + [ANY] * 2,
+        [spots, slopes] + blocks + [xhat, vectors, joint_row, cot_group[0], forward_block],
         [dma(dp_count)],
         10,
+        24,
     )
     branch = scatter_plane(own, away)
 
     middle, normed_two = call(
         kernel(middle_kernel, chip_count - 1),
-        own_out + low_out,
+        own_out + copies_out,
         [VMEM] * (chip_count + 2),
         branch + [tokens_own, vectors],
     )
-    normed_group = gather_plane(normed_two)
+    normed_group = gather_copies(normed_two)
     forward_operands = [spots] + normed_group + cot_group + [forward_weights]
-    forward_specs = [SMEM] + [ANY] * (2 * plane_count + 1)
+    forward_specs = [SMEM] + [HBM] * 5
     forward_scratch = [held(width), held(width), pltpu.VMEM((2 * units, width), bf16)]
     forward_scratch.append(dma(2 * plane_count + dp_count))
     activated, hidden_grad, own, away, hidden_sums = call(
-        kernel(forward_kernel, plane_count, dp_count),
+        kernel(forward_kernel, order, dp_count),
         [struct(row_count, units, bf16)] * 2 + halves_out + [struct(8, units, f32)],
         forward_specs + [VMEM],
         forward_operands + [expand_row],
         forward_scratch,
         8,
+        24,
     )
     normed_two_grad = scatter_plane(own, away)
     middle_grad, branch_grad, middle_sums = call(
@@ -1037,74 +1094,79 @@
         normed_two_grad + [middle, cotangent_own, vectors],
     )
     forward_grad, own, away = call(
-        kernel(forward_weights_kernel, plane_count, dp_count),
+        kernel(forward_weights_kernel, order, dp_count),
         [jax.ShapeDtypeStruct((dp_count, 2 * units, cut), bf16)] + halves_out,
         forward_specs + [VMEM, VMEM, ANY],
         forward_operands + [activated, hidden_grad, normed_two_grad[0]],
         forward_scratch,
         8,
+        24,
     )
     forward_grad = lax.psum_scatter(forward_grad, "dp", scatter_dimension=0, tiled=False)
     forward_grad = call(
-        kernel(split_kernel, 0, blk_count, False),
+        kernel(split_kernel, 1, blk_count, False, 0),
         [struct(2 * units, LANES, f32)] + [struct(2 * units, LANES, bf16)] * (blk_count - 1),
         [SMEM, VMEM],
         [spots, forward_grad],
         [pltpu.VMEM((2 * units, cut), f32)],
     )
+    forward_grad = exchange_blk(forward_grad)
     expand_grad, reduce_grad = call(
         kernel(forward_final_kernel, blk_count),
         [struct(LANES, blk_count * units, f32), struct(blk_count * units, LANES, f32)],
         [SMEM] + [VMEM] * blk_count,
-        [spots] + exchange_blk(forward_grad),
+        [spots] + forward_grad,
     )
 
     branch_group = gather_plane(branch_grad)
-    result = scatter_plane(own, away, branch_group[-1])
-    layer_output = call(
-        kernel(output_kernel, chip_count - 1, dp_count),
-        low_out,
-        [SMEM] + [VMEM] * (chip_count + 2),
-        [spots] + result + [middle, vectors],
-    )[0]
+    result_own, result_came = own, swap(away, PLANE, plane_count, core)
     mixed_grad, own, away = call(
         kernel(attend_back_kernel, order),
         [struct(row_count, QKV, bf16)] + halves_out,
-        [SMEM, SMEM] + [ANY] * plane_count + [VMEM] * 4 + [ANY],
-        [spots, slopes] + branch_group + [mixed, attended, log_sums, weights, result[0]],
+        [SMEM, SMEM] + [HBM] * plane_count + [VMEM] * 4 + [ANY],
+        [spots, slopes] + branch_group + [mixed, attended, log_sums, weights, spots],
         [held(width), held(PAIR)]
         + [pltpu.VMEM((row_count, PAIR), f32)] * 2
         + [dma(plane_count)],
         10,
+        24,
     )
     block_out = lambda dtype: struct(COLUMNS + small_deep, cut, dtype)
     attention_grad = call(
         kernel(attend_weights_kernel, order, dp_count, blk_count),
         [block_out(f32)] + [block_out(bf16)] * (dp_count - 1),
-        [SMEM] + [ANY] * plane_count + [VMEM] * 7,
+        [SMEM] + [HBM] * plane_count + [VMEM] * 7,
         [spots]
         + branch_group
         + [xhat, mixed_grad, attended, weights, vectors, middle_sums, hidden_sums],
         [held(width), pltpu.VMEM((dp_count * plane_count * SMALL, LANES), f32), dma(plane_count)],
-        8,
-    )
-    normed_one_grad = scatter_plane(own, away)
-    input_grad = call(
-        kernel(input_kernel, chip_count - 1, dp_count),
-        low_out,
-        [SMEM] + [VMEM] * (chip_count + 3),
-        [spots] + normed_one_grad + [middle_grad, tokens_own, vectors],
+        3,
+        24,
+    )
+    pieces = call(
+        kernel(add_rows_kernel, chip_count),
+        [struct(half_rows, 2 * width, bf16)],
+        [SMEM] + [VMEM] * 4 + [ANY],
+        [spots, own, swap(away, PLANE, plane_count, core), result_own, result_came]
+        + list(attention_grad[1:2]),
     )[0]
+    pieces = between_chips(pieces)
+    input_grad, layer_output = call(
+        kernel(final_kernel, dp_count),
+        low_out * 2,
+        [SMEM] + [VMEM] * 5,
+        [spots, pieces, middle_grad, tokens_own, middle, vectors],
+    )
     attention_grad = [attention_grad[0]] + [
         swap(attention_grad[d], "dp", dp_count, d) for d in range(1, dp_count)
     ]
     *attention_grad, small = call(
-        kernel(split_kernel, dp_count - 1, blk_count, True),
+        kernel(split_kernel, dp_count, blk_count, True, 2),
         [struct(COLUMNS, LANES, f32)]
         + [struct(COLUMNS, LANES, bf16)] * (blk_count - 1)
         + [struct(plane_count * SMALL, LANES, f32)],
-        [SMEM] + [VMEM] * dp_count,
-        [spots] + attention_grad,
+        [SMEM] + [VMEM] * dp_count + [ANY] * 2,
+        [spots] + attention_grad + [pieces, forward_grad[-1]],
         [pltpu.VMEM((COLUMNS + small_deep, cut), f32)],
     )
     joint_grad, output_grad = call(

time: 263 us -> 247 us (0.939); the launches traced: 259 us -> 246 us
  Pallas kernels: 45.4 us -> 57.5 us
  waiting for transfers between devices: 109 us -> 99.4 us
  local copies, waits for them, and re-layouts: 28.8 us -> 19.5 us
  starting transfers between devices: 60.3 us -> 52.9 us
    ppermute x60 -> x42, waiting for transfers between devices: 109 us -> 75.3 us  [swap(): return lax.ppermute(value, axes, [(i, i ^ offset) for i in range(count)])]
    ppermute x60 -> x42, starting transfers between devices: 60.2 us -> 42 us  [swap(): return lax.ppermute(value, axes, [(i, i ^ offset) for i in range(count)])]
    all_to_all x0 -> x3, waiting for transfers between devices: none -> 15.3 us  [between_chips(): lax.all_to_all(blocks, PLANE, 0, 0, axis_index_groups=groups, tiled=True)]
    pallas_call x23 -> x22, Pallas kernels: 45.4 us -> 57.5 us  [call(): pl.pallas_call(kernel, out_shape=outs, in_specs=specs, out_specs=[VMEM] *...]
    all_to_all x0 -> x3, starting transfers between devices: none -> 10.7 us  [between_chips(): lax.all_to_all(blocks, PLANE, 0, 0, axis_index_groups=groups, tiled=True)]
    unnamed x128 -> x78, local copies, waits for them, and re-layouts: 27.2 us -> 17.3 us
    all_gather x1, waiting for transfers between devices: 0.01 us -> 8.73 us  [local_heads(): forward_weights = lax.all_gather(forward_block, 'dp', axis=0, tiled=False)]
  transfers between devices with their start and end apart: 62 -> 47, of which waited for: 30 -> 24; matrix products, arithmetic and copies ran while one was open for 1% -> 1% of each run, Pallas kernels for 12% -> 15%
where the time goes in v2:
time: 247 us; the launch traced here: 246 us
  waiting for transfers between devices  99.4 us (40%)
  Pallas kernels  57.5 us (23%)
  starting transfers between devices  52.9 us (21%)
  local copies, waits for them, and re-layouts  19.5 us (8%)
  between operations  14.5 us (6%)
    ppermute x42, waiting for transfers between devices, swap(): return lax.ppermute(value, axes, [(i, i ^ offset) for i in range(count)])  75.3 us
    pallas_call x22, Pallas kernels, call(): pl.pallas_call(kernel, out_shape=outs, in_specs=specs, out_specs=[VMEM] *...  57.5 us
    ppermute x42, starting transfers between devices, swap(): return lax.ppermute(value, axes, [(i, i ^ offset) for i in range(count)])  42 us
    unnamed x78, local copies, waits for them, and re-layouts  17.3 us
    all_to_all x3, waiting for transfers between devices, between_chips(): lax.all_to_all(blocks, PLANE, 0, 0, axis_index_groups=groups, tiled=True)  15.3 us
    all_to_all x3, starting transfers between devices, between_chips(): lax.all_to_all(blocks, PLANE, 0, 0, axis_index_groups=groups, tiled=True)  10.7 us
    all_gather x1, waiting for transfers between devices, local_heads(): forward_weights = lax.all_gather(forward_block, 'dp', axis=0, tiled=False)  8.73 us
  transfers between devices with their start and end apart: 47, of which 24 were waited for; matrix products, arithmetic and copies ran while one was open for 1% of the time, Pallas kernels for 15%

profile of v2, /device:TPU:0, one launch (start us, length us, event | category | flops | bytes accessed | tf_op | source)
XLA Modules:
  0.0 246.0 jit_solution(2479690002914262897)
XLA Ops:
  7.8 2.9 %shard_map.245 = (bf16[512,128]{1,0:T(8,128)(2,1)}, bf16[512,128]{1,0:T(8,128)(2,1)}, bf16[128,1024]{1,0:T(8,128)(2,1)}, bf16[16,128]{1,0:T(8,128)(2,1)}) custom-call(s32[5]{0:T(128)} %stack.23.spots.refs_12_, bf16[128,768]{1,0:T(8,128)(2,1)} %refs_0_.2, bf16[256,128]{1,0:T(8,128)(2,1)} %refs_1_.2, bf16[128,1024]{1,0:T(8,128)(2,1)} %refs_2_.1, ...), custom_call_target="tpu_custom_call" | custom-call | flops 1100000000 | tf_op jit(solution)/shard_map/pallas_call | solution.py:386
  10.8 3.0 %collective-permute-start.1 = (bf16[16,128]{1,0:T(8,128)(2,1)}, bf16[16,128]{1,0:T(8,128)(2,1)S(1)}, u32[]{:S(2)}, u32[]{:S(2)}) collective-permute-start(bf16[16,128]{1,0:T(8,128)(2,1)} %get-tuple-element.70), channel_id=1, source_target_pairs={{0,1},{1,0},{2,3},{3,2},{4,5},{5,4},{6,7},{7,6},{8,9},{9,8},{10,11... | collective-permute-start | bytes 12296 | tf_op jit(solution)/shard_map/ppermute | solution.py:352
  24.9 2.7 %collective-permute-start.5 = (bf16[576,256]{1,0:T(8,128)(2,1)S(1)}, bf16[576,256]{1,0:T(8,128)(2,1)S(1)}, u32[]{:S(2)}, u32[]{:S(2)}) collective-permute-start(bf16[576,256]{1,0:T(8,128)(2,1)S(1)} %shard_map.246.refs_0_), channel_id=1, source_target_pairs={{0,16},{8,24},{16,0},{24,8},{1,17},{9,25},{17,1},{25,9},{2,18},{10... | collective-permute-start | bytes 884744 | tf_op jit(solution)/shard_map/ppermute | solution.py:352
  32.7 7.9 %collective-permute-done.5.refs_2_.refs_1_ = bf16[576,256]{1,0:T(8,128)(2,1)S(1)} collective-permute-done((bf16[576,256]{1,0:T(8,128)(2,1)S(1)}, bf16[576,256]{1,0:T(8,128)(2,1)S(1)}, u32[]{:S(2)}, u32[]{:S(2)}) %collective-permute-start.5) | collective-permute-done | bytes 294944 | tf_op jit(solution)/shard_map/ppermute | solution.py:352
  42.5 3.5 %all-to-all-start = ((bf16[4,128,1024]{2,1,0:T(8,128)(2,1)}), bf16[4,128,1024]{2,1,0:T(8,128)(2,1)S(1)}, u32[]{:S(2)}, u32[]{:S(2)}) async-start(bf16[4,128,1024]{2,1,0:T(8,128)(2,1)} %bitcast.11), calls=%async_computation | async-start | bytes 2097152 | tf_op jit(solution)/shard_map/all_to_all | solution.py:962
  47.1 3.2 %collective-permute-start.6 = (bf16[576,256]{1,0:T(8,128)(2,1)S(1)}, bf16[576,256]{1,0:T(8,128)(2,1)S(1)}, u32[]{:S(2)}, u32[]{:S(2)}) collective-permute-start(bf16[576,256]{1,0:T(8,128)(2,1)S(1)} %shard_map.246.refs_0_), channel_id=1, source_target_pairs={{0,24},{8,16},{16,8},{24,0},{1,25},{9,17},{17,9},{25,1},{2,26},{10... | collective-permute-start | bytes 884744 | tf_op jit(solution)/shard_map/ppermute | solution.py:352
  53.1 3.2 %shard_map.247.refs_4_.refs_8_ = f32[1024,1024]{1,0:T(8,128)S(1)} custom-call(s32[5]{0:T(128)S(1)} %copy-done.7, bf16[128,1024]{1,0:T(8,128)(2,1)S(1)} %copy-done.6, bf16[128,1024]{1,0:T(8,128)(2,1)} %collective-permute-done.7.refs_1_, bf16[128,1024]{1,0:T(8,128)(2,1)} %collective-permute-done.8.refs_2_, ...), custom_call_target="tpu_custom_call" | custom-call | flops 2200000000 | tf_op jit(solution)/shard_map/pallas_call | solution.py:386
  59.0 5.3 %collective-permute-done.14.refs_1_ = bf16[1024,128]{1,0:T(8,128)(2,1)S(1)} collective-permute-done((bf16[1024,128]{1,0:T(8,128)(2,1)S(1)}, bf16[1024,128]{1,0:T(8,128)(2,1)S(1)}, u32[]{:S(2)}, u32[]{:S(2)}) %collective-permute-start.14) | collective-permute-done | bytes 262176 | tf_op jit(solution)/shard_map/ppermute | solution.py:352
  67.9 7.6 %shard_map.252 = (bf16[1024,384]{1,0:T(8,128)(2,1)S(1)}, f32[1024,128]{1,0:T(8,128)S(1)}, f32[1024,128]{1,0:T(8,128)S(1)}, bf16[512,1024]{1,0:T(8,128)(2,1)S(1)}...) custom-call(s32[5]{0:T(128)S(1)} %copy-done.7, f32[2]{0:T(128)S(1)} %multiply_exponential_fusion.slope_ref, ...), custom_call_target="tpu_custom_call" | custom-call | flops 11000000512 | tf_op jit(solution)/shard_map/pallas_call | solution.py:386
  79.6 2.8 %collective-permute-done.15.came_ref = bf16[512,1024]{1,0:T(8,128)(2,1)S(1)} collective-permute-done((bf16[512,1024]{1,0:T(8,128)(2,1)}, bf16[512,1024]{1,0:T(8,128)(2,1)S(1)}, u32[]{:S(2)}, u32[]{:S(2)}) %collective-permute-start.15) | collective-permute-done | bytes 1048608 | tf_op jit(solution)/shard_map/ppermute | solution.py:352
  87.8 4.9 %collective-permute-done.16.refs_0_ = bf16[128,1024]{1,0:T(8,128)(2,1)S(1)} collective-permute-done((bf16[128,1024]{1,0:T(8,128)(2,1)S(1)}, bf16[128,1024]{1,0:T(8,128)(2,1)S(1)}, u32[]{:S(2)}, u32[]{:S(2)}) %collective-permute-start.16) | collective-permute-done | bytes 262176 | tf_op jit(solution)/shard_map/ppermute | solution.py:352
  93.8 5.7 %collective-permute-done.18.refs_2_ = bf16[128,1024]{1,0:T(8,128)(2,1)S(1)} collective-permute-done((bf16[128,1024]{1,0:T(8,128)(2,1)S(1)}, bf16[128,1024]{1,0:T(8,128)(2,1)S(1)}, u32[]{:S(2)}, u32[]{:S(2)}) %collective-permute-start.18) | collective-permute-done | bytes 262176 | tf_op jit(solution)/shard_map/ppermute | solution.py:352
  101.6 3.5 %all-to-all-start.1 = ((bf16[4,128,1024]{2,1,0:T(8,128)(2,1)}), bf16[4,128,1024]{2,1,0:T(8,128)(2,1)S(1)}, u32[]{:S(2)}, u32[]{:S(2)}) async-start(bf16[4,128,1024]{2,1,0:T(8,128)(2,1)} %bitcast.13), calls=%async_computation.1 | async-start | bytes 2097152 | tf_op jit(solution)/shard_map/all_to_all | solution.py:962
  105.4 12.8 %all-to-all-done.1 = bf16[4,128,1024]{2,1,0:T(8,128)(2,1)S(1)} async-done(((bf16[4,128,1024]{2,1,0:T(8,128)(2,1)}), bf16[4,128,1024]{2,1,0:T(8,128)(2,1)S(1)}, u32[]{:S(2)}, u32[]{:S(2)}) %all-to-all-start.1) | async-done | bytes 1048608 | tf_op jit(solution)/shard_map/all_to_all | solution.py:962
  118.3 8.7 %all-gather.3.cloned.1.call-done = bf16[4096,256]{1,0:T(8,128)(2,1)} async-done(((bf16[1024,256]{1,0:T(8,128)(2,1)}), bf16[4096,256]{1,0:T(8,128)(2,1)}) %all-gather.3.cloned.1.call-update) | async-done | bytes 2097168 | tf_op jit(solution)/shard_map/all_gather | solution.py:1032
  128.6 6.7 %shard_map.255 = (bf16[1024,512]{1,0:T(8,128)(2,1)S(1)}, bf16[1024,512]{1,0:T(8,128)(2,1)S(1)}, f32[512,1024]{1,0:T(8,128)S(1)}, bf16[512,1024]{1,0:T(8,128)(2,1)S(1)}, f32[8,512]{1,0:T(8,128)S(1)}) custom-call(s32[5]{0:T(128)S(1)} %copy-done.7, bf16[512,1024]{1,0:T(8,128)(2,1)S(1)} %bitcast.35, bf16[512,1024]{1,0:T(8,128)(2,1)} %collective-permute-done.19.refs_1_, ...), custom_call_target="tpu_custom_call" | custom-call | flops 8800000000 | tf_op jit(solution)/shard_map/pallas_call | solution.py:386
  135.4 2.6 %collective-permute-done.21.came_ref = bf16[512,1024]{1,0:T(8,128)(2,1)S(1)} collective-permute-done((bf16[512,1024]{1,0:T(8,128)(2,1)S(1)}, bf16[512,1024]{1,0:T(8,128)(2,1)S(1)}, u32[]{:S(2)}, u32[]{:S(2)}) %collective-permute-start.21) | collective-permute-done | bytes 1048608 | tf_op jit(solution)/shard_map/ppermute | solution.py:352
  142.6 5.5 %shard_map.259 = (bf16[4,1024,256]{2,1,0:T(8,128)(2,1)S(1)}, f32[512,1024]{1,0:T(8,128)S(1)}, bf16[512,1024]{1,0:T(8,128)(2,1)S(1)}) custom-call(s32[5]{0:T(128)S(1)} %copy-done.7, bf16[512,1024]{1,0:T(8,128)(2,1)S(1)} %bitcast.36, bf16[512,1024]{1,0:T(8,128)(2,1)} %collective-permute-done.19.refs_1_, bf16[512,1024]{1,0:T(8,128)(2,1)S(1)} %bitcast.33, ...), custom_call_target="tpu_custom_call" | custom-call | flops 8800000000 | tf_op jit(solution)/shard_map/pallas_call | solution.py:386
  150.6 4.0 %collective-permute-done.24.refs_2_ = bf16[128,1024]{1,0:T(8,128)(2,1)} collective-permute-done((bf16[128,1024]{1,0:T(8,128)(2,1)}, bf16[128,1024]{1,0:T(8,128)(2,1)}, u32[]{:S(2)}, u32[]{:S(2)}) %collective-permute-start.24) | collective-permute-done | bytes 262176 | tf_op jit(solution)/shard_map/ppermute | solution.py:352
  154.5 2.4 shard_map.257
  157.7 2.3 collective-permute-start.27
  161.2 6.7 %collective-permute-done.27.refs_3_ = bf16[128,1024]{1,0:T(8,128)(2,1)S(1)} collective-permute-done((bf16[128,1024]{1,0:T(8,128)(2,1)S(1)}, bf16[128,1024]{1,0:T(8,128)(2,1)S(1)}, u32[]{:S(2)}, u32[]{:S(2)}) %collective-permute-start.27) | collective-permute-done | bytes 262176 | tf_op jit(solution)/shard_map/ppermute | solution.py:352
  167.9 3.3 %collective-permute-done.26.refs_2_ = bf16[128,1024]{1,0:T(8,128)(2,1)S(1)} collective-permute-done((bf16[128,1024]{1,0:T(8,128)(2,1)S(1)}, bf16[128,1024]{1,0:T(8,128)(2,1)S(1)}, u32[]{:S(2)}, u32[]{:S(2)}) %collective-permute-start.26) | collective-permute-done | bytes 262176 | tf_op jit(solution)/shard_map/ppermute | solution.py:352
  173.1 8.3 %shard_map.258 = (bf16[1024,384]{1,0:T(8,128)(2,1)S(1)}, f32[512,1024]{1,0:T(8,128)S(1)}, bf16[512,1024]{1,0:T(8,128)(2,1)S(1)}) custom-call(s32[5]{0:T(128)S(1)} %copy-done.7, f32[2]{0:T(128)S(1)} %multiply_exponential_fusion.slope_ref, bf16[128,1024]{1,0:T(8,128)(2,1)S(1)} %get-tuple-element.91.refs_0_, ...), custom_call_target="tpu_custom_call" | custom-call | flops 11000000512 | tf_op jit(solution)/shard_map/pallas_call | solution.py:386
  181.6 2.3 shard_map.260
  184.2 2.3 shard_map.261
  186.4 3.6 %all-to-all-start.2 = ((bf16[4,128,2048]{2,1,0:T(8,128)(2,1)}), bf16[4,128,2048]{2,1,0:T(8,128)(2,1)S(1)}, u32[]{:S(2)}, u32[]{:S(2)}) async-start(bf16[4,128,2048]{2,1,0:T(8,128)(2,1)} %bitcast.16), calls=%async_computation.2 | async-start | bytes 4194304 | tf_op jit(solution)/shard_map/all_to_all | solution.py:962
  191.8 2.7 %collective-permute-start.36 = (bf16[576,256]{1,0:T(8,128)(2,1)S(1)}, bf16[576,256]{1,0:T(8,128)(2,1)}, u32[]{:S(2)}, u32[]{:S(2)}) collective-permute-start(bf16[576,256]{1,0:T(8,128)(2,1)S(1)} %get-tuple-element.111), channel_id=1, source_target_pairs={{0,24},{8,16},{16,8},{24,0},{1,25},{9,17},{17,9},{25,1},{2,26},{10... | collective-permute-start | bytes 884744 | tf_op jit(solution)/shard_map/ppermute | solution.py:352
  199.6 14.1 %collective-permute-done.35.refs_2_ = bf16[576,256]{1,0:T(8,128)(2,1)} collective-permute-done((bf16[576,256]{1,0:T(8,128)(2,1)S(1)}, bf16[576,256]{1,0:T(8,128)(2,1)}, u32[]{:S(2)}, u32[]{:S(2)}) %collective-permute-start.35) | collective-permute-done | bytes 294944 | tf_op jit(solution)/shard_map/ppermute | solution.py:352
  213.7 2.5 %all-to-all-done.2.parts_ref.refs_4_ = bf16[4,128,2048]{2,1,0:T(8,128)(2,1)S(1)} async-done(((bf16[4,128,2048]{2,1,0:T(8,128)(2,1)}), bf16[4,128,2048]{2,1,0:T(8,128)(2,1)S(1)}, u32[]{:S(2)}, u32[]{:S(2)}) %all-to-all-start.2) | async-done | bytes 2097184 | tf_op jit(solution)/shard_map/all_to_all | solution.py:962
  216.2 5.0 %collective-permute-done.37.refs_5_.refs_1_ = bf16[1024,128]{1,0:T(8,128)(2,1)} collective-permute-done((bf16[1024,128]{1,0:T(8,128)(2,1)}, bf16[1024,128]{1,0:T(8,128)(2,1)}, u32[]{:S(2)}, u32[]{:S(2)}) %collective-permute-start.37) | collective-permute-done | bytes 262176 | tf_op jit(solution)/shard_map/ppermute | solution.py:352
  225.3 2.5 collective-permute-done.38
  (178 shorter events, 76.8 us)
Async XLA Ops:
  16.3 7.1 %collective-permute-start = (bf16[512,128]{1,0:T(8,128)(2,1)}, bf16[512,128]{1,0:T(8,128)(2,1)S(1)}, u32[]{:S(2)}, u32[]{:S(2)}) collective-permute-start(bf16[512,128]{1,0:T(8,128)(2,1)} %get-tuple-element.69), channel_id=1, source_target_pairs={{0,1},{1,0},{2,3},{3,2},{4,5},{5,4},{6,7},{7,6},{8,9},{9,8},{10,11... | collective-permute-start | bytes 393224 | tf_op jit(solution)/shard_map/ppermute | solution.py:352
  24.9 15.7 %collective-permute-start.5 = (bf16[576,256]{1,0:T(8,128)(2,1)S(1)}, bf16[576,256]{1,0:T(8,128)(2,1)S(1)}, u32[]{:S(2)}, u32[]{:S(2)}) collective-permute-start(bf16[576,256]{1,0:T(8,128)(2,1)S(1)} %shard_map.246.refs_0_), channel_id=1, source_target_pairs={{0,16},{8,24},{16,0},{24,8},{1,17},{9,25},{17,1},{25,9},{2,18},{10... | collective-permute-start | bytes 884744 | tf_op jit(solution)/shard_map/ppermute | solution.py:352
  27.6 13.2 %collective-permute-start.4 = (bf16[576,256]{1,0:T(8,128)(2,1)S(1)}, bf16[576,256]{1,0:T(8,128)(2,1)S(1)}, u32[]{:S(2)}, u32[]{:S(2)}) collective-permute-start(bf16[576,256]{1,0:T(8,128)(2,1)S(1)} %shard_map.246.refs_0_), channel_id=1, source_target_pairs={{0,8},{8,0},{16,24},{24,16},{1,9},{9,1},{17,25},{25,17},{2,10},{10... | collective-permute-start | bytes 884744 | tf_op jit(solution)/shard_map/ppermute | solution.py:352
  29.2 16.9 %collective-permute-start.9 = (bf16[128,1024]{1,0:T(8,128)(2,1)S(1)}, bf16[128,1024]{1,0:T(8,128)(2,1)S(1)}, u32[]{:S(2)}, u32[]{:S(2)}) collective-permute-start(bf16[128,1024]{1,0:T(8,128)(2,1)S(1)} %copy-done.6), channel_id=1, source_target_pairs={{0,5},{1,4},{2,7},{3,6},{4,1},{5,0},{6,3},{7,2},{8,13},{9,12},{10,... | collective-permute-start | bytes 786440 | tf_op jit(solution)/shard_map/ppermute | solution.py:352
  31.3 15.3 %collective-permute-start.8 = (bf16[128,1024]{1,0:T(8,128)(2,1)S(1)}, bf16[128,1024]{1,0:T(8,128)(2,1)}, u32[]{:S(2)}, u32[]{:S(2)}) collective-permute-start(bf16[128,1024]{1,0:T(8,128)(2,1)S(1)} %copy-done.6), channel_id=1, source_target_pairs={{0,4},{1,5},{2,6},{3,7},{4,0},{5,1},{6,2},{7,3},{8,12},{9,13},{10,... | collective-permute-start | bytes 786440 | tf_op jit(solution)/shard_map/ppermute | solution.py:352
  31.8 14.9 %collective-permute-start.7 = (bf16[128,1024]{1,0:T(8,128)(2,1)S(1)}, bf16[128,1024]{1,0:T(8,128)(2,1)}, u32[]{:S(2)}, u32[]{:S(2)}) collective-permute-start(bf16[128,1024]{1,0:T(8,128)(2,1)S(1)} %copy-done.6), channel_id=1, source_target_pairs={{0,1},{1,0},{2,3},{3,2},{4,5},{5,4},{6,7},{7,6},{8,9},{9,8},{10,11... | collective-permute-start | bytes 786440 | tf_op jit(solution)/shard_map/ppermute | solution.py:352
  42.5 23.3 %all-to-all-start = ((bf16[4,128,1024]{2,1,0:T(8,128)(2,1)}), bf16[4,128,1024]{2,1,0:T(8,128)(2,1)S(1)}, u32[]{:S(2)}, u32[]{:S(2)}) async-start(bf16[4,128,1024]{2,1,0:T(8,128)(2,1)} %bitcast.11), calls=%async_computation | async-start | bytes 2097152 | tf_op jit(solution)/shard_map/all_to_all | solution.py:962
  46.0 81.0 %all-gather.3.cloned.1.call-start = ((), (), s32[]{:S(2)}) async-start(), calls=%async_computation.5 | async-start | bytes 2621440 | tf_op jit(solution)/shard_map/all_gather | solution.py:1032
  46.1 6.9 %collective-permute-start.13 = (bf16[128,1024]{1,0:T(8,128)(2,1)S(1)}, bf16[128,1024]{1,0:T(8,128)(2,1)}, u32[]{:S(2)}, u32[]{:S(2)}) collective-permute-start(bf16[128,1024]{1,0:T(8,128)(2,1)S(1)} %collective-permute-done.9.refs_3_), channel_id=1, source_target_pairs={{0,2},{1,3},{2,0},{3,1},{4,6},{5,7},{6,4},{7,5},{8,10},{9,11},{10,... | collective-permute-start | bytes 786440 | tf_op jit(solution)/shard_map/ppermute | solution.py:352
  47.1 10.9 %collective-permute-start.6 = (bf16[576,256]{1,0:T(8,128)(2,1)S(1)}, bf16[576,256]{1,0:T(8,128)(2,1)S(1)}, u32[]{:S(2)}, u32[]{:S(2)}) collective-permute-start(bf16[576,256]{1,0:T(8,128)(2,1)S(1)} %shard_map.246.refs_0_), channel_id=1, source_target_pairs={{0,24},{8,16},{16,8},{24,0},{1,25},{9,17},{17,9},{25,1},{2,26},{10... | collective-permute-start | bytes 884744 | tf_op jit(solution)/shard_map/ppermute | solution.py:352
  51.1 13.2 %collective-permute-start.14 = (bf16[1024,128]{1,0:T(8,128)(2,1)S(1)}, bf16[1024,128]{1,0:T(8,128)(2,1)S(1)}, u32[]{:S(2)}, u32[]{:S(2)}) collective-permute-start(bf16[1024,128]{1,0:T(8,128)(2,1)S(1)} %get-tuple-element.75), channel_id=1, source_target_pairs={{0,1},{1,0},{2,3},{3,2},{4,5},{5,4},{6,7},{7,6},{8,9},{9,8},{10,11... | collective-permute-start | bytes 786440 | tf_op jit(solution)/shard_map/ppermute | solution.py:352
  84.2 8.4 %collective-permute-start.16 = (bf16[128,1024]{1,0:T(8,128)(2,1)S(1)}, bf16[128,1024]{1,0:T(8,128)(2,1)S(1)}, u32[]{:S(2)}, u32[]{:S(2)}) collective-permute-start(bf16[128,1024]{1,0:T(8,128)(2,1)S(1)} %get-tuple-element.79), channel_id=1, source_target_pairs={{0,1},{1,0},{2,3},{3,2},{4,5},{5,4},{6,7},{7,6},{8,9},{9,8},{10,11... | collective-permute-start | bytes 786440 | tf_op jit(solution)/shard_map/ppermute | solution.py:352
  84.6 9.2 %collective-permute-start.17 = (bf16[128,1024]{1,0:T(8,128)(2,1)S(1)}, bf16[128,1024]{1,0:T(8,128)(2,1)S(1)}, u32[]{:S(2)}, u32[]{:S(2)}) collective-permute-start(bf16[128,1024]{1,0:T(8,128)(2,1)S(1)} %get-tuple-element.80), channel_id=1, source_target_pairs={{0,4},{1,5},{2,6},{3,7},{4,0},{5,1},{6,2},{7,3},{8,12},{9,13},{10,... | collective-permute-start | bytes 786440 | tf_op jit(solution)/shard_map/ppermute | solution.py:352
  86.0 13.4 %collective-permute-start.18 = (bf16[128,1024]{1,0:T(8,128)(2,1)S(1)}, bf16[128,1024]{1,0:T(8,128)(2,1)S(1)}, u32[]{:S(2)}, u32[]{:S(2)}) collective-permute-start(bf16[128,1024]{1,0:T(8,128)(2,1)S(1)} %get-tuple-element.81), channel_id=1, source_target_pairs={{0,5},{1,4},{2,7},{3,6},{4,1},{5,0},{6,3},{7,2},{8,13},{9,12},{10,... | collective-permute-start | bytes 786440 | tf_op jit(solution)/shard_map/ppermute | solution.py:352
  101.6 16.7 %all-to-all-start.1 = ((bf16[4,128,1024]{2,1,0:T(8,128)(2,1)}), bf16[4,128,1024]{2,1,0:T(8,128)(2,1)S(1)}, u32[]{:S(2)}, u32[]{:S(2)}) async-start(bf16[4,128,1024]{2,1,0:T(8,128)(2,1)} %bitcast.13), calls=%async_computation.1 | async-start | bytes 2097152 | tf_op jit(solution)/shard_map/all_to_all | solution.py:962
  105.1 89.4 %reduce-scatter.2.cloned.1.call-start = ((), (), s32[]{:S(2)}) async-start(), calls=%async_computation.4 | async-start | bytes 2621440 | tf_op jit(solution)/shard_map/reduce_scatter | solution.py:1105
  105.4 12.9 %collective-permute-start.20 = (bf16[512,1024]{1,0:T(8,128)(2,1)S(1)}, bf16[512,1024]{1,0:T(8,128)(2,1)S(1)}, u32[]{:S(2)}, u32[]{:S(2)}) collective-permute-start(bf16[512,1024]{1,0:T(8,128)(2,1)S(1)} %bitcast.31), channel_id=1, source_target_pairs={{0,2},{1,3},{2,0},{3,1},{4,6},{5,7},{6,4},{7,5},{8,10},{9,11},{10,... | collective-permute-start | bytes 3145736 | tf_op jit(solution)/shard_map/ppermute | solution.py:352
  118.3 8.8 %collective-permute-start.19 = (bf16[512,1024]{1,0:T(8,128)(2,1)S(1)}, bf16[512,1024]{1,0:T(8,128)(2,1)}, u32[]{:S(2)}, u32[]{:S(2)}) collective-permute-start(bf16[512,1024]{1,0:T(8,128)(2,1)S(1)} %bitcast.34), channel_id=1, source_target_pairs={{0,2},{1,3},{2,0},{3,1},{4,6},{5,7},{6,4},{7,5},{8,10},{9,11},{10,... | collective-permute-start | bytes 3145736 | tf_op jit(solution)/shard_map/ppermute | solution.py:352
  139.1 11.5 %collective-permute-start.22 = (bf16[128,1024]{1,0:T(8,128)(2,1)}, bf16[128,1024]{1,0:T(8,128)(2,1)}, u32[]{:S(2)}, u32[]{:S(2)}) collective-permute-start(bf16[128,1024]{1,0:T(8,128)(2,1)} %get-tuple-element.87), channel_id=1, source_target_pairs={{0,1},{1,0},{2,3},{3,2},{4,5},{5,4},{6,7},{7,6},{8,9},{9,8},{10,11... | collective-permute-start | bytes 786440 | tf_op jit(solution)/shard_map/ppermute | solution.py:352
  140.5 10.0 %collective-permute-start.23 = (bf16[128,1024]{1,0:T(8,128)(2,1)}, bf16[128,1024]{1,0:T(8,128)(2,1)}, u32[]{:S(2)}, u32[]{:S(2)}) collective-permute-start(bf16[128,1024]{1,0:T(8,128)(2,1)} %get-tuple-element.88), channel_id=1, source_target_pairs={{0,4},{1,5},{2,6},{3,7},{4,0},{5,1},{6,2},{7,3},{8,12},{9,13},{10,... | collective-permute-start | bytes 786440 | tf_op jit(solution)/shard_map/ppermute | solution.py:352
  142.0 12.5 %collective-permute-start.24 = (bf16[128,1024]{1,0:T(8,128)(2,1)}, bf16[128,1024]{1,0:T(8,128)(2,1)}, u32[]{:S(2)}, u32[]{:S(2)}) collective-permute-start(bf16[128,1024]{1,0:T(8,128)(2,1)} %get-tuple-element.89), channel_id=1, source_target_pairs={{0,5},{1,4},{2,7},{3,6},{4,1},{5,0},{6,3},{7,2},{8,13},{9,12},{10,... | collective-permute-start | bytes 786440 | tf_op jit(solution)/shard_map/ppermute | solution.py:352
  157.7 10.2 %collective-permute-start.27 = (bf16[128,1024]{1,0:T(8,128)(2,1)S(1)}, bf16[128,1024]{1,0:T(8,128)(2,1)S(1)}, u32[]{:S(2)}, u32[]{:S(2)}) collective-permute-start(bf16[128,1024]{1,0:T(8,128)(2,1)S(1)} %get-tuple-element.91.refs_0_), channel_id=1, source_target_pairs={{0,5},{1,4},{2,7},{3,6},{4,1},{5,0},{6,3},{7,2},{8,13},{9,12},{10,... | collective-permute-start | bytes 786440 | tf_op jit(solution)/shard_map/ppermute | solution.py:352
  160.0 11.1 %collective-permute-start.26 = (bf16[128,1024]{1,0:T(8,128)(2,1)S(1)}, bf16[128,1024]{1,0:T(8,128)(2,1)S(1)}, u32[]{:S(2)}, u32[]{:S(2)}) collective-permute-start(bf16[128,1024]{1,0:T(8,128)(2,1)S(1)} %get-tuple-element.91.refs_0_), channel_id=1, source_target_pairs={{0,4},{1,5},{2,6},{3,7},{4,0},{5,1},{6,2},{7,3},{8,12},{9,13},{10,... | collective-permute-start | bytes 786440 | tf_op jit(solution)/shard_map/ppermute | solution.py:352
  160.6 10.6 %collective-permute-start.25 = (bf16[128,1024]{1,0:T(8,128)(2,1)S(1)}, bf16[128,1024]{1,0:T(8,128)(2,1)S(1)}, u32[]{:S(2)}, u32[]{:S(2)}) collective-permute-start(bf16[128,1024]{1,0:T(8,128)(2,1)S(1)} %get-tuple-element.91.refs_0_), channel_id=1, source_target_pairs={{0,1},{1,0},{2,3},{3,2},{4,5},{5,4},{6,7},{7,6},{8,9},{9,8},{10,11... | collective-permute-start | bytes 786440 | tf_op jit(solution)/shard_map/ppermute | solution.py:352
  161.2 10.6 %collective-permute-start.28 = (bf16[128,1024]{1,0:T(8,128)(2,1)S(1)}, bf16[128,1024]{1,0:T(8,128)(2,1)S(1)}, u32[]{:S(2)}, u32[]{:S(2)}) collective-permute-start(bf16[128,1024]{1,0:T(8,128)(2,1)S(1)} %get-tuple-element.91.refs_0_), channel_id=1, source_target_pairs={{0,2},{1,3},{2,0},{3,1},{4,6},{5,7},{6,4},{7,5},{8,10},{9,11},{10,... | collective-permute-start | bytes 786440 | tf_op jit(solution)/shard_map/ppermute | solution.py:352
  171.7 12.3 %collective-permute-start.33 = (bf16[512,1024]{1,0:T(8,128)(2,1)S(1)}, bf16[512,1024]{1,0:T(8,128)(2,1)S(1)}, u32[]{:S(2)}, u32[]{:S(2)}) collective-permute-start(bf16[512,1024]{1,0:T(8,128)(2,1)S(1)} %copy-done.10), channel_id=1, source_target_pairs={{0,2},{1,3},{2,0},{3,1},{4,6},{5,7},{6,4},{7,5},{8,10},{9,11},{10,... | collective-permute-start | bytes 3145736 | tf_op jit(solution)/shard_map/ppermute | solution.py:352
  186.4 29.8 %all-to-all-start.2 = ((bf16[4,128,2048]{2,1,0:T(8,128)(2,1)}), bf16[4,128,2048]{2,1,0:T(8,128)(2,1)S(1)}, u32[]{:S(2)}, u32[]{:S(2)}) async-start(bf16[4,128,2048]{2,1,0:T(8,128)(2,1)} %bitcast.16), calls=%async_computation.2 | async-start | bytes 4194304 | tf_op jit(solution)/shard_map/all_to_all | solution.py:962
  190.0 23.7 %collective-permute-start.34 = (bf16[576,256]{1,0:T(8,128)(2,1)S(1)}, bf16[576,256]{1,0:T(8,128)(2,1)}, u32[]{:S(2)}, u32[]{:S(2)}) collective-permute-start(bf16[576,256]{1,0:T(8,128)(2,1)S(1)} %get-tuple-element.105._), channel_id=1, source_target_pairs={{0,8},{8,0},{16,24},{24,16},{1,9},{9,1},{17,25},{25,17},{2,10},{10... | collective-permute-start | bytes 884744 | tf_op jit(solution)/shard_map/ppermute | solution.py:352
  190.1 23.6 %collective-permute-start.35 = (bf16[576,256]{1,0:T(8,128)(2,1)S(1)}, bf16[576,256]{1,0:T(8,128)(2,1)}, u32[]{:S(2)}, u32[]{:S(2)}) collective-permute-start(bf16[576,256]{1,0:T(8,128)(2,1)S(1)} %get-tuple-element.110), channel_id=1, source_target_pairs={{0,16},{8,24},{16,0},{24,8},{1,17},{9,25},{17,1},{25,9},{2,18},{10... | collective-permute-start | bytes 884744 | tf_op jit(solution)/shard_map/ppermute | solution.py:352
  191.8 22.0 %collective-permute-start.36 = (bf16[576,256]{1,0:T(8,128)(2,1)S(1)}, bf16[576,256]{1,0:T(8,128)(2,1)}, u32[]{:S(2)}, u32[]{:S(2)}) collective-permute-start(bf16[576,256]{1,0:T(8,128)(2,1)S(1)} %get-tuple-element.111), channel_id=1, source_target_pairs={{0,24},{8,16},{16,8},{24,0},{1,25},{9,17},{17,9},{25,1},{2,26},{10... | collective-permute-start | bytes 884744 | tf_op jit(solution)/shard_map/ppermute | solution.py:352
  197.7 23.5 %collective-permute-start.37 = (bf16[1024,128]{1,0:T(8,128)(2,1)}, bf16[1024,128]{1,0:T(8,128)(2,1)}, u32[]{:S(2)}, u32[]{:S(2)}) collective-permute-start(bf16[1024,128]{1,0:T(8,128)(2,1)} %get-tuple-element.113), channel_id=1, source_target_pairs={{0,1},{1,0},{2,3},{3,2},{4,5},{5,4},{6,7},{7,6},{8,9},{9,8},{10,11... | collective-permute-start | bytes 786440 | tf_op jit(solution)/shard_map/ppermute | solution.py:352
  229.9 7.7 %collective-permute-start.41 = (bf16[512,128]{1,0:T(8,128)(2,1)S(1)}, bf16[512,128]{1,0:T(8,128)(2,1)S(1)}, u32[]{:S(2)}, u32[]{:S(2)}) collective-permute-start(bf16[512,128]{1,0:T(8,128)(2,1)S(1)} %get-tuple-element.116), channel_id=1, source_target_pairs={{0,1},{1,0},{2,3},{3,2},{4,5},{5,4},{6,7},{7,6},{8,9},{9,8},{10,11... | collective-permute-start | bytes 393224 | tf_op jit(solution)/shard_map/ppermute | solution.py:352
  (54 other events, 389.0 us)
Sparse Core Ops, SparseCore 0:
  79.7 47.2 all-gather.2
  150.6 42.5 reduce-scatter.1

commit v3 on v2

--- a/solution.py
+++ b/solution.py
@@ -415,10 +415,9 @@
     return pairs
 
 
-def copies(out_ref, values):
-    rows = values.shape[0]
-    for k in range(out_ref.shape[0] // rows):
-        out_ref[k * rows : (k + 1) * rows] = values
+def halves(pieces, target):
+    rows = pieces[0].shape[0]
+    return [(p, target.at[pl.ds(k * rows, rows)]) for k, p in enumerate(pieces)]
 
 
 def row_starts(place, order, rows):
@@ -518,7 +517,8 @@
     rows = blocks[0].shape[0]
     for b, block in enumerate(blocks):
         start = pl.multiple_of((spots[2] ^ b) * LANES, LANES)
-        out_ref[:rows, pl.ds(start, LANES)] = block[...]
+        for first in range(0, out_ref.shape[0], out_ref.shape[0] if has_small else rows):
+            out_ref[first : first + rows, pl.ds(start, LANES)] = block[...]
     if has_small:
         small_ref = refs[blk_count]
         count = small_ref.shape[0] // SMALL
@@ -747,7 +747,10 @@
 def split_kernel(count, blk_count, has_small, after, spots, *refs):
     parts, outs = refs[:count], refs[count + after :]
     total = outs[-1]
-    total[...] = wide(summed(parts[0], parts[1:]))
+    if len(parts[0].shape) == 3:
+        total[...] = jnp.sum(wide(parts[0][...]), 0)
+    else:
+        total[...] = wide(summed(parts[0], parts[1:]))
     rows = outs[0].shape[0]
     for b in range(blk_count):
         start = pl.multiple_of((spots[2] ^ b) * LANES, LANES)
@@ -788,8 +791,8 @@
 def forward_fetch(order, dp_count, spots, pieces, weights, left, right, held, sems):
     cut = weights.shape[2]
     fetch(
-        gathered(spots, pieces[:2], order, left)
-        + gathered(spots, pieces[2:], order, right)
+        halves(pieces[:-2], left)
+        + gathered(spots, pieces[-2:], order, right)
         + [
             (weights.at[spots[0] ^ d], held.at[:, pl.ds(d * cut, cut)]) for d in range(dp_count)
         ],
@@ -798,8 +801,9 @@
 
 
 def forward_kernel(order, dp_count, spots, *refs):
-    pieces, weights = refs[:4], refs[4]
-    bias_ref, act_ref, grad_ref, own_ref, away_ref, sum_ref, left, right, held, sems = refs[5:]
+    count = len(order) + 2
+    pieces, weights, refs = refs[:count], refs[count], refs[count + 1 :]
+    bias_ref, act_ref, grad_ref, own_ref, away_ref, sum_ref, left, right, held, sems = refs
     forward_fetch(order, dp_count, spots, pieces, weights, left, right, held, sems)
     units = act_ref.shape[1]
     half = left.shape[0] // 2
@@ -825,9 +829,10 @@
 
 
 def forward_weights_kernel(order, dp_count, spots, *refs):
-    pieces, weights = refs[:4], refs[4]
-    act_ref, grad_ref, _ = refs[5:8]
-    part_ref, own_ref, away_ref, left, right, held, sems = refs[8:]
+    count = len(order) + 2
+    pieces, weights, refs = refs[:count], refs[count], refs[count + 1 :]
+    act_ref, grad_ref, _ = refs[:3]
+    part_ref, own_ref, away_ref, left, right, held, sems = refs[3:]
     forward_fetch(order, dp_count, spots, pieces, weights, left, right, held, sems)
     units, cut = act_ref.shape[1], weights.shape[2]
     for d in range(dp_count):
@@ -866,7 +871,7 @@
     tokens_ref, vector_ref, middle_ref, normed_ref = refs[count:]
     middle = wide(tokens_ref[...]) + (summed(total_ref, came) + vector_ref[2:3])
     middle_ref[...] = middle
-    copies(normed_ref, low(normalise(middle)[0] * vector_ref[3:4] + vector_ref[4:5]))
+    normed_ref[...] = low(normalise(middle)[0] * vector_ref[3:4] + vector_ref[4:5])
 
 
 def middle_back_kernel(count, total_ref, *refs):
@@ -1025,11 +1030,13 @@
     )
     forward_block = call(
         kernel(pack_kernel, blk_count, False),
-        [struct(2 * units, cut, bf16)],
+        [struct(dp_count * 2 * units, cut, bf16)],
         [SMEM] + [VMEM] * blk_count,
         [spots] + exchange_blk(forward_blocks),
     )[0]
-    forward_weights = lax.all_gather(forward_block, "dp", axis=0, tiled=False)
+    forward_weights = lax.all_to_all(
+        forward_block.reshape(dp_count, 2 * units, cut), "dp", 0, 0, tiled=True
+    )
     cot_group = gather_copies(cotangent_own)
 
     xhat = call(
@@ -1068,13 +1075,13 @@
 
     middle, normed_two = call(
         kernel(middle_kernel, chip_count - 1),
-        own_out + copies_out,
+        own_out + low_out,
         [VMEM] * (chip_count + 2),
         branch + [tokens_own, vectors],
     )
-    normed_group = gather_copies(normed_two)
+    normed_group = gather_plane(normed_two)
     forward_operands = [spots] + normed_group + cot_group + [forward_weights]
-    forward_specs = [SMEM] + [HBM] * 5
+    forward_specs = [SMEM] + [HBM] * (plane_count + 3)
     forward_scratch = [held(width), held(width), pltpu.VMEM((2 * units, width), bf16)]
     forward_scratch.append(dma(2 * plane_count + dp_count))
     activated, hidden_grad, own, away, hidden_sums = call(
@@ -1084,7 +1091,7 @@
         forward_operands + [expand_row],
         forward_scratch,
         8,
-        24,
+        60,
     )
     normed_two_grad = scatter_plane(own, away)
     middle_grad, branch_grad, middle_sums = call(
@@ -1100,9 +1107,9 @@
         forward_operands + [activated, hidden_grad, normed_two_grad[0]],
         forward_scratch,
         8,
-        24,
-    )
-    forward_grad = lax.psum_scatter(forward_grad, "dp", scatter_dimension=0, tiled=False)
+        60,
+    )
+    forward_grad = lax.all_to_all(forward_grad, "dp", 0, 0, tiled=True)
     forward_grad = call(
         kernel(split_kernel, 1, blk_count, False, 0),
         [struct(2 * units, LANES, f32)] + [struct(2 * units, LANES, bf16)] * (blk_count - 1),

time: 247 us -> 245 us (level)
  between operations: 14.5 us -> 1.27 us
  starting transfers between devices: 52.9 us -> 63.2 us
  waiting for transfers between devices: 99.4 us -> 92.4 us
  Pallas kernels: 57.5 us -> 62.3 us
  local copies, waits for them, and re-layouts: 19.5 us -> 22.7 us
    all_to_all x3 -> x2, waiting for transfers between devices: 15.3 us -> 0.01 us  [between_chips(): lax.all_to_all(blocks, PLANE, 0, 0, axis_index_groups=groups, tiled=True)]
    ppermute x42 -> x48, waiting for transfers between devices: 75.3 us -> 90.5 us  [swap(): return lax.ppermute(value, axes, [(i, i ^ offset) for i in range(count)])]
    all_to_all x0 -> x2, starting transfers between devices: none -> 9.41 us  [the longest x1 5.8 us: local_heads(): lax.all_to_all(forward_block.reshape(dp_count, 2 * units, cut), 'dp', 0,...]
    all_gather x1 -> x0, waiting for transfers between devices: 8.73 us -> none  [local_heads(): forward_weights = lax.all_gather(forward_block, 'dp', axis=0, tiled=False)]
    pallas_call x22, Pallas kernels: 57.5 us -> 62.3 us  [call(): pl.pallas_call(kernel, out_shape=outs, in_specs=specs, out_specs=[VMEM] *...]
    ppermute x42 -> x48, starting transfers between devices: 42 us -> 45.5 us  [swap(): return lax.ppermute(value, axes, [(i, i ^ offset) for i in range(count)])]
    unnamed x78 -> x104, local copies, waits for them, and re-layouts: 17.3 us -> 20.5 us
    all_to_all x3 -> x2, starting transfers between devices: 10.7 us -> 8.25 us  [between_chips(): lax.all_to_all(blocks, PLANE, 0, 0, axis_index_groups=groups, tiled=True)]
  transfers between devices with their start and end apart: 47 -> 52, of which waited for: 24 -> 24; matrix products, arithmetic and copies ran while one was open for 1% -> 1% of each run, Pallas kernels for 15% -> 15%
where the time goes in v3:
time: 245 us; the launch traced here: 244 us
  waiting for transfers between devices  92.4 us (38%)
  starting transfers between devices  63.2 us (26%)
  Pallas kernels  62.3 us (25%)
  local copies, waits for them, and re-layouts  22.7 us (9%)
    ppermute x48, waiting for transfers between devices, swap(): return lax.ppermute(value, axes, [(i, i ^ offset) for i in range(count)])  90.5 us
    pallas_call x22, Pallas kernels, call(): pl.pallas_call(kernel, out_shape=outs, in_specs=specs, out_specs=[VMEM] *...  62.3 us
    ppermute x48, starting transfers between devices, swap(): return lax.ppermute(value, axes, [(i, i ^ offset) for i in range(count)])  45.5 us
    unnamed x104, local copies, waits for them, and re-layouts  20.5 us
    all_to_all x2, starting transfers between devices, between_chips(): lax.all_to_all(blocks, PLANE, 0, 0, axis_index_groups=groups, tiled=True)  8.25 us
    all_to_all x1, starting transfers between devices, local_heads(): lax.all_to_all(forward_block.reshape(dp_count, 2 * units, cut), 'dp', 0,...  5.8 us
  transfers between devices with their start and end apart: 52, of which 24 were waited for; matrix products, arithmetic and copies ran while one was open for 1% of the time, Pallas kernels for 15%

profile of v3, /device:TPU:0, one launch (start us, length us, event | category | flops | bytes accessed | tf_op | source)
XLA Modules:
  0.0 244.0 jit_solution(8957956167421031883)
XLA Ops:
  1.3 2.9 %shard_map.245 = (bf16[512,128]{1,0:T(8,128)(2,1)}, bf16[512,128]{1,0:T(8,128)(2,1)}, bf16[128,1024]{1,0:T(8,128)(2,1)}, bf16[16,128]{1,0:T(8,128)(2,1)}) custom-call(s32[5]{0:T(128)} %stack.23.spots.refs_12_, bf16[128,768]{1,0:T(8,128)(2,1)} %refs_0_.2, bf16[256,128]{1,0:T(8,128)(2,1)} %refs_1_.2, bf16[128,1024]{1,0:T(8,128)(2,1)} %refs_2_.1, ...), custom_call_target="tpu_custom_call" | custom-call | flops 1100000000 | tf_op jit(solution)/shard_map/pallas_call | solution.py:386
  4.2 3.0 %collective-permute-start.1 = (bf16[16,128]{1,0:T(8,128)(2,1)}, bf16[16,128]{1,0:T(8,128)(2,1)S(1)}, u32[]{:S(2)}, u32[]{:S(2)}) collective-permute-start(bf16[16,128]{1,0:T(8,128)(2,1)} %get-tuple-element.70), channel_id=1, source_target_pairs={{0,1},{1,0},{2,3},{3,2},{4,5},{5,4},{6,7},{7,6},{8,9},{9,8},{10,11... | collective-permute-start | bytes 12296 | tf_op jit(solution)/shard_map/ppermute | solution.py:352
  13.9 2.2 collective-permute-done.3
  18.4 2.7 %collective-permute-start.5 = (bf16[576,256]{1,0:T(8,128)(2,1)S(1)}, bf16[576,256]{1,0:T(8,128)(2,1)S(1)}, u32[]{:S(2)}, u32[]{:S(2)}) collective-permute-start(bf16[576,256]{1,0:T(8,128)(2,1)S(1)} %shard_map.246.refs_0_), channel_id=1, source_target_pairs={{0,16},{8,24},{16,0},{24,8},{1,17},{9,25},{17,1},{25,9},{2,18},{10... | collective-permute-start | bytes 884744 | tf_op jit(solution)/shard_map/ppermute | solution.py:352
  26.1 7.9 %collective-permute-done.5.refs_2_.refs_1_ = bf16[576,256]{1,0:T(8,128)(2,1)S(1)} collective-permute-done((bf16[576,256]{1,0:T(8,128)(2,1)S(1)}, bf16[576,256]{1,0:T(8,128)(2,1)S(1)}, u32[]{:S(2)}, u32[]{:S(2)}) %collective-permute-start.5) | collective-permute-done | bytes 294944 | tf_op jit(solution)/shard_map/ppermute | solution.py:352
  36.0 3.5 %all-to-all-start = ((bf16[4,128,1024]{2,1,0:T(8,128)(2,1)}), bf16[4,128,1024]{2,1,0:T(8,128)(2,1)S(1)}, u32[]{:S(2)}, u32[]{:S(2)}) async-start(bf16[4,128,1024]{2,1,0:T(8,128)(2,1)} %bitcast.11), calls=%async_computation | async-start | bytes 2097152 | tf_op jit(solution)/shard_map/all_to_all | solution.py:967
  44.1 3.2 %collective-permute-start.6 = (bf16[576,256]{1,0:T(8,128)(2,1)S(1)}, bf16[576,256]{1,0:T(8,128)(2,1)S(1)}, u32[]{:S(2)}, u32[]{:S(2)}) collective-permute-start(bf16[576,256]{1,0:T(8,128)(2,1)S(1)} %shard_map.246.refs_0_), channel_id=1, source_target_pairs={{0,24},{8,16},{16,8},{24,0},{1,25},{9,17},{17,9},{25,1},{2,26},{10... | collective-permute-start | bytes 884744 | tf_op jit(solution)/shard_map/ppermute | solution.py:352
  48.3 3.1 %shard_map.247.refs_4_.refs_8_ = f32[1024,1024]{1,0:T(8,128)S(1)} custom-call(s32[5]{0:T(128)S(1)} %copy-done.7, bf16[128,1024]{1,0:T(8,128)(2,1)S(1)} %copy-done.6, bf16[128,1024]{1,0:T(8,128)(2,1)} %collective-permute-done.7.refs_1_, bf16[128,1024]{1,0:T(8,128)(2,1)} %collective-permute-done.8.refs_2_, ...), custom_call_target="tpu_custom_call" | custom-call | flops 2200000000 | tf_op jit(solution)/shard_map/pallas_call | solution.py:386
  53.4 4.4 %collective-permute-done.14.refs_1_ = bf16[1024,128]{1,0:T(8,128)(2,1)S(1)} collective-permute-done((bf16[1024,128]{1,0:T(8,128)(2,1)S(1)}, bf16[1024,128]{1,0:T(8,128)(2,1)S(1)}, u32[]{:S(2)}, u32[]{:S(2)}) %collective-permute-start.14) | collective-permute-done | bytes 262176 | tf_op jit(solution)/shard_map/ppermute | solution.py:352
  57.8 2.2 shard_map.251.refs_8_
  60.0 5.8 %all-to-all-start.1 = ((bf16[4,1024,256]{2,1,0:T(8,128)(2,1)}), bf16[4,1024,256]{2,1,0:T(8,128)(2,1)}, u32[]{:S(2)}, u32[]{:S(2)}) async-start(bf16[4,1024,256]{2,1,0:T(8,128)(2,1)} %bitcast.13), calls=%async_computation.1 | async-start | bytes 4194304 | tf_op jit(solution)/shard_map/all_to_all | solution.py:1037
  70.2 6.8 %shard_map.252 = (bf16[1024,384]{1,0:T(8,128)(2,1)S(1)}, f32[1024,128]{1,0:T(8,128)S(1)}, f32[1024,128]{1,0:T(8,128)S(1)}, bf16[512,1024]{1,0:T(8,128)(2,1)S(1)}...) custom-call(s32[5]{0:T(128)S(1)} %copy-done.7, f32[2]{0:T(128)S(1)} %multiply_exponential_fusion.slope_ref, ...), custom_call_target="tpu_custom_call" | custom-call | flops 11000000512 | tf_op jit(solution)/shard_map/pallas_call | solution.py:386
  83.6 4.9 %collective-permute-done.16.refs_0_ = bf16[128,1024]{1,0:T(8,128)(2,1)S(1)} collective-permute-done((bf16[128,1024]{1,0:T(8,128)(2,1)S(1)}, bf16[128,1024]{1,0:T(8,128)(2,1)S(1)}, u32[]{:S(2)}, u32[]{:S(2)}) %collective-permute-start.16) | collective-permute-done | bytes 262176 | tf_op jit(solution)/shard_map/ppermute | solution.py:352
  89.6 5.7 %collective-permute-done.18.refs_2_ = bf16[128,1024]{1,0:T(8,128)(2,1)S(1)} collective-permute-done((bf16[128,1024]{1,0:T(8,128)(2,1)S(1)}, bf16[128,1024]{1,0:T(8,128)(2,1)S(1)}, u32[]{:S(2)}, u32[]{:S(2)}) %collective-permute-start.18) | collective-permute-done | bytes 262176 | tf_op jit(solution)/shard_map/ppermute | solution.py:352
  99.2 6.7 %collective-permute-done.21.refs_3_ = bf16[128,1024]{1,0:T(8,128)(2,1)S(1)} collective-permute-done((bf16[128,1024]{1,0:T(8,128)(2,1)S(1)}, bf16[128,1024]{1,0:T(8,128)(2,1)S(1)}, u32[]{:S(2)}, u32[]{:S(2)}) %collective-permute-start.21) | collective-permute-done | bytes 262176 | tf_op jit(solution)/shard_map/ppermute | solution.py:352
  105.9 2.5 %collective-permute-done.20.refs_2_ = bf16[128,1024]{1,0:T(8,128)(2,1)S(1)} collective-permute-done((bf16[128,1024]{1,0:T(8,128)(2,1)S(1)}, bf16[128,1024]{1,0:T(8,128)(2,1)S(1)}, u32[]{:S(2)}, u32[]{:S(2)}) %collective-permute-start.20) | collective-permute-done | bytes 262176 | tf_op jit(solution)/shard_map/ppermute | solution.py:352
  113.5 10.4 %shard_map.255 = (bf16[1024,512]{1,0:T(8,128)(2,1)}, bf16[1024,512]{1,0:T(8,128)(2,1)}, f32[512,1024]{1,0:T(8,128)}, bf16[512,1024]{1,0:T(8,128)(2,1)}, f32[8,512]{1,0:T(8,128)}) custom-call(s32[5]{0:T(128)} %stack.23.spots.refs_12_, bf16[128,1024]{1,0:T(8,128)(2,1)} %copy-done.16, bf16[128,1024]{1,0:T(8,128)(2,1)} %copy-done.48, ...), custom_call_target="tpu_custom_call" | custom-call | flops 8800000000 | tf_op jit(solution)/shard_map/pallas_call | solution.py:386
  124.0 2.9 %collective-permute-done.27.came_ref = bf16[512,1024]{1,0:T(8,128)(2,1)S(1)} collective-permute-done((bf16[512,1024]{1,0:T(8,128)(2,1)}, bf16[512,1024]{1,0:T(8,128)(2,1)S(1)}, u32[]{:S(2)}, u32[]{:S(2)}) %collective-permute-start.27) | collective-permute-done | bytes 1048608 | tf_op jit(solution)/shard_map/ppermute | solution.py:352
  129.4 9.4 %shard_map.259 = (bf16[4,1024,256]{2,1,0:T(8,128)(2,1)}, f32[512,1024]{1,0:T(8,128)}, bf16[512,1024]{1,0:T(8,128)(2,1)}) custom-call(s32[5]{0:T(128)} %stack.23.spots.refs_12_, bf16[128,1024]{1,0:T(8,128)(2,1)} %copy-done.16, bf16[128,1024]{1,0:T(8,128)(2,1)} %copy-done.48, bf16[128,1024]{1,0:T(8,128)(2,1)} %copy-done.47, bf16[128,1024]{1,0:T(8,128)(2,1)} %copy-done.46, ...), custom_call_target="tpu_custom_call" | custom-call | flops 8800000000 | tf_op jit(solution)/shard_map/pallas_call | solution.py:386
  138.8 3.6 %all-to-all-start.3 = ((bf16[4,1024,256]{2,1,0:T(8,128)(2,1)}), bf16[4,1024,256]{2,1,0:T(8,128)(2,1)S(1)}, u32[]{:S(2)}, u32[]{:S(2)}) async-start(bf16[4,1024,256]{2,1,0:T(8,128)(2,1)} %get-tuple-element.112), calls=%async_computation.3 | async-start | bytes 4194304 | tf_op jit(solution)/shard_map/all_to_all | solution.py:1112
  146.3 4.5 %collective-permute-done.28.refs_0_ = bf16[128,1024]{1,0:T(8,128)(2,1)S(1)} collective-permute-done((bf16[128,1024]{1,0:T(8,128)(2,1)S(1)}, bf16[128,1024]{1,0:T(8,128)(2,1)S(1)}, u32[]{:S(2)}, u32[]{:S(2)}) %collective-permute-start.28) | collective-permute-done | bytes 262176 | tf_op jit(solution)/shard_map/ppermute | solution.py:352
  152.3 6.0 %collective-permute-done.30.refs_2_ = bf16[128,1024]{1,0:T(8,128)(2,1)S(1)} collective-permute-done((bf16[128,1024]{1,0:T(8,128)(2,1)S(1)}, bf16[128,1024]{1,0:T(8,128)(2,1)S(1)}, u32[]{:S(2)}, u32[]{:S(2)}) %collective-permute-start.30) | collective-permute-done | bytes 262176 | tf_op jit(solution)/shard_map/ppermute | solution.py:352
  166.0 6.7 %collective-permute-done.33.refs_3_ = bf16[128,1024]{1,0:T(8,128)(2,1)S(1)} collective-permute-done((bf16[128,1024]{1,0:T(8,128)(2,1)S(1)}, bf16[128,1024]{1,0:T(8,128)(2,1)S(1)}, u32[]{:S(2)}, u32[]{:S(2)}) %collective-permute-start.33) | collective-permute-done | bytes 262176 | tf_op jit(solution)/shard_map/ppermute | solution.py:352
  172.7 2.9 %collective-permute-done.32.refs_2_ = bf16[128,1024]{1,0:T(8,128)(2,1)S(1)} collective-permute-done((bf16[128,1024]{1,0:T(8,128)(2,1)S(1)}, bf16[128,1024]{1,0:T(8,128)(2,1)S(1)}, u32[]{:S(2)}, u32[]{:S(2)}) %collective-permute-start.32) | collective-permute-done | bytes 262176 | tf_op jit(solution)/shard_map/ppermute | solution.py:352
  178.1 8.1 %shard_map.258 = (bf16[1024,384]{1,0:T(8,128)(2,1)S(1)}, f32[512,1024]{1,0:T(8,128)S(1)}, bf16[512,1024]{1,0:T(8,128)(2,1)S(1)}) custom-call(s32[5]{0:T(128)S(1)} %copy-done.8, f32[2]{0:T(128)S(1)} %multiply_exponential_fusion.slope_ref, bf16[128,1024]{1,0:T(8,128)(2,1)S(1)} %get-tuple-element.91.refs_0_, ...), custom_call_target="tpu_custom_call" | custom-call | flops 11000000512 | tf_op jit(solution)/shard_map/pallas_call | solution.py:386
  186.4 2.5 %shard_map.260 = (f32[576,256]{1,0:T(8,128)S(1)}, bf16[576,256]{1,0:T(8,128)(2,1)S(1)}, bf16[576,256]{1,0:T(8,128)(2,1)S(1)}, bf16[576,256]{1,0:T(8,128)(2,1)S(1)}) custom-call(s32[5]{0:T(128)S(1)} %copy-done.8, bf16[128,1024]{1,0:T(8,128)(2,1)S(1)} %get-tuple-element.91.refs_0_, bf16[128,1024]{1,0:T(8,128)(2,1)S(1)} %collective-permute-done.31.refs_1_, ...), custom_call_target="tpu_custom_call" | custom-call | flops 3300000000 | tf_op jit(solution)/shard_map/pallas_call | solution.py:386
  189.7 2.2 shard_map.261
  191.9 4.7 %all-to-all-start.2 = ((bf16[4,128,2048]{2,1,0:T(8,128)(2,1)}), bf16[4,128,2048]{2,1,0:T(8,128)(2,1)}, u32[]{:S(2)}, u32[]{:S(2)}) async-start(bf16[4,128,2048]{2,1,0:T(8,128)(2,1)} %bitcast.14), calls=%async_computation.2 | async-start | bytes 4194304 | tf_op jit(solution)/shard_map/all_to_all | solution.py:967
  198.0 2.4 collective-permute-start.41
  204.5 16.9 %collective-permute-done.41.refs_2_ = bf16[576,256]{1,0:T(8,128)(2,1)S(1)} collective-permute-done((bf16[576,256]{1,0:T(8,128)(2,1)S(1)}, bf16[576,256]{1,0:T(8,128)(2,1)S(1)}, u32[]{:S(2)}, u32[]{:S(2)}) %collective-permute-start.41) | collective-permute-done | bytes 294944 | tf_op jit(solution)/shard_map/ppermute | solution.py:352
  222.9 4.7 %collective-permute-done.43.refs_5_.refs_1_ = bf16[1024,128]{1,0:T(8,128)(2,1)S(1)} collective-permute-done((bf16[1024,128]{1,0:T(8,128)(2,1)S(1)}, bf16[1024,128]{1,0:T(8,128)(2,1)S(1)}, u32[]{:S(2)}, u32[]{:S(2)}) %collective-permute-start.43) | collective-permute-done | bytes 262176 | tf_op jit(solution)/shard_map/ppermute | solution.py:352
  237.8 3.1 %shard_map.262 = (bf16[128,1024]{1,0:T(8,128)(2,1)}, bf16[128,1024]{1,0:T(8,128)(2,1)}) custom-call(s32[5]{0:T(128)S(1)} %copy-done.8, bf16[4,128,2048]{2,1,0:T(8,128)(2,1)} %all-to-all-done.2.parts_ref.refs_4_, f32[128,1024]{1,0:T(8,128)S(1)} %copy-done.29, bf16[128,1024]{1,0:T(8,128)(2,1)S(1)} %copy-done.6, f32[128,1024]{1,0:T(8,128)S(1)} %copy-done.27, ...), custom_call_target="tpu_custom_call" | custom-call | flops 1100000000 | tf_op jit(solution)/shard_map/pallas_call | solution.py:386
  (212 shorter events, 84.2 us)
Async XLA Ops:
  18.4 15.7 %collective-permute-start.5 = (bf16[576,256]{1,0:T(8,128)(2,1)S(1)}, bf16[576,256]{1,0:T(8,128)(2,1)S(1)}, u32[]{:S(2)}, u32[]{:S(2)}) collective-permute-start(bf16[576,256]{1,0:T(8,128)(2,1)S(1)} %shard_map.246.refs_0_), channel_id=1, source_target_pairs={{0,16},{8,24},{16,0},{24,8},{1,17},{9,25},{17,1},{25,9},{2,18},{10... | collective-permute-start | bytes 884744 | tf_op jit(solution)/shard_map/ppermute | solution.py:352
  21.1 13.2 %collective-permute-start.4 = (bf16[576,256]{1,0:T(8,128)(2,1)S(1)}, bf16[576,256]{1,0:T(8,128)(2,1)S(1)}, u32[]{:S(2)}, u32[]{:S(2)}) collective-permute-start(bf16[576,256]{1,0:T(8,128)(2,1)S(1)} %shard_map.246.refs_0_), channel_id=1, source_target_pairs={{0,8},{8,0},{16,24},{24,16},{1,9},{9,1},{17,25},{25,17},{2,10},{10... | collective-permute-start | bytes 884744 | tf_op jit(solution)/shard_map/ppermute | solution.py:352
  22.6 17.0 %collective-permute-start.9 = (bf16[128,1024]{1,0:T(8,128)(2,1)S(1)}, bf16[128,1024]{1,0:T(8,128)(2,1)S(1)}, u32[]{:S(2)}, u32[]{:S(2)}) collective-permute-start(bf16[128,1024]{1,0:T(8,128)(2,1)S(1)} %copy-done.6), channel_id=1, source_target_pairs={{0,5},{1,4},{2,7},{3,6},{4,1},{5,0},{6,3},{7,2},{8,13},{9,12},{10,... | collective-permute-start | bytes 786440 | tf_op jit(solution)/shard_map/ppermute | solution.py:352
  24.7 15.4 %collective-permute-start.8 = (bf16[128,1024]{1,0:T(8,128)(2,1)S(1)}, bf16[128,1024]{1,0:T(8,128)(2,1)}, u32[]{:S(2)}, u32[]{:S(2)}) collective-permute-start(bf16[128,1024]{1,0:T(8,128)(2,1)S(1)} %copy-done.6), channel_id=1, source_target_pairs={{0,4},{1,5},{2,6},{3,7},{4,0},{5,1},{6,2},{7,3},{8,12},{9,13},{10,... | collective-permute-start | bytes 786440 | tf_op jit(solution)/shard_map/ppermute | solution.py:352
  25.3 14.9 %collective-permute-start.7 = (bf16[128,1024]{1,0:T(8,128)(2,1)S(1)}, bf16[128,1024]{1,0:T(8,128)(2,1)}, u32[]{:S(2)}, u32[]{:S(2)}) collective-permute-start(bf16[128,1024]{1,0:T(8,128)(2,1)S(1)} %copy-done.6), channel_id=1, source_target_pairs={{0,1},{1,0},{2,3},{3,2},{4,5},{5,4},{6,7},{7,6},{8,9},{9,8},{10,11... | collective-permute-start | bytes 786440 | tf_op jit(solution)/shard_map/ppermute | solution.py:352
  36.0 24.0 %all-to-all-start = ((bf16[4,128,1024]{2,1,0:T(8,128)(2,1)}), bf16[4,128,1024]{2,1,0:T(8,128)(2,1)S(1)}, u32[]{:S(2)}, u32[]{:S(2)}) async-start(bf16[4,128,1024]{2,1,0:T(8,128)(2,1)} %bitcast.11), calls=%async_computation | async-start | bytes 2097152 | tf_op jit(solution)/shard_map/all_to_all | solution.py:967
  41.3 16.5 %collective-permute-start.14 = (bf16[1024,128]{1,0:T(8,128)(2,1)S(1)}, bf16[1024,128]{1,0:T(8,128)(2,1)S(1)}, u32[]{:S(2)}, u32[]{:S(2)}) collective-permute-start(bf16[1024,128]{1,0:T(8,128)(2,1)S(1)} %get-tuple-element.75), channel_id=1, source_target_pairs={{0,1},{1,0},{2,3},{3,2},{4,5},{5,4},{6,7},{7,6},{8,9},{9,8},{10,11... | collective-permute-start | bytes 786440 | tf_op jit(solution)/shard_map/ppermute | solution.py:352
  44.1 21.7 %collective-permute-start.6 = (bf16[576,256]{1,0:T(8,128)(2,1)S(1)}, bf16[576,256]{1,0:T(8,128)(2,1)S(1)}, u32[]{:S(2)}, u32[]{:S(2)}) collective-permute-start(bf16[576,256]{1,0:T(8,128)(2,1)S(1)} %shard_map.246.refs_0_), channel_id=1, source_target_pairs={{0,24},{8,16},{16,8},{24,0},{1,25},{9,17},{17,9},{25,1},{2,26},{10... | collective-permute-start | bytes 884744 | tf_op jit(solution)/shard_map/ppermute | solution.py:352
  60.0 53.4 %all-to-all-start.1 = ((bf16[4,1024,256]{2,1,0:T(8,128)(2,1)}), bf16[4,1024,256]{2,1,0:T(8,128)(2,1)}, u32[]{:S(2)}, u32[]{:S(2)}) async-start(bf16[4,1024,256]{2,1,0:T(8,128)(2,1)} %bitcast.13), calls=%async_computation.1 | async-start | bytes 4194304 | tf_op jit(solution)/shard_map/all_to_all | solution.py:1037
  77.2 32.4 %collective-permute-start.26 = (bf16[512,1024]{1,0:T(8,128)(2,1)S(1)}, bf16[512,1024]{1,0:T(8,128)(2,1)S(1)}, u32[]{:S(2)}, u32[]{:S(2)}) collective-permute-start(bf16[512,1024]{1,0:T(8,128)(2,1)S(1)} %bitcast.28), channel_id=1, source_target_pairs={{0,2},{1,3},{2,0},{3,1},{4,6},{5,7},{6,4},{7,5},{8,10},{9,11},{10,... | collective-permute-start | bytes 3145736 | tf_op jit(solution)/shard_map/ppermute | solution.py:352
  80.0 8.4 %collective-permute-start.16 = (bf16[128,1024]{1,0:T(8,128)(2,1)S(1)}, bf16[128,1024]{1,0:T(8,128)(2,1)S(1)}, u32[]{:S(2)}, u32[]{:S(2)}) collective-permute-start(bf16[128,1024]{1,0:T(8,128)(2,1)S(1)} %get-tuple-element.79), channel_id=1, source_target_pairs={{0,1},{1,0},{2,3},{3,2},{4,5},{5,4},{6,7},{7,6},{8,9},{9,8},{10,11... | collective-permute-start | bytes 786440 | tf_op jit(solution)/shard_map/ppermute | solution.py:352
  80.4 9.2 %collective-permute-start.17 = (bf16[128,1024]{1,0:T(8,128)(2,1)S(1)}, bf16[128,1024]{1,0:T(8,128)(2,1)S(1)}, u32[]{:S(2)}, u32[]{:S(2)}) collective-permute-start(bf16[128,1024]{1,0:T(8,128)(2,1)S(1)} %get-tuple-element.80), channel_id=1, source_target_pairs={{0,4},{1,5},{2,6},{3,7},{4,0},{5,1},{6,2},{7,3},{8,12},{9,13},{10,... | collective-permute-start | bytes 786440 | tf_op jit(solution)/shard_map/ppermute | solution.py:352
  81.9 13.4 %collective-permute-start.18 = (bf16[128,1024]{1,0:T(8,128)(2,1)S(1)}, bf16[128,1024]{1,0:T(8,128)(2,1)S(1)}, u32[]{:S(2)}, u32[]{:S(2)}) collective-permute-start(bf16[128,1024]{1,0:T(8,128)(2,1)S(1)} %get-tuple-element.81), channel_id=1, source_target_pairs={{0,5},{1,4},{2,7},{3,6},{4,1},{5,0},{6,3},{7,2},{8,13},{9,12},{10,... | collective-permute-start | bytes 786440 | tf_op jit(solution)/shard_map/ppermute | solution.py:352
  95.7 10.2 %collective-permute-start.21 = (bf16[128,1024]{1,0:T(8,128)(2,1)S(1)}, bf16[128,1024]{1,0:T(8,128)(2,1)S(1)}, u32[]{:S(2)}, u32[]{:S(2)}) collective-permute-start(bf16[128,1024]{1,0:T(8,128)(2,1)S(1)} %get-tuple-element.82.refs_0_), channel_id=1, source_target_pairs={{0,5},{1,4},{2,7},{3,6},{4,1},{5,0},{6,3},{7,2},{8,13},{9,12},{10,... | collective-permute-start | bytes 786440 | tf_op jit(solution)/shard_map/ppermute | solution.py:352
  97.0 11.5 %collective-permute-start.20 = (bf16[128,1024]{1,0:T(8,128)(2,1)S(1)}, bf16[128,1024]{1,0:T(8,128)(2,1)S(1)}, u32[]{:S(2)}, u32[]{:S(2)}) collective-permute-start(bf16[128,1024]{1,0:T(8,128)(2,1)S(1)} %get-tuple-element.82.refs_0_), channel_id=1, source_target_pairs={{0,4},{1,5},{2,6},{3,7},{4,0},{5,1},{6,2},{7,3},{8,12},{9,13},{10,... | collective-permute-start | bytes 786440 | tf_op jit(solution)/shard_map/ppermute | solution.py:352
  97.6 11.9 %collective-permute-start.19 = (bf16[128,1024]{1,0:T(8,128)(2,1)S(1)}, bf16[128,1024]{1,0:T(8,128)(2,1)S(1)}, u32[]{:S(2)}, u32[]{:S(2)}) collective-permute-start(bf16[128,1024]{1,0:T(8,128)(2,1)S(1)} %get-tuple-element.82.refs_0_), channel_id=1, source_target_pairs={{0,1},{1,0},{2,3},{3,2},{4,5},{5,4},{6,7},{7,6},{8,9},{9,8},{10,11... | collective-permute-start | bytes 786440 | tf_op jit(solution)/shard_map/ppermute | solution.py:352
  99.2 10.4 %collective-permute-start.22 = (bf16[128,1024]{1,0:T(8,128)(2,1)S(1)}, bf16[128,1024]{1,0:T(8,128)(2,1)S(1)}, u32[]{:S(2)}, u32[]{:S(2)}) collective-permute-start(bf16[128,1024]{1,0:T(8,128)(2,1)S(1)} %get-tuple-element.82.refs_0_), channel_id=1, source_target_pairs={{0,2},{1,3},{2,0},{3,1},{4,6},{5,7},{6,4},{7,5},{8,10},{9,11},{10,... | collective-permute-start | bytes 786440 | tf_op jit(solution)/shard_map/ppermute | solution.py:352
  138.8 53.1 %all-to-all-start.3 = ((bf16[4,1024,256]{2,1,0:T(8,128)(2,1)}), bf16[4,1024,256]{2,1,0:T(8,128)(2,1)S(1)}, u32[]{:S(2)}, u32[]{:S(2)}) async-start(bf16[4,1024,256]{2,1,0:T(8,128)(2,1)} %get-tuple-element.112), calls=%async_computation.3 | async-start | bytes 4194304 | tf_op jit(solution)/shard_map/all_to_all | solution.py:1112
  142.4 8.4 %collective-permute-start.28 = (bf16[128,1024]{1,0:T(8,128)(2,1)S(1)}, bf16[128,1024]{1,0:T(8,128)(2,1)S(1)}, u32[]{:S(2)}, u32[]{:S(2)}) collective-permute-start(bf16[128,1024]{1,0:T(8,128)(2,1)S(1)} %get-tuple-element.87), channel_id=1, source_target_pairs={{0,1},{1,0},{2,3},{3,2},{4,5},{5,4},{6,7},{7,6},{8,9},{9,8},{10,11... | collective-permute-start | bytes 786440 | tf_op jit(solution)/shard_map/ppermute | solution.py:352
  143.1 9.2 %collective-permute-start.29 = (bf16[128,1024]{1,0:T(8,128)(2,1)S(1)}, bf16[128,1024]{1,0:T(8,128)(2,1)S(1)}, u32[]{:S(2)}, u32[]{:S(2)}) collective-permute-start(bf16[128,1024]{1,0:T(8,128)(2,1)S(1)} %get-tuple-element.88), channel_id=1, source_target_pairs={{0,4},{1,5},{2,6},{3,7},{4,0},{5,1},{6,2},{7,3},{8,12},{9,13},{10,... | collective-permute-start | bytes 786440 | tf_op jit(solution)/shard_map/ppermute | solution.py:352
  145.2 13.1 %collective-permute-start.30 = (bf16[128,1024]{1,0:T(8,128)(2,1)S(1)}, bf16[128,1024]{1,0:T(8,128)(2,1)S(1)}, u32[]{:S(2)}, u32[]{:S(2)}) collective-permute-start(bf16[128,1024]{1,0:T(8,128)(2,1)S(1)} %get-tuple-element.89), channel_id=1, source_target_pairs={{0,5},{1,4},{2,7},{3,6},{4,1},{5,0},{6,3},{7,2},{8,13},{9,12},{10,... | collective-permute-start | bytes 786440 | tf_op jit(solution)/shard_map/ppermute | solution.py:352
  162.4 10.2 %collective-permute-start.33 = (bf16[128,1024]{1,0:T(8,128)(2,1)S(1)}, bf16[128,1024]{1,0:T(8,128)(2,1)S(1)}, u32[]{:S(2)}, u32[]{:S(2)}) collective-permute-start(bf16[128,1024]{1,0:T(8,128)(2,1)S(1)} %get-tuple-element.91.refs_0_), channel_id=1, source_target_pairs={{0,5},{1,4},{2,7},{3,6},{4,1},{5,0},{6,3},{7,2},{8,13},{9,12},{10,... | collective-permute-start | bytes 786440 | tf_op jit(solution)/shard_map/ppermute | solution.py:352
  164.0 11.5 %collective-permute-start.32 = (bf16[128,1024]{1,0:T(8,128)(2,1)S(1)}, bf16[128,1024]{1,0:T(8,128)(2,1)S(1)}, u32[]{:S(2)}, u32[]{:S(2)}) collective-permute-start(bf16[128,1024]{1,0:T(8,128)(2,1)S(1)} %get-tuple-element.91.refs_0_), channel_id=1, source_target_pairs={{0,4},{1,5},{2,6},{3,7},{4,0},{5,1},{6,2},{7,3},{8,12},{9,13},{10,... | collective-permute-start | bytes 786440 | tf_op jit(solution)/shard_map/ppermute | solution.py:352
  164.3 12.2 %collective-permute-start.31 = (bf16[128,1024]{1,0:T(8,128)(2,1)S(1)}, bf16[128,1024]{1,0:T(8,128)(2,1)S(1)}, u32[]{:S(2)}, u32[]{:S(2)}) collective-permute-start(bf16[128,1024]{1,0:T(8,128)(2,1)S(1)} %get-tuple-element.91.refs_0_), channel_id=1, source_target_pairs={{0,1},{1,0},{2,3},{3,2},{4,5},{5,4},{6,7},{7,6},{8,9},{9,8},{10,11... | collective-permute-start | bytes 786440 | tf_op jit(solution)/shard_map/ppermute | solution.py:352
  166.0 11.1 %collective-permute-start.34 = (bf16[128,1024]{1,0:T(8,128)(2,1)S(1)}, bf16[128,1024]{1,0:T(8,128)(2,1)S(1)}, u32[]{:S(2)}, u32[]{:S(2)}) collective-permute-start(bf16[128,1024]{1,0:T(8,128)(2,1)S(1)} %get-tuple-element.91.refs_0_), channel_id=1, source_target_pairs={{0,2},{1,3},{2,0},{3,1},{4,6},{5,7},{6,4},{7,5},{8,10},{9,11},{10,... | collective-permute-start | bytes 786440 | tf_op jit(solution)/shard_map/ppermute | solution.py:352
  176.5 13.2 %collective-permute-start.39 = (bf16[512,1024]{1,0:T(8,128)(2,1)S(1)}, bf16[512,1024]{1,0:T(8,128)(2,1)S(1)}, u32[]{:S(2)}, u32[]{:S(2)}) collective-permute-start(bf16[512,1024]{1,0:T(8,128)(2,1)S(1)} %copy-done.44), channel_id=1, source_target_pairs={{0,2},{1,3},{2,0},{3,1},{4,6},{5,7},{6,4},{7,5},{8,10},{9,11},{10,... | collective-permute-start | bytes 3145736 | tf_op jit(solution)/shard_map/ppermute | solution.py:352
  191.9 35.7 %all-to-all-start.2 = ((bf16[4,128,2048]{2,1,0:T(8,128)(2,1)}), bf16[4,128,2048]{2,1,0:T(8,128)(2,1)}, u32[]{:S(2)}, u32[]{:S(2)}) async-start(bf16[4,128,2048]{2,1,0:T(8,128)(2,1)} %bitcast.14), calls=%async_computation.2 | async-start | bytes 4194304 | tf_op jit(solution)/shard_map/all_to_all | solution.py:967
  196.6 26.3 %collective-permute-start.40 = (bf16[576,256]{1,0:T(8,128)(2,1)S(1)}, bf16[576,256]{1,0:T(8,128)(2,1)S(1)}, u32[]{:S(2)}, u32[]{:S(2)}) collective-permute-start(bf16[576,256]{1,0:T(8,128)(2,1)S(1)} %get-tuple-element.105._), channel_id=1, source_target_pairs={{0,8},{8,0},{16,24},{24,16},{1,9},{9,1},{17,25},{25,17},{2,10},{10... | collective-permute-start | bytes 884744 | tf_op jit(solution)/shard_map/ppermute | solution.py:352
  198.0 23.4 %collective-permute-start.41 = (bf16[576,256]{1,0:T(8,128)(2,1)S(1)}, bf16[576,256]{1,0:T(8,128)(2,1)S(1)}, u32[]{:S(2)}, u32[]{:S(2)}) collective-permute-start(bf16[576,256]{1,0:T(8,128)(2,1)S(1)} %get-tuple-element.110), channel_id=1, source_target_pairs={{0,16},{8,24},{16,0},{24,8},{1,17},{9,25},{17,1},{25,9},{2,18},{10... | collective-permute-start | bytes 884744 | tf_op jit(solution)/shard_map/ppermute | solution.py:352
  200.4 21.8 %collective-permute-start.42 = (bf16[576,256]{1,0:T(8,128)(2,1)S(1)}, bf16[576,256]{1,0:T(8,128)(2,1)S(1)}, u32[]{:S(2)}, u32[]{:S(2)}) collective-permute-start(bf16[576,256]{1,0:T(8,128)(2,1)S(1)} %get-tuple-element.111), channel_id=1, source_target_pairs={{0,24},{8,16},{16,8},{24,0},{1,25},{9,17},{17,9},{25,1},{2,26},{10... | collective-permute-start | bytes 884744 | tf_op jit(solution)/shard_map/ppermute | solution.py:352
  202.9 24.7 %collective-permute-start.43 = (bf16[1024,128]{1,0:T(8,128)(2,1)S(1)}, bf16[1024,128]{1,0:T(8,128)(2,1)S(1)}, u32[]{:S(2)}, u32[]{:S(2)}) collective-permute-start(bf16[1024,128]{1,0:T(8,128)(2,1)S(1)} %get-tuple-element.113), channel_id=1, source_target_pairs={{0,1},{1,0},{2,3},{3,2},{4,5},{5,4},{6,7},{7,6},{8,9},{9,8},{10,11... | collective-permute-start | bytes 786440 | tf_op jit(solution)/shard_map/ppermute | solution.py:352
  232.9 9.6 %collective-permute-start.47 = (bf16[512,128]{1,0:T(8,128)(2,1)S(1)}, bf16[512,128]{1,0:T(8,128)(2,1)S(1)}, u32[]{:S(2)}, u32[]{:S(2)}) collective-permute-start(bf16[512,128]{1,0:T(8,128)(2,1)S(1)} %get-tuple-element.116), channel_id=1, source_target_pairs={{0,1},{1,0},{2,3},{3,2},{4,5},{5,4},{6,7},{7,6},{8,9},{9,8},{10,11... | collective-permute-start | bytes 393224 | tf_op jit(solution)/shard_map/ppermute | solution.py:352
  (72 other events, 663.3 us)
